TPU v7x, 32 devices: a whole 2x2x4 slice. The times are simulated.
32 devices in a mesh: dp: 16 (over z, x, core), tensor: 2 (over y).
Axes of the slice: x: 2, y: 2, z: 4, core: 2. Of those that a mesh axis runs over, the one named last changes fastest.
Arguments:
- block_in: bfloat16 [4096, 1536], P('dp', 'tensor'), may hold values from -6 to 6
- cotangent: bfloat16 [4096, 1536], P('dp', 'tensor'), may hold values from -6 to 6
- lengths: int32 [16, 1], P('dp'), may hold values from 0 to 256, as said below
- dest_slot: int32 [4096], replicated, may hold values from 0 to 4095, as said below
- return_slot: int32 [4096], replicated, may hold values from 0 to 4095, as said below
- norm_gain: float32 [1536], replicated, may hold values from 0.5 to 1.5
- inner_weight: bfloat16 [1536, 2, 3072], P(None, None, 'tensor'), may hold values from -0.15625 to 0.15625
- state_weight: bfloat16 [1536, 256], replicated, may hold values from -0.15625 to 0.15625
- step_weight: bfloat16 [1536, 48], P(None, 'tensor'), may hold values from -0.15625 to 0.15625
- conv_inner: float32 [4, 3072], P(None, 'tensor'), may hold values from -3 to 3
- conv_inner_bias: float32 [3072], P('tensor'), may hold values from -3 to 3
- conv_state: float32 [4, 256], replicated, may hold values from -3 to 3
- conv_state_bias: float32 [256], replicated, may hold values from -3 to 3
- step_bias: float32 [48], P('tensor'), may hold values from -7 to -2
- log_rate: float32 [48], P('tensor'), may hold values from 0 to 2.77
- skip_gain: float32 [48], P('tensor'), may hold values from 0.5 to 2
- gate_gain: float32 [3072], P('tensor'), may hold values from 0.5 to 1.5
- out_weight: bfloat16 [3072, 1536], P('tensor'), may hold values from -0.109375 to 0.109375
Outputs:
- block_out: bfloat16 [4096, 1536], P('dp', 'tensor')
- input_grad: bfloat16 [4096, 1536], P('dp', 'tensor')
- norm_gain_grad: float32 [1536], P('dp')
- inner_weight_grad: float32 [1536, 2, 3072], P('dp', None, 'tensor')
- state_weight_grad: float32 [1536, 256], P('dp')
- step_weight_grad: float32 [1536, 48], P('dp', 'tensor')
- conv_inner_grad: float32 [4, 3072], P(None, 'tensor')
- conv_inner_bias_grad: float32 [3072], P('tensor')
- conv_state_grad: float32 [4, 256], replicated
- conv_state_bias_grad: float32 [256], replicated
- step_bias_grad: float32 [48], P('tensor')
- log_rate_grad: float32 [48], P('tensor')
- skip_gain_grad: float32 [48], P('tensor')
- gate_gain_grad: float32 [3072], P('tensor')
- out_weight_grad: float32 [3072, 1536], P('tensor', 'dp')
Inputs may be any that keep to these rules, and one draw needn't show every extreme that they name: lengths[g, k] > 0 exactly where a sequence begins at stretch k of group g; stretch 0 of every group begins one; a sequence fills lengths[g, k] slots from the first slot of its stretch and ends before the next stretch that begins a sequence, or at the group's end; some group holds one sequence of 256 slots. A permutation of the slots: input row p goes to slot dest_slot[p] % 256 of group dest_slot[p] // 256. Of the 256 rows of one dp device, at most 32 go to one group, and some device sends exactly 32 rows to some group. A permutation of the slots: returned row q takes the output of slot return_slot[q] % 256 of group return_slot[q] // 256. Of the 256 rows of one dp device, at most 32 come from one group, and some device takes exactly 32 rows from some group.
All inputs are finite; a program needn't handle non-finite values.
Results may differ from a plain program's by a relative error of at most 0.0082.
Values may be sent and summed in bfloat16 or wider, within the bound.
A program may use at most 192 MiB of HBM per device.

v0:
```python
import jax
import jax.numpy as jnp
from jax import lax
from jax.sharding import PartitionSpec as P

STRETCH = 256


PRECISE = lax.Precision.HIGHEST
EPSILON = 1e-05


def silu_slope(values):
    logistic = jax.nn.sigmoid(values)
    return logistic * (1.0 + values * (1.0 - logistic))


def stretch_layout(seq_lengths, stretch_rows):
    total_stretches = seq_lengths.shape[0]
    numbers = jnp.arange(total_stretches, dtype=jnp.int32)
    begins = seq_lengths > 0
    first_stretch = jnp.max(
        jnp.where(begins[None, :] & (numbers[None, :] <= numbers[:, None]), numbers[None, :], 0),
        axis=1,
    )
    seq_length = jnp.sum(
        jnp.where(numbers[None, :] == first_stretch[:, None], seq_lengths[None, :], 0), axis=1
    )
    within = (
        jnp.arange(stretch_rows, dtype=jnp.int32)[None, :]
        + ((numbers - first_stretch) * stretch_rows)[:, None]
    )
    live_mask = (within < seq_length[:, None]).astype(jnp.float32).reshape(-1)
    keep_state = 1.0 - begins.astype(jnp.float32)
    return (within.reshape(-1), live_mask, keep_state)


def shift_down(values, steps):
    return jnp.concatenate(
        [jnp.zeros((steps,) + values.shape[1:], values.dtype), values[:-steps]], axis=0
    )


def shift_up(values, steps):
    return jnp.concatenate(
        [values[steps:], jnp.zeros((steps,) + values.shape[1:], values.dtype)], axis=0
    )


def conv_forward(raw_in, tap_weights, tap_bias, seq_pos):
    total = tap_bias[None, :] + tap_weights[0][None, :] * raw_in
    for tap_index in range(1, tap_weights.shape[0]):
        valid = (seq_pos >= tap_index).astype(jnp.float32)[:, None]
        total = total + tap_weights[tap_index][None, :] * shift_down(raw_in, tap_index) * valid
    return total


def conv_backward(raw_in, tap_weights, seq_pos, conv_grad):
    tap_grads = [jnp.sum(conv_grad * raw_in, axis=0)]
    raw_grad = tap_weights[0][None, :] * conv_grad
    for tap_index in range(1, tap_weights.shape[0]):
        masked = conv_grad * (seq_pos >= tap_index).astype(jnp.float32)[:, None]
        tap_grads.append(jnp.sum(masked * shift_down(raw_in, tap_index), axis=0))
        raw_grad = raw_grad + tap_weights[tap_index][None, :] * shift_up(masked, tap_index)
    return (raw_grad, jnp.stack(tap_grads, axis=0), jnp.sum(conv_grad, axis=0))


def send_layout(targets, group_rows, capacity, groups):
    owner_group = targets // group_rows
    onehot = (owner_group[:, None] == jnp.arange(groups, dtype=jnp.int32)[None, :]).astype(
        jnp.int32
    )
    arrival = jnp.sum(jnp.cumsum(onehot, axis=0) * onehot, axis=1) - 1
    return owner_group * capacity + arrival


def arrivals(targets, group_rows, capacity, groups, own_group):
    by_source = targets.reshape(groups, group_rows)
    owner_group = by_source // group_rows
    is_mine = (owner_group == own_group).astype(jnp.int32)
    arrival = jnp.cumsum(is_mine, axis=1) - 1
    position = jnp.arange(groups, dtype=jnp.int32)[:, None] * capacity + arrival
    position = jnp.where(is_mine > 0, position, groups * capacity)
    filler = jnp.full((groups * capacity,), group_rows, jnp.int32)
    return filler.at[position.reshape(-1)].set(
        (by_source - owner_group * group_rows).reshape(-1), mode="drop"
    )


def state_forward(x_heads, written, readout, step_size, decay_rate, stretch_rows):
    rows_all, heads, head_dim = x_heads.shape
    stretches = rows_all // stretch_rows
    x_blocks = x_heads.reshape(stretches, stretch_rows, heads, head_dim)
    w_blocks = written.reshape(stretches, stretch_rows, -1)
    r_blocks = readout.reshape(stretches, stretch_rows, -1)
    step_blocks = step_size.reshape(stretches, stretch_rows, heads)
    log_decay = jnp.cumsum(step_blocks * decay_rate[None, None, :], axis=1)
    by_head = jnp.transpose(log_decay, (0, 2, 1))
    causal = jnp.arange(stretch_rows)[:, None] >= jnp.arange(stretch_rows)[None, :]
    spread = by_head[:, :, :, None] - by_head[:, :, None, :]
    fading = jnp.where(causal, jnp.exp(jnp.where(causal, spread, 0.0)), 0.0)
    intersection = jnp.einsum("cin,cjn->cij", r_blocks, w_blocks, precision=PRECISE)
    mixing = intersection[:, None, :, :] * fading
    driven = step_blocks[..., None] * x_blocks
    to_end = jnp.exp(log_decay[:, -1:, :] - log_decay)
    stretch_state = jnp.einsum(
        "cjhp,cjn->chpn", to_end[..., None] * driven, w_blocks, precision=PRECISE
    )
    end_fade = jnp.exp(log_decay[:, -1, :])
    running = jnp.zeros(stretch_state.shape[1:], jnp.float32)
    entering = []
    entering.append(running)
    entering = jnp.stack(entering)
    from_start = jnp.exp(log_decay)
    carried_out = from_start[..., None] * jnp.einsum(
        "chpn,cin->cihp", entering, r_blocks, precision=PRECISE
    )
    inner_out = jnp.einsum("chij,cjhp->cihp", mixing, driven, precision=PRECISE)
    saved = (
        x_blocks,
        w_blocks,
        r_blocks,
        step_blocks,
        causal,
        fading,
        mixing,
        driven,
        to_end,
        entering,
        end_fade,
        from_start,
        carried_out,
    )
    return ((inner_out + carried_out).reshape(rows_all, heads * head_dim), saved)


def state_backward(saved, mixed_grad, decay_rate):
    (
        x_blocks,
        w_blocks,
        r_blocks,
        step_blocks,
        causal,
        fading,
        mixing,
        driven,
        to_end,
        entering,
        end_fade,
        from_start,
        carried_out,
    ) = saved
    stretches = x_blocks.shape[0]
    scaled = from_start[..., None] * mixed_grad
    readout_grad = jnp.einsum("cihp,chpn->cin", scaled, entering, precision=PRECISE)
    from_out = jnp.einsum("cihp,cin->chpn", scaled, r_blocks, precision=PRECISE)
    decay_grad = jnp.sum(carried_out * mixed_grad, axis=3)
    downstream = jnp.zeros(from_out.shape[1:], jnp.float32)
    passed = []
    end_grads = []
    for number in reversed(range(stretches)):
        handed = jnp.zeros_like(downstream)
        passed.append(handed)
        end_grads.append(jnp.sum(handed * entering[number], axis=(1, 2)))
        downstream = from_out[number] + end_fade[number][:, None, None] * handed
    passed = jnp.stack(passed[::-1])
    end_grads = jnp.stack(end_grads[::-1])
    pulled = jnp.einsum("chpn,cjn->cjhp", passed, w_blocks, precision=PRECISE)
    driven_grad = to_end[..., None] * pulled
    written_grad = jnp.einsum(
        "cjhp,chpn->cjn", to_end[..., None] * driven, passed, precision=PRECISE
    )
    tail_grad = jnp.sum(pulled * driven, axis=3) * to_end
    decay_grad = decay_grad - tail_grad
    last_extra = jnp.sum(tail_grad, axis=1) + end_grads * end_fade
    mixing_grad = jnp.where(
        causal, jnp.einsum("cihp,cjhp->chij", mixed_grad, driven, precision=PRECISE), 0.0
    )
    driven_grad = driven_grad + jnp.einsum("chij,cihp->cjhp", mixing, mixed_grad, precision=PRECISE)
    intersection_grad = jnp.sum(mixing_grad * fading, axis=1)
    readout_grad = readout_grad + jnp.einsum(
        "cij,cjn->cin", intersection_grad, w_blocks, precision=PRECISE
    )
    written_grad = written_grad + jnp.einsum(
        "cij,cin->cjn", intersection_grad, r_blocks, precision=PRECISE
    )
    product = mixing_grad * mixing
    decay_grad = decay_grad + jnp.transpose(
        jnp.sum(product, axis=3) - jnp.sum(product, axis=2), (0, 2, 1)
    )
    decay_grad = decay_grad.at[:, -1, :].add(last_extra)
    step_grad = jnp.sum(driven_grad * x_blocks, axis=3)
    x_state_grad = step_blocks[..., None] * driven_grad
    rate_grad = jnp.flip(jnp.cumsum(jnp.flip(decay_grad, axis=1), axis=1), axis=1)
    step_grad = step_grad + rate_grad * decay_rate[None, None, :]
    rate_total = jnp.sum(rate_grad * step_blocks, axis=(0, 1))
    return (x_state_grad, written_grad, readout_grad, step_grad, rate_total)


def on_device(
    block_in,
    cotangent,
    lengths,
    dest_slot,
    return_slot,
    norm_gain,
    inner_weight,
    state_weight,
    step_weight,
    conv_inner,
    conv_inner_bias,
    conv_state,
    conv_state_bias,
    step_bias,
    log_rate,
    skip_gain,
    gate_gain,
    out_weight,
):
    groups = lax.axis_size("dp")
    group_rows = block_in.shape[0]
    half_width = block_in.shape[1]
    capacity = 2 * group_rows // groups
    own_group = lax.axis_index("dp")
    own_dest = lax.dynamic_slice_in_dim(dest_slot, own_group * group_rows, group_rows)
    own_return = lax.dynamic_slice_in_dim(return_slot, own_group * group_rows, group_rows)
    send_spot = send_layout(own_dest, group_rows, capacity, groups)
    back_spot = send_layout(own_return, group_rows, capacity, groups)
    slots_in = arrivals(dest_slot, group_rows, capacity, groups, own_group)
    slots_back = arrivals(return_slot, group_rows, capacity, groups, own_group)
    blank_rows = jnp.zeros((groups * capacity, half_width), jnp.bfloat16)
    packed_rows = blank_rows.at[send_spot].set(block_in).reshape(groups, capacity, half_width)
    packed_grads = blank_rows.at[back_spot].set(cotangent).reshape(groups, capacity, half_width)
    came_rows, came_grads = (
        lax.all_to_all(packed_rows, "dp", split_axis=0, concat_axis=0, tiled=True),
        lax.all_to_all(packed_grads, "dp", split_axis=0, concat_axis=0, tiled=True),
    )
    empty_rows = jnp.zeros((group_rows, half_width), jnp.bfloat16)
    own_rows = empty_rows.at[slots_in].set(came_rows.reshape(-1, half_width), mode="drop")
    own_grads = empty_rows.at[slots_back].set(came_grads.reshape(-1, half_width), mode="drop")
    full_rows, full_grads = (
        lax.all_gather(own_rows, "tensor", axis=1, tiled=True),
        lax.all_gather(own_grads, "tensor", axis=1, tiled=True),
    )
    seq_pos, live_mask, keep_state = stretch_layout(lengths[0], STRETCH)
    live_col = live_mask[:, None]
    hidden = full_rows.astype(jnp.float32)
    norm_scale = lax.rsqrt(jnp.mean(hidden * hidden, axis=1, keepdims=True) + EPSILON)
    normed = (hidden * norm_scale * norm_gain).astype(jnp.bfloat16)
    inner_local = inner_weight.shape[2]
    zx_weight = inner_weight.reshape(inner_weight.shape[0], 2 * inner_local)
    projected = jnp.dot(normed, zx_weight, preferred_element_type=jnp.float32)
    gate_raw = projected[:, :inner_local]
    conv_in_x = projected[:, inner_local:]
    conv_in_state = jnp.dot(normed, state_weight, preferred_element_type=jnp.float32)
    step_raw = jnp.dot(normed, step_weight, preferred_element_type=jnp.float32)
    x_conv = conv_forward(conv_in_x, conv_inner, conv_inner_bias, seq_pos)
    state_conv = conv_forward(conv_in_state, conv_state, conv_state_bias, seq_pos)
    x_act = jax.nn.silu(x_conv)
    state_act = jax.nn.silu(state_conv)
    state_width = state_act.shape[1] // 2
    heads_local = step_weight.shape[1]
    head_dim = inner_local // heads_local
    stretches = group_rows // STRETCH
    step_input = step_raw + step_bias[None, :]
    step_size = jax.nn.softplus(step_input) * live_col
    decay_rate = -jnp.exp(log_rate)
    skip_wide = jnp.repeat(skip_gain, head_dim)[None, :]
    scanned, saved = state_forward(
        x_act.reshape(group_rows, heads_local, head_dim),
        state_act[:, :state_width],
        state_act[:, state_width:],
        step_size,
        decay_rate,
        STRETCH,
    )
    mixed = scanned + skip_wide * x_act
    gate_act = jax.nn.silu(gate_raw)
    gated = mixed * gate_act
    inner_total = inner_local * lax.axis_size("tensor")
    square_sum = lax.psum(jnp.sum(gated * gated, axis=1), "tensor")
    gate_scale = lax.rsqrt(square_sum / inner_total + EPSILON)[:, None]
    gate_normed = (gated * gate_scale * gate_gain).astype(jnp.bfloat16)
    partial_out = jnp.dot(gate_normed, out_weight, preferred_element_type=jnp.float32)
    branch_half = lax.psum_scatter(partial_out, "tensor", scatter_dimension=1, tiled=True)
    half_index = lax.axis_index("tensor")
    out_half = (own_rows.astype(jnp.float32) + live_col * branch_half).astype(jnp.bfloat16)
    zero_row = jnp.zeros((1, half_width), jnp.bfloat16)
    reply_rows = jnp.concatenate([out_half, zero_row], axis=0)[slots_back]
    returned = lax.all_to_all(
        reply_rows.reshape(groups, capacity, half_width),
        "dp",
        split_axis=0,
        concat_axis=0,
        tiled=True,
    )
    block_out = returned.reshape(-1, half_width)[back_spot]
    owner_ct = full_grads.astype(jnp.float32)
    out_grad = (owner_ct * live_col).astype(jnp.bfloat16)
    out_weight_grad = jnp.einsum(
        "ti,td->id", gate_normed, out_grad, preferred_element_type=jnp.float32
    )
    normed_out_grad = jnp.einsum(
        "td,id->ti", out_grad, out_weight, preferred_element_type=jnp.float32
    )
    gate_gain_grad = jnp.sum(normed_out_grad * gated * gate_scale, axis=0)
    scaled_grad = gate_gain * normed_out_grad
    cross = lax.psum(jnp.sum(gated * scaled_grad, axis=1), "tensor")[:, None]
    gated_grad = gate_scale * scaled_grad - gated * gate_scale**3 * cross / inner_total
    mixed_grad = gated_grad * gate_act
    gate_raw_grad = gated_grad * mixed * silu_slope(gate_raw)
    skip_gain_grad = jnp.sum(
        (mixed_grad * x_act).reshape(group_rows, heads_local, head_dim), axis=(0, 2)
    )
    x_state_grad, written_grad, readout_grad, step_grad, rate_total = state_backward(
        saved, mixed_grad.reshape(stretches, STRETCH, heads_local, head_dim), decay_rate
    )
    x_act_grad = x_state_grad.reshape(group_rows, inner_local) + skip_wide * mixed_grad
    state_grad = lax.psum(
        jnp.concatenate(
            [written_grad.reshape(group_rows, -1), readout_grad.reshape(group_rows, -1)], axis=1
        ),
        "tensor",
    )
    state_conv_grad = state_grad * silu_slope(state_conv)
    x_conv_grad = x_act_grad * silu_slope(x_conv)
    state_raw_grad, conv_state_grad, conv_state_bias_grad = conv_backward(
        conv_in_state, conv_state, seq_pos, state_conv_grad
    )
    x_raw_grad, conv_inner_grad, conv_inner_bias_grad = conv_backward(
        conv_in_x, conv_inner, seq_pos, x_conv_grad
    )
    step_raw_grad = (
        step_grad.reshape(group_rows, heads_local) * live_col * jax.nn.sigmoid(step_input)
    )
    step_bias_grad = jnp.sum(step_raw_grad, axis=0)
    log_rate_grad = rate_total * decay_rate
    zx_low = jnp.concatenate([gate_raw_grad, x_raw_grad], axis=1).astype(jnp.bfloat16)
    state_low = state_raw_grad.astype(jnp.bfloat16)
    step_low = step_raw_grad.astype(jnp.bfloat16)
    inner_weight_grad = jnp.einsum(
        "td,tk->dk", normed, zx_low, preferred_element_type=jnp.float32
    ).reshape(inner_weight.shape)
    state_weight_grad = jnp.einsum(
        "td,tk->dk", normed, state_low, preferred_element_type=jnp.float32
    )
    step_weight_grad = jnp.einsum("td,tk->dk", normed, step_low, preferred_element_type=jnp.float32)
    lead_share = (half_index == 0).astype(jnp.float32)
    normed_grad = jnp.einsum("tk,dk->td", zx_low, zx_weight, preferred_element_type=jnp.float32)
    normed_grad = normed_grad + jnp.einsum(
        "tk,dk->td", step_low, step_weight, preferred_element_type=jnp.float32
    )
    normed_grad = normed_grad + lead_share * jnp.einsum(
        "tk,dk->td", state_low, state_weight, preferred_element_type=jnp.float32
    )
    normed_grad = lax.psum(normed_grad, "tensor")
    norm_gain_grad = jnp.sum(normed_grad * hidden * norm_scale, axis=0)
    input_scaled = norm_gain * normed_grad
    hidden_grad = (
        norm_scale * input_scaled
        - hidden * norm_scale**3 * jnp.mean(hidden * input_scaled, axis=1, keepdims=True)
        + owner_ct
    )
    own_grad = lax.dynamic_slice_in_dim(hidden_grad, half_index * half_width, half_width, 1).astype(
        jnp.bfloat16
    )
    answer_rows = jnp.concatenate([own_grad, zero_row], axis=0)[slots_in]
    gone = lax.all_to_all(
        answer_rows.reshape(groups, capacity, half_width),
        "dp",
        split_axis=0,
        concat_axis=0,
        tiled=True,
    )
    input_grad = gone.reshape(-1, half_width)[send_spot]
    (
        conv_inner_grad,
        conv_inner_bias_grad,
        conv_state_grad,
        conv_state_bias_grad,
        step_bias_grad,
        log_rate_grad,
        skip_gain_grad,
        gate_gain_grad,
    ) = lax.psum(
        (
            conv_inner_grad,
            conv_inner_bias_grad,
            conv_state_grad,
            conv_state_bias_grad,
            step_bias_grad,
            log_rate_grad,
            skip_gain_grad,
            gate_gain_grad,
        ),
        "dp",
    )
    zx_share, state_share, step_share, gain_share, out_share = (
        lax.psum_scatter(inner_weight_grad, "dp", scatter_dimension=0, tiled=True),
        lax.psum_scatter(state_weight_grad, "dp", scatter_dimension=0, tiled=True),
        lax.psum_scatter(step_weight_grad, "dp", scatter_dimension=0, tiled=True),
        lax.psum_scatter(norm_gain_grad, "dp", scatter_dimension=0, tiled=True),
        lax.psum_scatter(out_weight_grad, "dp", scatter_dimension=1, tiled=True),
    )
    return (
        block_out,
        input_grad,
        gain_share,
        zx_share,
        state_share,
        step_share,
        conv_inner_grad,
        conv_inner_bias_grad,
        conv_state_grad,
        conv_state_bias_grad,
        step_bias_grad,
        log_rate_grad,
        skip_gain_grad,
        gate_gain_grad,
        out_share,
    )


def solution(mesh):
    placed = (
        P("dp", "tensor"),
        P("dp", "tensor"),
        P("dp", None),
        P(),
        P(),
        P(),
        P(None, None, "tensor"),
        P(),
        P(None, "tensor"),
        P(None, "tensor"),
        P("tensor"),
        P(),
        P(),
        P("tensor"),
        P("tensor"),
        P("tensor"),
        P("tensor"),
        P("tensor", None),
    )
    return jax.shard_map(
        on_device,
        mesh=mesh,
        in_specs=placed,
        out_specs=(
            P("dp", "tensor"),
            P("dp", "tensor"),
            P("dp"),
            P("dp", None, "tensor"),
            P("dp", None),
            P("dp", "tensor"),
            P(None, "tensor"),
            P("tensor"),
            P(),
            P(),
            P("tensor"),
            P("tensor"),
            P("tensor"),
            P("tensor"),
            P("tensor", "dp"),
        ),
        check_vma=False,
    )
```

profile of v0, /device:TPU:0, one launch (start us, length us, event | category | flops | bytes accessed | tf_op | source)
XLA Modules:
  0.0 952.2 jit_solution(12864653479343501964)
XLA Ops:
  13.6 7.4 all-to-all-start
  24.7 9.8 %copy.282 = bf16[192,8,2,1536]{3,1,2,0:T(8,128)(2,1)} copy(bf16[192,8,2,1536]{3,2,1,0:T(2,128)(2,1)} %bitcast.209) | data formatting | bytes 18874368
  34.6 15.5 %scatter_custom_fusion.3 = s32[512]{0:T(512)S(1)} fusion(s32[4096]{0:T(1024)S(1)} %get-tuple-element.95, s32[4096]{0:T(1024)S(1)} %get-tuple-element.94, s32[]{:T(128)} %constant.149.clone.1), kind=kCustom, calls=%fused_computation.245 | custom fusion | bytes 2052 | tf_op jit(solution)/shard_map/scatter | solution.py:85
  50.1 15.5 %scatter_custom_fusion = s32[512]{0:T(512)S(1)} fusion(s32[4096]{0:T(1024)S(1)} %get-tuple-element.96, s32[4096]{0:T(1024)S(1)} %get-tuple-element.97, s32[]{:T(128)} %constant.149.clone.1), kind=kCustom, calls=%fused_computation.247 | custom fusion | bytes 2052 | tf_op jit(solution)/shard_map/scatter | solution.py:85
  71.3 6.0 all-to-all-start.2
  80.1 12.5 %all_gather.6 = bf16[256,1536]{1,0:T(8,128)(2,1)S(1)} all-gather(bf16[256,768]{1,0:T(8,128)(2,1)S(1)} %scatter_custom_fusion.2), channel_id=1, replica_groups=mesh['dp'=16,'tensor'=2] {'tensor'}, dimensions={1}, use_global_device_ids=true | all-gather | bytes 1179648 | tf_op jit(solution)/shard_map/all_gather | solution.py:242
  107.9 11.5 %all_gather.7 = bf16[256,1536]{1,0:T(8,128)(2,1)} all-gather(bf16[256,768]{1,0:T(8,128)(2,1)S(1)} %scatter_custom_fusion.5), channel_id=1, replica_groups=mesh['dp'=16,'tensor'=2] {'tensor'}, dimensions={1}, use_global_device_ids=true | all-gather | bytes 1179648 | tf_op jit(solution)/shard_map/all_gather | solution.py:243
  130.4 6.3 multiply_multiply_fusion
  142.2 9.7 %bitcast_add_fusion.1 = f32[1,256,24,64]{1,3,2,0:T(8,128)} fusion(f32[256,24,64]{0,2,1:T(8,128)} %convolution_multiply_fusion.1, f32[24,256]{1,0:T(8,128)S(1)} %bitcast_add_fusion.4, f32[256,256]{1,0:T(8,128)} %fusion.58, pred[256,256]{1,0:T(8,128)(4,1)} %iota_compare_fusion, f32[256,24,64]{0,2,1:T(8,128)} %bitcast.212, f32[256,24]{0,1:T(8,128)} %get-tuple-element.79), kind=kOutput, calls=%fused_computation.33 | convolution fusion | flops 1215037440 | bytes 5095424 | tf_op jit(solution)/shard_map/chij,cjhp->cihp/dot_general | solution.py:118
  166.3 6.3 multiply_reduce_fusion.1
  172.7 5.8 psum.85
  189.7 10.8 %fusion.6 = (f32[24,256]{1,0:T(8,128)}, f32[24,256]{1,0:T(8,128)}, f32[256,256]{1,0:T(8,128)}) fusion(f32[24,256]{1,0:T(8,128)} %copy-done.62, f32[256,256]{1,0:T(8,128)} %fusion.58, pred[256,256]{1,0:T(8,128)(4,1)} %iota_compare_fusion, f32[256,24,64]{0,2,1:T(8,128)S(1)} %bitcast.218, f32[256,24,64]{0,2,1:T(8,128)S(1)} %bitcast.214, ...), kind=kOutput, calls=%fused_computation.16 | convolution fusion | flops 1224003584 | bytes 3833856 | tf_op jit(solution)/shard_map/cihp,cjhp->chij/dot_general | solution.py:177
  220.1 9.1 multiply_reduce_fusion.11
  274.5 13.0 %all-reduce.21.cloned.1.call-done = f32[256,256]{1,0:T(8,128)} async-done(((f32[256,256]{1,0:T(8,128)}), f32[256,256]{1,0:T(8,128)}) %all-reduce.21.cloned.1.call-update) | async-done | bytes 262160 | tf_op jit(solution)/shard_map/psum | solution.py:319
  301.3 9.7 %fusion.28 = f32[1536,3072]{1,0:T(8,128)} fusion(bf16[256,1536]{1,0:T(8,128)(2,1)} %copy-done.21, bf16[256,1536]{1,0:T(8,128)(2,1)} %get-tuple-element.80, bf16[256,1536]{1,0:T(8,128)(2,1)S(1)} %all_gather.6, f32[1536]{0:T(1024)S(1)} %copy-done.27, f32[256]{0:T(256)S(1)} %copy-done.47), kind=kOutput, calls=%fused_computation.71 | convolution fusion | flops 2420637696 | bytes 21240832 | tf_op jit(solution)/shard_map/td,tk->dk/dot_general | solution.py:341
  311.0 24.6 %reshape.521 = f32[1536,2,1536]{2,1,0:T(2,128)} reshape(f32[1536,3072]{1,0:T(8,128)} %fusion.28) | data formatting | bytes 37748736 | tf_op jit(solution)/shard_map/reshape | solution.py:343
  337.5 6.3 fusion.46
  358.3 14.5 %reduce-scatter.7.cloned.1.call-done = f32[256,768]{1,0:T(8,128)} async-done(((f32[256,1536]{1,0:T(8,128)}), f32[256,768]{1,0:T(8,128)}) %reduce-scatter.7.cloned.1.call-update) | async-done | bytes 786448 | tf_op jit(solution)/shard_map/reduce_scatter | solution.py:285
  377.0 5.8 all-to-all-start.1
  384.6 48.6 %reduce-scatter.13.cloned.1.call-done = f32[96,24]{1,0:T(8,128)} async-done(((f32[1536,24]{1,0:T(8,128)}), f32[96,24]{1,0:T(8,128)}) %reduce-scatter.13.cloned.1.call-update) | async-done | bytes 9232
  434.7 61.7 %all-reduce.16 = (f32[1536]{0:T(1024)S(1)}, f32[4,1536]{1,0:T(4,128)}, f32[1536]{0:T(1024)}, f32[4,256]{1,0:T(4,128)}, f32[256]{0:T(256)}, /*index=5*/f32[24]{0:T(128)}, f32[24]{0:T(128)}, f32[24]{0:T(128)}, f32[1536]{0:T(1024)}) all-reduce(f32[1536]{0:T(1024)S(1)} %get-tuple-element.34, ...), channel_id=3, replica_groups=mesh['dp'=16,'tensor'=2] {'dp'}, use_global_device_ids=true, to_apply=%region_37.38.clone | all-reduce | flops 12104 | bytes 96832
  500.8 264.9 %all-reduce.25.cloned.1.call-done = f32[1536,2,1536]{2,1,0:T(2,128)} async-done(((f32[1536,2,1536]{2,1,0:T(2,128)}), f32[1536,2,1536]{2,1,0:T(2,128)}) %all-reduce.25.cloned.1.call-update) | async-done | bytes 18874384
  768.1 61.8 %reduce-scatter.9.cloned.1.call-done = f32[96,256]{1,0:T(8,128)} async-done(((f32[1536,256]{1,0:T(8,128)}), f32[96,256]{1,0:T(8,128)}) %reduce-scatter.9.cloned.1.call-update) | async-done | bytes 98320 | tf_op jit(solution)/shard_map/reduce_scatter | solution.py:400
  829.8 115.1 %reduce-scatter.11.cloned.1.call-done = f32[1536,96]{0,1:T(8,128)} async-done(((f32[1536,1536]{0,1:T(8,128)}), f32[1536,96]{0,1:T(8,128)}) %reduce-scatter.11.cloned.1.call-update) | async-done | bytes 589840 | tf_op jit(solution)/shard_map/reduce_scatter | solution.py:403
  (393 shorter events, 182.8 us)
Async XLA Ops:
  7.2 113.8 %copy-start = (bf16[1536,256]{1,0:T(8,128)(2,1)S(1)}, bf16[1536,256]{1,0:T(8,128)(2,1)}, u32[]{:S(2)}) copy-start(bf16[1536,256]{1,0:T(8,128)(2,1)} %param.27) | copy-start | bytes 2359300
  13.6 57.7 %all-to-all-start = ((bf16[16,32,768]{2,1,0:T(8,128)(2,1)}), bf16[16,32,768]{2,1,0:T(8,128)(2,1)S(1)}, u32[]{:S(2)}, u32[]{:S(2)}) async-start(bf16[16,32,768]{2,1,0:T(8,128)(2,1)} %bitcast.4), calls=%async_computation | async-start | bytes 1572864 | tf_op jit(solution)/shard_map/all_to_all | solution.py:235
  68.7 52.8 %copy-start.63 = (f32[256]{0:T(256)}, f32[256]{0:T(256)S(1)}, u32[]{:S(2)}) copy-start(f32[256]{0:T(256)S(1)} %compare_convert_fusion.2) | copy-start | bytes 3076
  68.7 52.7 %copy-start.54 = (f32[256]{0:T(256)}, f32[256]{0:T(256)S(1)}, u32[]{:S(2)}) copy-start(f32[256]{0:T(256)S(1)} %get-tuple-element.117) | copy-start | bytes 3076
  68.7 52.7 %copy-start.57 = (f32[256]{0:T(256)}, f32[256]{0:T(256)S(1)}, u32[]{:S(2)}) copy-start(f32[256]{0:T(256)S(1)} %get-tuple-element.118) | copy-start | bytes 3076
  71.3 50.2 %copy-start.73 = (f32[1,256]{1,0:T(1,128)}, f32[1,256]{1,0:T(1,128)S(1)}, u32[]{:S(2)}) copy-start(f32[1,256]{1,0:T(1,128)S(1)} %get-tuple-element.99) | copy-start | bytes 3076
  71.3 33.8 %all-to-all-start.2 = ((bf16[16,32,768]{2,1,0:T(8,128)(2,1)}), bf16[16,32,768]{2,1,0:T(8,128)(2,1)S(1)}, u32[]{:S(2)}, u32[]{:S(2)}) async-start(bf16[16,32,768]{2,1,0:T(8,128)(2,1)} %bitcast.31), calls=%async_computation.3 | async-start | bytes 1572864 | tf_op jit(solution)/shard_map/all_to_all | solution.py:236
  77.4 210.2 %all-reduce.21.cloned.1.call-start = ((), (), s32[]{:S(2)}) async-start(), calls=%async_computation.9 | async-start | bytes 524288 | tf_op jit(solution)/shard_map/psum | solution.py:319
  263.4 83.8 %all-reduce.23.cloned.1.call-start = ((), (), s32[]{:S(2)}) async-start(), calls=%async_computation.10 | async-start | bytes 3145728 | tf_op jit(solution)/shard_map/psum | solution.py:356
  292.8 80.0 %reduce-scatter.7.cloned.1.call-start = ((), (), s32[]{:S(2)}) async-start(), calls=%async_computation.8 | async-start | bytes 2359296 | tf_op jit(solution)/shard_map/reduce_scatter | solution.py:285
  299.1 134.0 %reduce-scatter.13.cloned.1.call-start = ((), (), s32[]{:S(2)}) async-start(), calls=%async_computation.13 | async-start | bytes 835584
  301.3 464.4 %all-reduce.25.cloned.1.call-start = ((), (), s32[]{:S(2)}) async-start(), calls=%async_computation.14 | async-start | bytes 37748736
  335.7 494.1 %reduce-scatter.9.cloned.1.call-start = ((), (), s32[]{:S(2)}) async-start(), calls=%async_computation.11 | async-start | bytes 1671168 | tf_op jit(solution)/shard_map/reduce_scatter | solution.py:400
  337.4 607.4 %reduce-scatter.11.cloned.1.call-start = ((), (), s32[]{:S(2)}) async-start(), calls=%async_computation.12 | async-start | bytes 10027008 | tf_op jit(solution)/shard_map/reduce_scatter | solution.py:403
  352.6 24.5 %all-to-all-start.3 = ((bf16[16,32,768]{2,1,0:T(8,128)(2,1)}), bf16[16,32,768]{2,1,0:T(8,128)(2,1)S(1)}, u32[]{:S(2)}, u32[]{:S(2)}) async-start(bf16[16,32,768]{2,1,0:T(8,128)(2,1)} %bitcast.60), calls=%async_computation.4 | async-start | bytes 1572864 | tf_op jit(solution)/shard_map/all_to_all | solution.py:368
  376.9 57.7 %copy-start.83 = (f32[256]{0:T(256)S(1)}, f32[256]{0:T(256)}, u32[]{:S(2)}) copy-start(f32[256]{0:T(256)} %get-tuple-element.56) | copy-start | bytes 3076
  377.0 57.7 %copy-start.84 = (f32[256]{0:T(256)S(1)}, f32[256]{0:T(256)}, u32[]{:S(2)}) copy-start(f32[256]{0:T(256)} %get-tuple-element.90) | copy-start | bytes 3076
  377.0 57.7 %copy-start.85 = (f32[256]{0:T(256)S(1)}, f32[256]{0:T(256)}, u32[]{:S(2)}) copy-start(f32[256]{0:T(256)} %get-tuple-element.92) | copy-start | bytes 3076
  377.0 57.7 %copy-start.92 = (f32[256]{0:T(256)S(1)}, f32[256]{0:T(256)}, u32[]{:S(2)}) copy-start(f32[256]{0:T(256)} %get-tuple-element.37) | copy-start | bytes 3076
  377.0 57.7 %copy-start.48 = (f32[1536]{0:T(1024)S(1)}, f32[1536]{0:T(1024)}, u32[]{:S(2)}) copy-start(f32[1536]{0:T(1024)} %get-tuple-element.32) | copy-start | bytes 18436
  377.0 57.7 %copy-start.79 = (f32[1536]{0:T(1024)S(1)}, f32[1536]{0:T(1024)}, u32[]{:S(2)}) copy-start(f32[1536]{0:T(1024)} %get-tuple-element.30) | copy-start | bytes 18436
  377.0 57.7 %copy-start.91 = (f32[256]{0:T(256)S(1)}, f32[256]{0:T(256)}, u32[]{:S(2)}) copy-start(f32[256]{0:T(256)} %get-tuple-element.36) | copy-start | bytes 3076
  377.0 57.7 %copy-start.94 = (f32[24]{0:T(128)S(1)}, f32[24]{0:T(128)}, u32[]{:S(2)}) copy-start(f32[24]{0:T(128)} %get-tuple-element.53) | copy-start | bytes 292
  377.0 121.9 %all-to-all-start.1 = ((bf16[16,32,768]{2,1,0:T(8,128)(2,1)}), bf16[16,32,768]{2,1,0:T(8,128)(2,1)S(1)}, u32[]{:S(2)}, u32[]{:S(2)}) async-start(bf16[16,32,768]{2,1,0:T(8,128)(2,1)} %bitcast.27), calls=%async_computation.2 | async-start | bytes 1572864 | tf_op jit(solution)/shard_map/all_to_all | solution.py:290
  (90 other events, 918.3 us)
Sparse Core Ops, SparseCore 0:
  263.5 23.9 all-reduce.20
  292.9 51.4 all-reduce.22
  346.7 26.0 reduce-scatter.6
  376.6 56.4 reduce-scatter.12
  436.8 328.8 all-reduce.24
  770.2 59.5 reduce-scatter.8
  834.5 110.3 reduce-scatter.10
where the time goes:
time: 963 us; the launch traced here: 952 us
  waiting for transfers between devices  518 us (54%)
  local copies, waits for them, and re-layouts  145 us (15%)
  blocking collectives  97 us (10%)
  matrix products  90.1 us (9%)
  other arithmetic  59.2 us (6%)
  starting transfers between devices  25.1 us (3%)
  between operations  17.4 us (2%)
    unnamed x9, waiting for transfers between devices  314 us
    reduce_scatter x1, waiting for transfers between devices, on_device(): lax.psum_scatter(out_weight_grad, 'dp', scatter_dimension=1, tiled=True)  115 us
    reduce_scatter x1, waiting for transfers between devices, on_device(): lax.psum_scatter(state_weight_grad, 'dp', scatter_dimension=0, tiled=True)  61.8 us
    unnamed x1, blocking collectives  61.7 us
    scatter x2, local copies, waits for them, and re-layouts, arrivals(): filler.at[position.reshape(-1)]  31 us
    reshape x1, local copies, waits for them, and re-layouts, on_device(): inner_weight_grad = jnp.einsum('td,tk->dk', normed, zx_low, preferred_ele...  24.6 us
    unnamed x213, local copies, waits for them, and re-layouts  20.7 us
  transfers between devices with their start and end apart: 11, of which 6 were waited for; matrix products, arithmetic and copies ran while one was open for 15% of the time, Pallas kernels for 0%

commit v1 on v0

--- a/solution.py
+++ b/solution.py
@@ -340,7 +340,7 @@
     step_low = step_raw_grad.astype(jnp.bfloat16)
     inner_weight_grad = jnp.einsum(
         "td,tk->dk", normed, zx_low, preferred_element_type=jnp.float32
-    ).reshape(inner_weight.shape)
+    )
     state_weight_grad = jnp.einsum(
         "td,tk->dk", normed, state_low, preferred_element_type=jnp.float32
     )
@@ -396,12 +396,14 @@
         "dp",
     )
     zx_share, state_share, step_share, gain_share, out_share = (
-        lax.psum_scatter(inner_weight_grad, "dp", scatter_dimension=0, tiled=True),
+        lax.psum_scatter(inner_weight_grad.astype(jnp.bfloat16), "dp", scatter_dimension=0, tiled=True),
         lax.psum_scatter(state_weight_grad, "dp", scatter_dimension=0, tiled=True),
         lax.psum_scatter(step_weight_grad, "dp", scatter_dimension=0, tiled=True),
         lax.psum_scatter(norm_gain_grad, "dp", scatter_dimension=0, tiled=True),
-        lax.psum_scatter(out_weight_grad, "dp", scatter_dimension=1, tiled=True),
-    )
+        lax.psum_scatter(out_weight_grad.astype(jnp.bfloat16), "dp", scatter_dimension=1, tiled=True),
+    )
+    zx_share = zx_share.astype(jnp.float32).reshape((-1,) + inner_weight.shape[1:])
+    out_share = out_share.astype(jnp.float32)
     return (
         block_out,
         input_grad,

time: 963 us -> 698 us (0.72)
  waiting for transfers between devices: 518 us -> 280 us
  local copies, waits for them, and re-layouts: 145 us -> 126 us
    unnamed x9 -> x8, waiting for transfers between devices: 314 us -> 48.5 us
    psum x1, waiting for transfers between devices: 0.01 us -> 28.5 us  [on_device(): normed_grad = lax.psum(normed_grad, 'tensor')]
    reshape x1, local copies, waits for them, and re-layouts: 24.6 us -> 3.06 us  [on_device(): zx_share.astype(jnp.float32).reshape((-1,) + inner_weight.shape[1:])]
    psum x1, waiting for transfers between devices: 13 us -> 0.03 us  [on_device(): lax.psum(jnp.concatenate([written_grad.reshape(group_rows, -1), readout_g...]
    reduce_scatter x1 -> x2, waiting for transfers between devices: 115 us -> 127 us  [the longest x1 113 us: on_device(): lax.psum_scatter(inner_weight_grad.astype(jnp.bfloat16), 'dp', scatter_di...]
    unnamed x213 -> x206, local copies, waits for them, and re-layouts: 20.7 us -> 21.1 us
  transfers between devices with their start and end apart: 11 -> 11, of which waited for: 6 -> 6; matrix products, arithmetic and copies ran while one was open for 15% -> 26% of each run, Pallas kernels for 0% -> 0%
where the time goes in v1:
time: 698 us; the launch traced here: 688 us
  waiting for transfers between devices  280 us (40%)
  local copies, waits for them, and re-layouts  126 us (18%)
  blocking collectives  93.5 us (13%)
  matrix products  86.2 us (12%)
  other arithmetic  59.9 us (9%)
  starting transfers between devices  25.3 us (4%)
  between operations  16.9 us (2%)
    reduce_scatter x1, waiting for transfers between devices, on_device(): lax.psum_scatter(inner_weight_grad.astype(jnp.bfloat16), 'dp', scatter_di...  113 us
    reduce_scatter x1, waiting for transfers between devices, on_device(): lax.psum_scatter(state_weight_grad, 'dp', scatter_dimension=0, tiled=True)  60.5 us
    unnamed x1, blocking collectives  59.3 us
    unnamed x8, waiting for transfers between devices  48.5 us
    scatter x2, local copies, waits for them, and re-layouts, arrivals(): filler.at[position.reshape(-1)]  31 us
    psum x1, waiting for transfers between devices, on_device(): normed_grad = lax.psum(normed_grad, 'tensor')  28.5 us
    unnamed x206, local copies, waits for them, and re-layouts  21.1 us
    reduce_scatter x1, waiting for transfers between devices, on_device(): lax.psum_scatter(partial_out, 'tensor', scatter_dimension=1, tiled=True)  16 us
  transfers between devices with their start and end apart: 11, of which 6 were waited for; matrix products, arithmetic and copies ran while one was open for 26% of the time, Pallas kernels for 0%

profile of v1, /device:TPU:0, one launch (start us, length us, event | category | flops | bytes accessed | tf_op | source)
XLA Modules:
  0.0 687.9 jit_solution(11035838053878036620)
XLA Ops:
  13.6 7.4 %all-to-all-start = ((bf16[16,32,768]{2,1,0:T(8,128)(2,1)}), bf16[16,32,768]{2,1,0:T(8,128)(2,1)S(1)}, u32[]{:S(2)}, u32[]{:S(2)}) async-start(bf16[16,32,768]{2,1,0:T(8,128)(2,1)} %bitcast.4), calls=%async_computation | async-start | bytes 1572864 | tf_op jit(solution)/shard_map/all_to_all | solution.py:235
  24.6 9.8 %copy.282 = bf16[192,8,2,1536]{3,1,2,0:T(8,128)(2,1)} copy(bf16[192,8,2,1536]{3,2,1,0:T(2,128)(2,1)} %bitcast.203) | data formatting | bytes 18874368
  34.6 15.5 %scatter_custom_fusion = s32[512]{0:T(512)S(1)} fusion(s32[4096]{0:T(1024)S(1)} %get-tuple-element.96, s32[4096]{0:T(1024)S(1)} %get-tuple-element.97, s32[]{:T(128)} %constant.149.clone.1), kind=kCustom, calls=%fused_computation.247 | custom fusion | bytes 2052 | tf_op jit(solution)/shard_map/scatter | solution.py:85
  53.2 15.5 %scatter_custom_fusion.3 = s32[512]{0:T(512)S(1)} fusion(s32[4096]{0:T(1024)S(1)} %get-tuple-element.95, s32[4096]{0:T(1024)S(1)} %get-tuple-element.94, s32[]{:T(128)} %constant.149.clone.1), kind=kCustom, calls=%fused_computation.245 | custom fusion | bytes 2052 | tf_op jit(solution)/shard_map/scatter | solution.py:85
  73.0 6.1 all-to-all-start.2
  81.8 12.5 %all_gather.6 = bf16[256,1536]{1,0:T(8,128)(2,1)S(1)} all-gather(bf16[256,768]{1,0:T(8,128)(2,1)S(1)} %scatter_custom_fusion.2), channel_id=1, replica_groups=mesh['dp'=16,'tensor'=2] {'tensor'}, dimensions={1}, use_global_device_ids=true | all-gather | bytes 1179648 | tf_op jit(solution)/shard_map/all_gather | solution.py:242
  111.8 6.2 multiply_multiply_fusion
  133.8 9.7 %bitcast_add_fusion.1 = f32[1,256,24,64]{1,3,2,0:T(8,128)} fusion(f32[256,24,64]{0,2,1:T(8,128)} %convolution_multiply_fusion.1, f32[24,256]{1,0:T(8,128)S(1)} %bitcast_add_fusion.4, f32[256,256]{1,0:T(8,128)} %fusion.56, pred[256,256]{1,0:T(8,128)(4,1)} %iota_compare_fusion, f32[256,24,64]{0,2,1:T(8,128)} %bitcast.206, f32[256,24]{0,1:T(8,128)} %copy-done.29), kind=kOutput, calls=%fused_computation.35 | convolution fusion | flops 1215037440 | bytes 5095424 | tf_op jit(solution)/shard_map/chij,cjhp->cihp/dot_general | solution.py:118
  151.0 5.8 psum.84
  166.5 10.3 %all_gather.7 = bf16[256,1536]{1,0:T(8,128)(2,1)S(1)} all-gather(bf16[256,768]{1,0:T(8,128)(2,1)} %scatter_custom_fusion.5), channel_id=1, replica_groups=mesh['dp'=16,'tensor'=2] {'tensor'}, dimensions={1}, use_global_device_ids=true | all-gather | bytes 1179648 | tf_op jit(solution)/shard_map/all_gather | solution.py:243
  176.8 6.4 multiply_reduce_fusion.1
  197.3 11.8 %fusion.6 = (f32[24,256]{1,0:T(8,128)}, f32[24,256]{1,0:T(8,128)}, f32[256,256]{1,0:T(8,128)}) fusion(f32[24,256]{1,0:T(8,128)} %copy-done.64, f32[256,256]{1,0:T(8,128)} %fusion.56, pred[256,256]{1,0:T(8,128)(4,1)} %iota_compare_fusion, f32[256,24,64]{0,2,1:T(8,128)} %bitcast.210, f32[256,24,64]{0,2,1:T(8,128)} %bitcast.208, f32[256,24]{0,1:T(8,128)} %copy-done.29), kind=kOutput, calls=%fused_computation.18 | convolution fusion | flops 1224003584 | bytes 3833856 | tf_op jit(solution)/shard_map/cihp,cjhp->chij/dot_general | solution.py:177
  211.0 7.5 %multiply_reduce_fusion.11 = (f32[256,24]{0,1:T(8,128)}, f32[1,256,24,64]{1,3,2,0:T(8,128)}) fusion(f32[1,256,24,64]{1,3,2,0:T(8,128)S(1)} %bitcast.209, f32[256,24]{0,1:T(8,128)S(1)} %copy-done.30, f32[256,24,64]{0,2,1:T(8,128)S(1)} %bitcast.212, f32[24,256]{1,0:T(8,128)S(1)} %copy-done.65, f32[256,256]{1,0:T(8,128)S(1)} %copy-done.32, ...), kind=kOutput, calls=%fused_computation.47 | convolution fusion | flops 1216210944 | bytes 6717440 | tf_op jit(solution)/shard_map/chij,cihp->cjhp/dot_general | solution.py:179
  226.7 5.7 fusion.104
  269.2 5.6 fusion.28
  306.5 28.5 %all-reduce.21.cloned.1.call-done = f32[256,1536]{1,0:T(8,128)} async-done(((f32[256,1536]{1,0:T(8,128)}), f32[256,1536]{1,0:T(8,128)}) %all-reduce.21.cloned.1.call-update) | async-done | bytes 1572880 | tf_op jit(solution)/shard_map/psum | solution.py:356
  340.0 5.6 all-to-all-start.3
  347.4 16.0 %reduce-scatter.8.cloned.1.call-done = f32[256,768]{1,0:T(8,128)} async-done(((f32[256,1536]{1,0:T(8,128)}), f32[256,768]{1,0:T(8,128)}) %reduce-scatter.8.cloned.1.call-update) | async-done | bytes 786448 | tf_op jit(solution)/shard_map/reduce_scatter | solution.py:285
  367.6 5.9 all-to-all-start.1
  375.3 48.4 %reduce-scatter.16.cloned.1.call-done = f32[96,24]{1,0:T(8,128)} async-done(((f32[1536,24]{1,0:T(8,128)}), f32[96,24]{1,0:T(8,128)}) %reduce-scatter.16.cloned.1.call-update) | async-done | bytes 9232
  425.2 59.3 %all-reduce.15 = (f32[1536]{0:T(1024)S(1)}, f32[4,1536]{1,0:T(4,128)}, f32[1536]{0:T(1024)}, f32[4,256]{1,0:T(4,128)}, f32[256]{0:T(256)}, /*index=5*/f32[24]{0:T(128)}, f32[24]{0:T(128)}, f32[24]{0:T(128)}, f32[1536]{0:T(1024)}) all-reduce(f32[1536]{0:T(1024)S(1)} %get-tuple-element.34, ...), channel_id=3, replica_groups=mesh['dp'=16,'tensor'=2] {'dp'}, use_global_device_ids=true, to_apply=%region_37.38.clone | all-reduce | flops 12104 | bytes 96832
  488.9 13.4 %reduce-scatter.14.cloned.1.call-done = bf16[1536,96]{0,1:T(8,128)(2,1)} async-done(((bf16[1536,1536]{0,1:T(8,128)(2,1)}), bf16[1536,96]{0,1:T(8,128)(2,1)}) %reduce-scatter.14.cloned.1.call-update) | async-done | bytes 294928 | tf_op jit(solution)/shard_map/reduce_scatter | solution.py:403
  504.2 113.1 %reduce-scatter.10.cloned.1.call-done = bf16[96,3072]{1,0:T(8,128)(2,1)} async-done(((bf16[1536,3072]{1,0:T(8,128)(2,1)}), bf16[96,3072]{1,0:T(8,128)(2,1)}) %reduce-scatter.10.cloned.1.call-update) | async-done | bytes 589840 | tf_op jit(solution)/shard_map/reduce_scatter | solution.py:399
  620.4 60.5 %reduce-scatter.12.cloned.1.call-done = f32[96,256]{1,0:T(8,128)} async-done(((f32[1536,256]{1,0:T(8,128)}), f32[96,256]{1,0:T(8,128)}) %reduce-scatter.12.cloned.1.call-update) | async-done | bytes 98320 | tf_op jit(solution)/shard_map/reduce_scatter | solution.py:400
  (387 shorter events, 184.4 us)
Async XLA Ops:
  7.2 115.6 %copy-start = (bf16[1536,256]{1,0:T(8,128)(2,1)S(1)}, bf16[1536,256]{1,0:T(8,128)(2,1)}, u32[]{:S(2)}) copy-start(bf16[1536,256]{1,0:T(8,128)(2,1)} %param.27) | copy-start | bytes 2359300
  13.6 59.4 %all-to-all-start = ((bf16[16,32,768]{2,1,0:T(8,128)(2,1)}), bf16[16,32,768]{2,1,0:T(8,128)(2,1)S(1)}, u32[]{:S(2)}, u32[]{:S(2)}) async-start(bf16[16,32,768]{2,1,0:T(8,128)(2,1)} %bitcast.4), calls=%async_computation | async-start | bytes 1572864 | tf_op jit(solution)/shard_map/all_to_all | solution.py:235
  24.6 46.0 %copy-start.62 = (f32[4,1536]{1,0:T(4,128)S(1)}, f32[4,1536]{1,0:T(4,128)}, u32[]{:S(2)}) copy-start(f32[4,1536]{1,0:T(4,128)} %param.29) | copy-start | bytes 73732
  24.6 46.6 %copy-start.97 = (f32[24]{0:T(128)S(1)}, f32[24]{0:T(128)}, u32[]{:S(2)}) copy-start(f32[24]{0:T(128)} %param.34) | copy-start | bytes 292
  24.6 47.8 %copy-start.87 = (f32[4,256]{1,0:T(4,128)S(1)}, f32[4,256]{1,0:T(4,128)}, u32[]{:S(2)}) copy-start(f32[4,256]{1,0:T(4,128)} %param.31) | copy-start | bytes 12292
  73.0 89.6 %all-to-all-start.2 = ((bf16[16,32,768]{2,1,0:T(8,128)(2,1)}), bf16[16,32,768]{2,1,0:T(8,128)(2,1)}, u32[]{:S(2)}, u32[]{:S(2)}) async-start(bf16[16,32,768]{2,1,0:T(8,128)(2,1)} %bitcast.31), calls=%async_computation.3 | async-start | bytes 1572864 | tf_op jit(solution)/shard_map/all_to_all | solution.py:236
  79.0 198.0 %all-reduce.19.cloned.1.call-start = ((), (), s32[]{:S(2)}) async-start(), calls=%async_computation.10 | async-start | bytes 524288 | tf_op jit(solution)/shard_map/psum | solution.py:319
  252.6 82.3 %all-reduce.21.cloned.1.call-start = ((), (), s32[]{:S(2)}) async-start(), calls=%async_computation.11 | async-start | bytes 3145728 | tf_op jit(solution)/shard_map/psum | solution.py:356
  282.3 81.0 %reduce-scatter.8.cloned.1.call-start = ((), (), s32[]{:S(2)}) async-start(), calls=%async_computation.9 | async-start | bytes 2359296 | tf_op jit(solution)/shard_map/reduce_scatter | solution.py:285
  288.7 135.0 %reduce-scatter.16.cloned.1.call-start = ((), (), s32[]{:S(2)}) async-start(), calls=%async_computation.15 | async-start | bytes 835584
  290.8 211.6 %reduce-scatter.14.cloned.1.call-start = ((), (), s32[]{:S(2)}) async-start(), calls=%async_computation.14 | async-start | bytes 5013504 | tf_op jit(solution)/shard_map/reduce_scatter | solution.py:403
  295.8 321.5 %reduce-scatter.10.cloned.1.call-start = ((), (), s32[]{:S(2)}) async-start(), calls=%async_computation.12 | async-start | bytes 10027008 | tf_op jit(solution)/shard_map/reduce_scatter | solution.py:399
  306.5 30.5 %copy-start.81 = (f32[256]{0:T(256)S(1)}, f32[256]{0:T(256)}, u32[]{:S(2)}) copy-start(f32[256]{0:T(256)} %get-tuple-element.106) | copy-start | bytes 3076
  340.0 27.6 %all-to-all-start.3 = ((bf16[16,32,768]{2,1,0:T(8,128)(2,1)}), bf16[16,32,768]{2,1,0:T(8,128)(2,1)S(1)}, u32[]{:S(2)}, u32[]{:S(2)}) async-start(bf16[16,32,768]{2,1,0:T(8,128)(2,1)} %bitcast.60), calls=%async_computation.4 | async-start | bytes 1572864 | tf_op jit(solution)/shard_map/all_to_all | solution.py:368
  345.6 335.2 %reduce-scatter.12.cloned.1.call-start = ((), (), s32[]{:S(2)}) async-start(), calls=%async_computation.13 | async-start | bytes 1671168 | tf_op jit(solution)/shard_map/reduce_scatter | solution.py:400
  367.5 57.7 %copy-start.82 = (f32[256]{0:T(256)S(1)}, f32[256]{0:T(256)}, u32[]{:S(2)}) copy-start(f32[256]{0:T(256)} %get-tuple-element.56) | copy-start | bytes 3076
  367.5 57.6 %copy-start.83 = (f32[256]{0:T(256)S(1)}, f32[256]{0:T(256)}, u32[]{:S(2)}) copy-start(f32[256]{0:T(256)} %get-tuple-element.90) | copy-start | bytes 3076
  367.5 57.6 %copy-start.84 = (f32[256]{0:T(256)S(1)}, f32[256]{0:T(256)}, u32[]{:S(2)}) copy-start(f32[256]{0:T(256)} %get-tuple-element.92) | copy-start | bytes 3076
  367.5 57.6 %copy-start.91 = (f32[256]{0:T(256)S(1)}, f32[256]{0:T(256)}, u32[]{:S(2)}) copy-start(f32[256]{0:T(256)} %get-tuple-element.37) | copy-start | bytes 3076
  367.5 57.7 %copy-start.52 = (f32[1536]{0:T(1024)S(1)}, f32[1536]{0:T(1024)}, u32[]{:S(2)}) copy-start(f32[1536]{0:T(1024)} %get-tuple-element.32) | copy-start | bytes 18436
  367.5 57.7 %copy-start.78 = (f32[1536]{0:T(1024)S(1)}, f32[1536]{0:T(1024)}, u32[]{:S(2)}) copy-start(f32[1536]{0:T(1024)} %get-tuple-element.30) | copy-start | bytes 18436
  367.5 57.7 %copy-start.90 = (f32[256]{0:T(256)S(1)}, f32[256]{0:T(256)}, u32[]{:S(2)}) copy-start(f32[256]{0:T(256)} %get-tuple-element.36) | copy-start | bytes 3076
  367.6 57.6 %copy-start.93 = (f32[24]{0:T(128)S(1)}, f32[24]{0:T(128)}, u32[]{:S(2)}) copy-start(f32[24]{0:T(128)} %get-tuple-element.53) | copy-start | bytes 292
  367.6 119.4 %all-to-all-start.1 = ((bf16[16,32,768]{2,1,0:T(8,128)(2,1)}), bf16[16,32,768]{2,1,0:T(8,128)(2,1)S(1)}, u32[]{:S(2)}, u32[]{:S(2)}) async-start(bf16[16,32,768]{2,1,0:T(8,128)(2,1)} %bitcast.27), calls=%async_computation.2 | async-start | bytes 1572864 | tf_op jit(solution)/shard_map/all_to_all | solution.py:290
  (87 other events, 617.7 us)
Sparse Core Ops, SparseCore 0:
  252.8 24.2 all-reduce.18
  282.4 52.4 all-reduce.20
  337.2 26.0 reduce-scatter.7
  367.2 56.4 reduce-scatter.15
  427.4 74.9 reduce-scatter.13
  506.9 110.4 reduce-scatter.9
  621.6 59.2 reduce-scatter.11

commit v2 on v1

--- a/solution.py
+++ b/solution.py
@@ -1,6 +1,10 @@
+import functools
+
 import jax
 import jax.numpy as jnp
 from jax import lax
+from jax.experimental import pallas as pl
+from jax.experimental.pallas import tpu as pltpu
 from jax.sharding import PartitionSpec as P
 
 STRETCH = 256
@@ -197,7 +201,759 @@
     return (x_state_grad, written_grad, readout_grad, step_grad, rate_total)
 
 
-def on_device(
+MESH = pl.DeviceIdType.MESH
+BF = jnp.bfloat16
+F32 = jnp.float32
+NEG = -1e30
+
+
+def dot_nn(a, b):
+    return lax.dot_general(a, b, (((1,), (0,)), ((), ())), preferred_element_type=F32)
+
+
+def dot_nt(a, b):
+    return lax.dot_general(a, b, (((1,), (1,)), ((), ())), preferred_element_type=F32)
+
+
+def dot_tn(a, b):
+    return lax.dot_general(a, b, (((0,), (0,)), ((), ())), preferred_element_type=F32)
+
+
+def iota(shape, axis):
+    return lax.broadcasted_iota(jnp.int32, shape, axis)
+
+
+def one_hot(cond):
+    return jnp.where(cond, 1.0, 0.0).astype(BF)
+
+
+def split3(v):
+    high = v.astype(BF)
+    rest = v - high.astype(F32)
+    mid = rest.astype(BF)
+    return high, mid, (rest - mid.astype(F32)).astype(BF)
+
+
+def sigmoid(v):
+    return 1.0 / (1.0 + jnp.exp(-v))
+
+
+def rows_down(v, k):
+    return jnp.where(iota(v.shape, 0) >= k, pltpu.roll(v, k, 0), 0.0)
+
+
+def rows_up(v, k):
+    n = v.shape[0]
+    return jnp.where(iota(v.shape, 0) < n - k, pltpu.roll(v, n - k, 0), 0.0)
+
+
+def pick(v, lane, index):
+    return jnp.sum(jnp.where(lane == index, v, 0.0), axis=1, keepdims=True)
+
+
+class Sizes:
+    def __init__(self, dp, rows, half, inner, heads, state, capacity):
+        self.dp, self.rows, self.half, self.inner = dp, rows, half, inner
+        self.heads, self.state, self.cap = heads, state, capacity
+        self.width = 2 * half
+        self.nz = dp // 4
+        self.share = self.width // dp
+        self.quarter = self.nz * self.share
+        self.slots = dp * capacity
+        self.tiles = inner // 128
+        self.extra = 2 * state + 128
+        self.cols = 3 * inner + self.extra
+        n = inner // 2
+        self.chunks = [(i * n, n) for i in range(6)] + [(6 * n, self.extra)]
+        self.levels = self.nz.bit_length() - 1
+
+
+def send_table(targets, g, sz):
+    strict = one_hot(iota((sz.rows, sz.rows), 0) < iota((sz.rows, sz.rows), 1))
+    group = lax.shift_right_logical(targets[pl.ds(g, 1), :], 8)
+    hot = jnp.where(iota((sz.dp, sz.rows), 0) == group, 1.0, 0.0)
+    before = dot_nn(hot.astype(BF), strict)
+    rank = jnp.sum(hot * before, axis=0, keepdims=True)
+    spot = group.astype(F32) * sz.cap + rank
+    return one_hot(iota((sz.slots, sz.rows), 0).astype(F32) == spot)
+
+
+def owner_table(targets, g, sz):
+    strict = one_hot(iota((sz.rows, sz.rows), 0) < iota((sz.rows, sz.rows), 1))
+    every = targets[...]
+    mine = jnp.where(lax.shift_right_logical(every, 8) == g, 1.0, 0.0)
+    rank = dot_nn(mine.astype(BF), strict)
+    slot = mine * ((every & 255) + 1).astype(F32)
+    lane = iota((sz.dp, 128), 1)
+    found = jnp.zeros((sz.dp, 128), F32)
+    for a in range(sz.cap):
+        one = jnp.sum(jnp.where(rank == float(a), slot, 0.0), axis=1, keepdims=True)
+        found = jnp.where(lane == a, one, found)
+    place = iota((128, sz.slots), 1)
+    spread = one_hot((place % sz.cap) == iota((128, sz.slots), 0))
+    wide = dot_nn(found.astype(BF), spread)
+    keep = (iota((sz.dp, sz.slots), 1) // sz.cap) == iota((sz.dp, sz.slots), 0)
+    row = jnp.sum(jnp.where(keep, wide, 0.0), axis=0, keepdims=True) - 1.0
+    return one_hot(iota((sz.rows, sz.slots), 0).astype(F32) == row)
+
+
+def block_kernel(sz, *refs):
+    (dest, back, length, rows_hbm, ct_hbm, win_hbm, wout_hbm, wst_hbm, wstep_hbm, par,
+     out_rows, out_grads, inner_out, proj_out, extra_out, small_out, gain_out,
+     win, wout, wst, wstep,
+     pk_in, pk_ct, rc_in, rc_ct, ry_in, ry_ct, gn_o, gn_g,
+     p_in, p_bk, q_in, q_bk,
+     hid, cts, normed, lowct, perm, xA, xE, tA, tE,
+     gr, xr, xa, xs, mx, ng,
+     yb, pb, r0, rl,
+     inter, interT, igrad, ptile,
+     sraw, sslope, wr, dtv, lac, lar, sgr, rgr, stepsig, acc1, acc2, scale,
+     stat_s, stat_r, half_s, half_r, st_s, st_r,
+     sms, smr, gall, gsum,
+     a2a_s, a2a_r, fw_s, fw_r, quad_s, quad_r, xq_s, xq_r, z_s, z_r, y_s, y_r, gg_s, gg_r, sm_s, sm_r, w_s, o_s) = refs
+    dp, R, H, C = sz.dp, sz.rows, sz.half, sz.inner
+    W, NT_ = sz.width, sz.tiles
+    g = lax.axis_index("dp")
+    t = lax.axis_index("tensor")
+    o = 1 - t
+    c, x, z = g % 2, (g // 2) % 2, g // 4
+    q = g % 4
+    sib, xp = g + 1 - 2 * c, g + 2 - 4 * x
+    diag = sib + 2 - 4 * x
+
+    def rcopy(src, dst, ss, rs, peer, side=None):
+        return pltpu.make_async_remote_copy(
+            src_ref=src, dst_ref=dst, send_sem=ss, recv_sem=rs,
+            device_id=(peer, t if side is None else side), device_id_type=MESH)
+
+    sent = []
+
+    def go(copy):
+        copy.start()
+        sent.append(copy)
+        return copy
+
+    loads = [pltpu.make_async_copy(a, b, w_s.at[i]) for i, (a, b) in enumerate(
+        [(wst_hbm, wst), (wstep_hbm, wstep), (win_hbm, win), (wout_hbm, wout),
+         (rows_hbm, cts.at[0]), (ct_hbm, cts.at[1])])]
+    loads[4].start()
+    loads[5].start()
+
+    barrier = pltpu.get_barrier_semaphore()
+    for off in range(1, dp):
+        pl.semaphore_signal(barrier, inc=1, device_id=((g + off) % dp, t), device_id_type=MESH)
+    pl.semaphore_signal(barrier, inc=1, device_id=(g, o), device_id_type=MESH)
+
+    far = sorted(range(1, dp), key=lambda k: (abs(k - dp // 2), k))
+
+    def exchange(i, source, target):
+        copies = []
+        for off in far:
+            peer = (g + off) % dp
+            copies.append(rcopy(source.at[peer], target.at[g], a2a_s.at[i, peer], a2a_r.at[i, g], peer))
+            copies[-1].start()
+        target[pl.ds(g, 1)] = source[pl.ds(g, 1)]
+        return copies
+
+    def settle(copies):
+        for copy in copies:
+            copy.wait_send()
+
+    def arrived(i, target, src):
+        rcopy(target.at[src], target.at[src], a2a_s.at[i, src], a2a_r.at[i, src], src).wait_recv()
+
+    def pack(table, source, target):
+        for k in range(2):
+            n = sz.slots // 2
+            part = dot_nn(table[k * n:(k + 1) * n, :], source[...]).astype(BF)
+            target[k * (dp // 2):(k + 1) * (dp // 2)] = part.reshape(dp // 2, sz.cap, H)
+
+    p_in[...] = send_table(dest, g, sz)
+    loads[4].wait()
+    pack(p_in, cts.at[0], pk_in)
+    pl.semaphore_wait(barrier, dp)
+    rows_away = exchange(0, pk_in, rc_in)
+    for load in loads[:4]:
+        load.start()
+    p_bk[...] = send_table(back, g, sz)
+    loads[5].wait()
+    pack(p_bk, cts.at[1], pk_ct)
+    grads_away = exchange(1, pk_ct, rc_ct)
+    q_in[...] = owner_table(dest, g, sz)
+    q_bk[...] = owner_table(back, g, sz)
+
+    near = [k for k in reversed(far)]
+
+    def forward(i, arr, dst, src):
+        arrived(i, arr, src)
+        return rcopy(arr.at[src], dst.at[src], fw_s.at[i, src], fw_r.at[i, src], g, o)
+
+    go(rcopy(rc_in.at[g], ry_in.at[g], fw_s.at[0, g], fw_r.at[0, g], g, o))
+    go(rcopy(rc_ct.at[g], ry_ct.at[g], fw_s.at[1, g], fw_r.at[1, g], g, o))
+    for off in near:
+        go(forward(0, rc_in, ry_in, (g + off) % dp))
+    hid[pl.ds(t, 1)] = dot_nn(q_in[...], rc_in[...].reshape(sz.slots, H)).astype(BF)[None]
+    for d in range(dp):
+        rcopy(ry_in.at[d], ry_in.at[d], fw_s.at[0, d], fw_r.at[0, d], g, o).wait_recv()
+    hid[pl.ds(o, 1)] = dot_nn(q_in[...], ry_in[...].reshape(sz.slots, H)).astype(BF)[None]
+
+    total = jnp.zeros((R, 128), F32)
+    for k in range(W // 128):
+        v = hid[k // (H // 128), :, (k % (H // 128)) * 128:(k % (H // 128)) * 128 + 128].astype(F32)
+        total = total + v * v
+    norm_scale = lax.rsqrt(jnp.sum(total, axis=1, keepdims=True) / W + EPSILON)
+    scale[...] = jnp.broadcast_to(norm_scale, (R, 128))
+    for k in range(W // 128):
+        v = hid[k // (H // 128), :, (k % (H // 128)) * 128:(k % (H // 128)) * 128 + 128].astype(F32)
+        normed[:, k * 128:(k + 1) * 128] = (v * scale[...] * par[6:7, k * 128:(k + 1) * 128]).astype(BF)
+
+    def quarters(source):
+        for qq in range(4):
+            perm[qq] = jnp.concatenate(
+                [source[:, sz.share * (4 * zz + qq):sz.share * (4 * zz + qq + 1)] for zz in range(sz.nz)], axis=1)
+
+    def send_quarter(i, dst):
+        copies = [
+            rcopy(perm.at[peer % 4], dst.at[rel], xq_s.at[i, rel - 1], xq_r.at[i, rel - 1], peer)
+            for rel, peer in ((2, xp), (3, diag), (1, sib))]
+        for copy in copies:
+            copy.start()
+        dst[0:1] = perm[pl.ds(q, 1)]
+        return copies
+
+    def turn_quarter(i, dst, turned):
+        for rel, peer in ((1, sib), (2, xp), (3, diag)):
+            rcopy(dst.at[rel], dst.at[rel], xq_s.at[i, rel - 1], xq_r.at[i, rel - 1], peer).wait_recv()
+        for rel in range(4):
+            turned[:, rel * R:(rel + 1) * R] = jnp.transpose(dst[rel].astype(F32)).astype(BF)
+
+    quarters(normed)
+    quarter_away = send_quarter(0, xA)
+
+    loads[0].wait()
+    loads[1].wait()
+    row = iota((R, 128), 0)
+    lane = iota((R, 128), 1)
+    live = jnp.where(row < length[0, 0], 1.0, 0.0)
+    sraw[...] = dot_nn(normed[...], wst[...])
+    step_in = dot_nn(normed[...], wstep[...]) + par[9:10, :128]
+    S = sz.state
+    for k in range(2):
+        cut = slice(k * S, (k + 1) * S)
+        raw = sraw[:, cut]
+        conv = par[8:9, 4 * 2 * S + k * S:4 * 2 * S + (k + 1) * S] + par[8:9, cut] * raw
+        for tap in range(1, 4):
+            conv = conv + par[8:9, tap * 2 * S + k * S:tap * 2 * S + (k + 1) * S] * rows_down(raw, tap)
+        sg = sigmoid(conv)
+        sslope[:, cut] = sg * (1.0 + conv * (1.0 - sg))
+        wr[:, cut] = (conv * sg).astype(BF)
+    written, readout = wr[:, :S], wr[:, S:]
+    inter[...] = dot_nt(readout, written)
+    interT[...] = dot_nt(written, readout)
+    stepsig[...] = sigmoid(step_in) * live
+    heads_live = jnp.where(lane < sz.heads, live, 0.0)
+    step = (jnp.maximum(step_in, 0.0) + jnp.log1p(jnp.exp(-jnp.abs(step_in)))) * heads_live
+    rate = -jnp.exp(par[10:11, :128])
+    dtv[...] = step
+    lower = one_hot(iota((R, R), 0) >= iota((R, R), 1))
+    log_decay = sum(dot_nn(lower, part) for part in split3(step * rate))
+    lac[...] = log_decay
+    lar[...] = jnp.transpose(log_decay)
+
+    loads[2].wait()
+
+    def project(dst, base):
+        def body(n, carry):
+            at = pl.multiple_of(n * 256, 256)
+            dst[:, pl.ds(at, 256)] = dot_nn(normed[...], win[:, pl.ds(pl.multiple_of(base + n * 256, 256), 256)])
+            return carry
+        lax.fori_loop(0, C // 256, body, 0)
+
+    project(xr, C)
+    project(gr, 0)
+
+    def lanes(p):
+        return pl.ds(pl.multiple_of(p * 128, 128), 128)
+
+    B = 64
+
+    def step_columns(p, lane):
+        first = lane < 64
+        return jnp.where(first, pick(dtv[...], lane, 2 * p), pick(dtv[...], lane, 2 * p + 1))
+
+    def scan(p, carry):
+        at = lanes(p)
+        row = iota((R, 128), 0)
+        lane = iota((R, 128), 1)
+        raw = xr[:, at]
+        conv = par[4:5, at] + par[0:1, at] * raw
+        for tap in range(1, 4):
+            conv = conv + par[tap:tap + 1, at] * rows_down(raw, tap)
+        sg = sigmoid(conv)
+        act = conv * sg
+        xa[:, at] = act
+        xs[:, at] = (sg * (1.0 + conv * (1.0 - sg))).astype(BF)
+        driven = act * step_columns(p, lane)
+        parts = [jnp.where(lane < 64, driven, 0.0).astype(BF), jnp.where(lane >= 64, driven, 0.0).astype(BF)]
+        cols = [pick(lac[...], lane, 2 * p + k) for k in range(2)]
+        for b in range(R // B):
+            reach = 128 * ((b * B) // 128 + 1)
+            cut = slice(b * B, (b + 1) * B)
+            causal = iota((B, reach), 0) + b * B >= iota((B, reach), 1)
+            mixed = par[7:8, at] * act[cut]
+            for k in range(2):
+                spread = cols[k][cut] - lar[pl.ds(2 * p + k, 1), :][:, :reach]
+                fading = jnp.exp(jnp.where(causal, spread, NEG))
+                mixing = (inter[cut, :reach] * fading).astype(BF)
+                mixed = mixed + dot_nn(mixing, parts[k][:reach])
+            mx[cut, at] = mixed
+        return carry
+
+    def scan_and_forward(p, carry):
+        scan(p, carry)
+        src = (g + 1 + p) % dp
+        forward(1, rc_ct, ry_ct, src).start()
+        return carry
+
+    lax.fori_loop(0, NT_, scan_and_forward, 0)
+    for k in range(NT_, dp - 1):
+        go(forward(1, rc_ct, ry_ct, (g + 1 + k) % dp))
+    for k in range(min(NT_, dp - 1)):
+        sent.append(rcopy(rc_ct.at[(g + 1 + k) % dp], ry_ct.at[(g + 1 + k) % dp], fw_s.at[1, (g + 1 + k) % dp],
+                          fw_r.at[1, (g + 1 + k) % dp], g, o))
+
+    cts[pl.ds(t, 1)] = dot_nn(q_bk[...], rc_ct[...].reshape(sz.slots, H)).astype(BF)[None]
+    for d in range(dp):
+        rcopy(ry_ct.at[d], ry_ct.at[d], fw_s.at[1, d], fw_r.at[1, d], g, o).wait_recv()
+    cts[pl.ds(o, 1)] = dot_nn(q_bk[...], ry_ct[...].reshape(sz.slots, H)).astype(BF)[None]
+    for k in range(W // 128):
+        v = cts[k // (H // 128), :, (k % (H // 128)) * 128:(k % (H // 128)) * 128 + 128].astype(F32)
+        lowct[:, k * 128:(k + 1) * 128] = (v * live).astype(BF)
+    settle(quarter_away)
+    quarters(lowct)
+    sent.extend(send_quarter(1, xE))
+    loads[3].wait()
+
+    def back_project(n, carry):
+        at = pl.ds(pl.multiple_of(n * 256, 256), 256)
+        ng[:, at] = dot_nt(lowct[...], wout[at, :])
+        return carry
+    lax.fori_loop(0, C // 256, back_project, 0)
+
+    acc1[...] = jnp.zeros_like(acc1)
+    acc2[...] = jnp.zeros_like(acc2)
+
+    def stats(p, carry):
+        at = lanes(p)
+        raw = gr[:, at]
+        gated = mx[:, at] * raw * sigmoid(raw)
+        acc1[...] += gated * gated
+        acc2[...] += gated * (par[5:6, at] * ng[:, at])
+        return carry
+    lax.fori_loop(0, NT_, stats, 0)
+    squares = jnp.sum(acc1[...], axis=1, keepdims=True)
+    cross = jnp.sum(acc2[...], axis=1, keepdims=True)
+    both = jnp.where(lane == 0, squares, jnp.where(lane == 1, cross, 0.0))
+    stat_s[0] = jnp.transpose(both)[:8]
+    go(rcopy(stat_s.at[0], stat_r.at[0], y_s.at[0], y_r.at[0], g, o)).wait_recv()
+    both = jnp.transpose(jnp.concatenate([stat_s[0] + stat_r[0], jnp.zeros((120, R), F32)], axis=0))
+    whole = float(2 * C)
+    gate_scale = lax.rsqrt(pick(both, lane, 0) / whole + EPSILON)
+    pull = gate_scale * gate_scale * gate_scale * (pick(both, lane, 1) / whole)
+    acc1[...] = jnp.broadcast_to(gate_scale, (R, 128))
+    acc2[...] = jnp.broadcast_to(pull, (R, 128))
+
+    def gate_back(p, carry):
+        at = lanes(p)
+        raw, mixed, grad = gr[:, at], mx[:, at], ng[:, at]
+        sg = sigmoid(raw)
+        act = raw * sg
+        gated = mixed * act
+        scaled = gated * acc1[...]
+        gain = par[5:6, at]
+        yb[0, :, at] = (scaled * gain).astype(BF)
+        gated_grad = acc1[...] * (gain * grad) - gated * acc2[...]
+        sms[0, 5:6, at] = jnp.sum(grad * scaled, axis=0, keepdims=True)
+        mixed_grad = gated_grad * act
+        ng[:, at] = mixed_grad
+        sms[0, 6:7, at] = jnp.sum(mixed_grad * xa[:, at], axis=0, keepdims=True)
+        yb[0, :, pl.ds(pl.multiple_of(C + p * 128, 128), 128)] = (
+            gated_grad * mixed * (sg * (1.0 + raw * (1.0 - sg)))).astype(BF)
+        return carry
+    lax.fori_loop(0, NT_, gate_back, 0)
+
+    def cols_of(i):
+        return pl.ds(sz.chunks[i][0], sz.chunks[i][1])
+
+    def quad_send(i):
+        at = cols_of(i)
+        go(rcopy(yb.at[0, :, at], yb.at[2, :, at], quad_s.at[i, 1], quad_r.at[i, 1], xp))
+        go(rcopy(yb.at[0, :, at], yb.at[1, :, at], quad_s.at[i, 0], quad_r.at[i, 0], sib))
+
+    def quad_pass(i):
+        at = cols_of(i)
+        rcopy(yb.at[2, :, at], yb.at[2, :, at], quad_s.at[i, 1], quad_r.at[i, 1], xp).wait_recv()
+        go(rcopy(yb.at[2, :, at], yb.at[3, :, at], quad_s.at[i, 2], quad_r.at[i, 2], sib))
+
+    def z_peer(level):
+        bit = (z // 2 ** level) % 2
+        return bit, g + (1 - 2 * bit) * 4 * 2 ** level
+
+    bases = []
+    at0 = 0
+    for level in range(sz.levels):
+        bases.append(at0)
+        at0 += sz.nz // 2 ** (level + 1)
+    landing = [r0, rl]
+
+    def z_send(i, level):
+        bit, peer = z_peer(level)
+        at = cols_of(i)
+        for k in range(sz.nz // 2 ** (level + 1)):
+            low = z % 2 ** level
+            block = (2 * k + 1 - bit) * 2 ** level + low
+            go(rcopy(pb.at[block, :, at], landing[level].at[k, :, at], z_s.at[i, bases[level] + k],
+                     z_r.at[i, bases[level] + k], peer))
+
+    def z_add(i, level):
+        bit, peer = z_peer(level)
+        at = cols_of(i)
+        start, size = sz.chunks[i]
+        for k in range(sz.nz // 2 ** (level + 1)):
+            low = z % 2 ** level
+            block = (2 * k + bit) * 2 ** level + low
+            sem = bases[level] + k
+            rcopy(landing[level].at[k, :, at], landing[level].at[k, :, at], z_s.at[i, sem], z_r.at[i, sem], peer).wait_recv()
+            for n in range(0, size, 128):
+                cut = slice(start + n, start + n + 128)
+                value = pb[pl.ds(block, 1), :, cut].astype(F32)[0] + landing[level][k, :, cut].astype(F32)
+                if level + 1 < sz.levels:
+                    pb[pl.ds(block, 1), :, cut] = value.astype(BF)[None]
+                elif start + n < C:
+                    proj_out[:, cut] = value
+                elif start + n < 3 * C:
+                    inner_out[:, start + n - C:start + n - C + 128] = value
+                else:
+                    extra_out[:, start + n - 3 * C:start + n - 3 * C + 128] = value
+
+    def partial_sum(i, turned):
+        at = cols_of(i)
+        start, size = sz.chunks[i]
+        rcopy(yb.at[1, :, at], yb.at[1, :, at], quad_s.at[i, 0], quad_r.at[i, 0], sib).wait_recv()
+        rcopy(yb.at[3, :, at], yb.at[3, :, at], quad_s.at[i, 2], quad_r.at[i, 2], sib).wait_recv()
+        n = 384 if size % 256 else 256
+
+        def body(k, carry):
+            at = pl.ds(pl.multiple_of(start + k * n, 128), n)
+            part = dot_nn(turned[...], yb[:, :, at].reshape(4 * R, n))
+            pb[:, :, at] = part.astype(BF).reshape(sz.nz, sz.share, n)
+            return carry
+        lax.fori_loop(0, size // n, body, 0)
+        z_send(i, 0)
+
+    for i in range(4):
+        quad_send(i)
+    turn_quarter(0, xA, tA)
+
+    def out_half(side, dst, cast):
+        def body(n, carry):
+            at = pl.ds(pl.multiple_of(side * H + n * 256, 256), 256)
+            dst[:, pl.ds(pl.multiple_of(n * 256, 256), 256)] = dot_nn(yb[0, :, :C], wout[:, at]).astype(cast)
+            return carry
+        lax.fori_loop(0, H // 256, body, 0)
+    out_half(o, half_s.at[0], BF)
+    go(rcopy(half_s.at[0], half_r.at[0], y_s.at[1], y_r.at[1], g, o))
+    out_half(t, gr, F32)
+    turn_quarter(1, xE, tE)
+
+    igrad[...] = jnp.zeros_like(igrad)
+    sgr[...] = jnp.zeros_like(sgr)
+    rgr[...] = jnp.zeros_like(rgr)
+    ptile[...] = jnp.zeros_like(ptile)
+
+    def scan_back(p, carry):
+        at = lanes(p)
+        lane = iota((R, 128), 1)
+        grad = ng[:, at]
+        act = xa[:, at]
+        stepw = step_columns(p, lane)
+        driven = (act * stepw).astype(BF)
+        parts = [jnp.where(lane < 64, grad, 0.0).astype(BF), jnp.where(lane >= 64, grad, 0.0).astype(BF)]
+        cols = [pick(lac[...], lane, 2 * p + k) for k in range(2)]
+        pieces = []
+        for b in range(R // B):
+            skip = 128 * ((b * B) // 128)
+            cut = slice(b * B, (b + 1) * B)
+            causal = iota((B, R - skip), 1) + skip >= iota((B, R - skip), 0) + b * B
+            turned = interT[cut, skip:]
+            piece = jnp.zeros((B, 128), F32)
+            total = igrad[cut, skip:]
+            for k in range(2):
+                spread = lar[pl.ds(2 * p + k, 1), :][:, skip:] - cols[k][cut]
+                fading = jnp.exp(jnp.where(causal, spread, NEG))
+                faded = dot_nt(driven[cut], parts[k][skip:]) * fading
+                total = total + faded
+                piece = piece + dot_nn((turned * fading).astype(BF), parts[k][skip:])
+                ptile[k, cut, skip:] = (faded * turned).astype(BF)
+            igrad[cut, skip:] = total
+            pieces.append(piece)
+        strict = one_hot(iota((R, R), 0) > iota((R, R), 1))
+        for k in range(2):
+            found = []
+            for b in range(R // B):
+                skip = 128 * ((b * B) // 128)
+                cut = slice(b * B, (b + 1) * B)
+                causal = iota((B, R - skip), 1) + skip >= iota((B, R - skip), 0) + b * B
+                sums = dot_nn(strict[cut], ptile[k, :, skip:])
+                found.append(jnp.sum(jnp.where(causal, sums, 0.0), axis=1, keepdims=True))
+            rgr[...] = jnp.where(lane == 2 * p + k, jnp.concatenate(found, axis=0), rgr[...])
+        driven_grad = jnp.concatenate(pieces, axis=0)
+        pulled = driven_grad * act
+        low = jnp.sum(jnp.where(lane < 64, pulled, 0.0), axis=1, keepdims=True)
+        high = jnp.sum(jnp.where(lane >= 64, pulled, 0.0), axis=1, keepdims=True)
+        sgr[...] = jnp.where(lane == 2 * p, low, jnp.where(lane == 2 * p + 1, high, sgr[...]))
+        conv_grad = (par[7:8, at] * grad + stepw * driven_grad) * xs[:, at].astype(F32)
+        raw = xr[:, at]
+        raw_grad = par[0:1, at] * conv_grad
+        sms[0, 0:1, at] = jnp.sum(conv_grad * raw, axis=0, keepdims=True)
+        sms[0, 4:5, at] = jnp.sum(conv_grad, axis=0, keepdims=True)
+        for tap in range(1, 4):
+            up = rows_up(conv_grad, tap)
+            raw_grad = raw_grad + par[tap:tap + 1, at] * up
+            sms[0, tap:tap + 1, at] = jnp.sum(up * raw, axis=0, keepdims=True)
+        yb[0, :, pl.ds(pl.multiple_of(2 * C + p * 128, 128), 128)] = raw_grad.astype(BF)
+        return carry
+
+    lax.fori_loop(0, NT_ // 2, scan_back, 0)
+    quad_send(4)
+
+    rcopy(half_r.at[0], half_r.at[0], y_s.at[1], y_r.at[1], g, o).wait_recv()
+
+    def answer(table, value, dst):
+        for k in range(2):
+            n = sz.slots // 2
+            part = dot_tn(table[:, k * n:(k + 1) * n], value).astype(BF)
+            dst[k * (dp // 2):(k + 1) * (dp // 2)] = part.reshape(dp // 2, sz.cap, H)
+
+    pieces = []
+    mine = hid[pl.ds(t, 1)][0]
+    for k in range(H // 128):
+        cut = slice(k * 128, (k + 1) * 128)
+        branch = gr[:, cut] + half_r[0, :, cut].astype(F32)
+        pieces.append((mine[:, cut].astype(F32) + live * branch).astype(BF))
+    settle(rows_away)
+    answer(q_bk, jnp.concatenate(pieces, axis=1), pk_in)
+    sent.extend(exchange(2, pk_in, gn_o))
+    quad_pass(0)
+    quad_pass(1)
+
+    lax.fori_loop(NT_ // 2, NT_, scan_back, 0)
+    quad_send(5)
+    quad_pass(2)
+
+    ig = igrad[...].astype(BF)
+    st_s[:, :S] = dot_nn(ig, wr[:, S:]).astype(BF)
+    st_s[:, S:] = dot_tn(ig, wr[:, :S]).astype(BF)
+    go(rcopy(st_s, st_r, y_s.at[2], y_r.at[2], g, o))
+    step_grad = (sgr[...] + rgr[...] * rate) * stepsig[...]
+    yb[0, :, 3 * C + 2 * S:] = step_grad.astype(BF)
+    sms[0, 7:8, 10 * S:10 * S + 128] = jnp.sum(step_grad, axis=0, keepdims=True)
+    sms[0, 7:8, 10 * S + 128:10 * S + 256] = jnp.sum(rgr[...] * dtv[...], axis=0, keepdims=True) * rate
+    partial_sum(0, tE)
+    rcopy(st_r, st_r, y_s.at[2], y_r.at[2], g, o).wait_recv()
+    for k in range(2):
+        cut = slice(k * S, (k + 1) * S)
+        conv_grad = (st_s[:, cut].astype(F32) + st_r[:, cut].astype(F32)) * sslope[:, cut]
+        raw = sraw[:, cut]
+        raw_grad = par[8:9, cut] * conv_grad
+        sms[0, 7:8, cut] = jnp.sum(conv_grad * raw, axis=0, keepdims=True)
+        sms[0, 7:8, 8 * S + k * S:8 * S + (k + 1) * S] = jnp.sum(conv_grad, axis=0, keepdims=True)
+        for tap in range(1, 4):
+            up = rows_up(conv_grad, tap)
+            taps = slice(tap * 2 * S + k * S, tap * 2 * S + (k + 1) * S)
+            raw_grad = raw_grad + par[8:9, taps] * up
+            sms[0, 7:8, taps] = jnp.sum(up * raw, axis=0, keepdims=True)
+        yb[0, :, 3 * C + k * S:3 * C + (k + 1) * S] = raw_grad.astype(BF)
+    quad_send(6)
+
+    acc1[...] = jnp.zeros_like(acc1)
+
+    def normed_grad(side, dst, cast):
+        def body(n, carry):
+            at = pl.ds(pl.multiple_of(side * H + n * 256, 256), 256)
+            value = dot_nt(yb[0, :, C:3 * C], win[at, :])
+            mine_state = pl.ds(pl.multiple_of(t * S, 128), S)
+            value = value + dot_nt(yb[0, :, pl.ds(pl.multiple_of(3 * C + t * S, 128), S)], wst[at, mine_state])
+            value = value + dot_nt(yb[0, :, 3 * C + 2 * S:], wstep[at, :])
+            for k in range(2):
+                cut = slice(k * 128, (k + 1) * 128)
+                here = pl.ds(pl.multiple_of(n * 256 + k * 128, 128), 128)
+                there = pl.ds(pl.multiple_of(side * H + n * 256 + k * 128, 128), 128)
+                acc1[...] += hid[pl.ds(side, 1), :, here][0].astype(F32) * (par[6:7, there] * value[:, cut])
+            dst[:, pl.ds(pl.multiple_of(n * 256, 256), 256)] = value.astype(cast)
+            return carry
+        lax.fori_loop(0, H // 256, body, 0)
+    normed_grad(o, half_s.at[1], BF)
+    go(rcopy(half_s.at[1], half_r.at[1], y_s.at[3], y_r.at[3], g, o))
+    normed_grad(t, gr, F32)
+    inner_sum = jnp.where(lane == 0, jnp.sum(acc1[...], axis=1, keepdims=True), 0.0)
+    stat_s[1] = jnp.transpose(inner_sum)[:8]
+    go(rcopy(stat_s.at[1], stat_r.at[1], y_s.at[4], y_r.at[4], g, o))
+    quad_pass(3)
+    partial_sum(1, tE)
+
+    rcopy(half_r.at[1], half_r.at[1], y_s.at[3], y_r.at[3], g, o).wait_recv()
+    rcopy(stat_r.at[1], stat_r.at[1], y_s.at[4], y_r.at[4], g, o).wait_recv()
+    both = jnp.transpose(jnp.concatenate([stat_s[1] + stat_r[1], jnp.zeros((120, R), F32)], axis=0))
+    pull = pick(both, lane, 0) / W * (scale[...] * scale[...] * scale[...])
+    pieces = []
+    mine = hid[pl.ds(t, 1)][0]
+    mine_ct = cts[pl.ds(t, 1)][0]
+    gall[pl.ds(g, 1)] = jnp.zeros((1, 8, 128), F32)
+    for k in range(H // 128):
+        cut = slice(k * 128, (k + 1) * 128)
+        there = pl.ds(pl.multiple_of(t * H + k * 128, 128), 128)
+        value = gr[:, cut] + half_r[1, :, cut].astype(F32)
+        rows_here = mine[:, cut].astype(F32)
+        gall[pl.ds(g, 1), k:k + 1, :] = jnp.sum(value * rows_here * scale[...], axis=0, keepdims=True)[None]
+        pieces.append((scale[...] * (par[6:7, there] * value) - rows_here * pull
+                       + mine_ct[:, cut].astype(F32)).astype(BF))
+    settle(grads_away)
+    answer(q_in, jnp.concatenate(pieces, axis=1), pk_ct)
+    for off in far:
+        peer = (g + off) % dp
+        go(rcopy(gall.at[g], gall.at[g], gg_s.at[peer], gg_r.at[g], peer))
+    sent.extend(exchange(3, pk_ct, gn_g))
+
+    quad_pass(4)
+    quad_pass(5)
+    quad_pass(6)
+    z_add(0, 0)
+    z_send(0, 1)
+    partial_sum(2, tA)
+    z_add(1, 0)
+    z_send(1, 1)
+    partial_sum(3, tA)
+    z_add(2, 0)
+    z_send(2, 1)
+    partial_sum(4, tA)
+    z_add(3, 0)
+    z_send(3, 1)
+    partial_sum(5, tA)
+    partial_sum(6, tA)
+
+    for level in range(dp.bit_length() - 1):
+        bit = (g // 2 ** level) % 2
+        peer = g + (1 - 2 * bit) * 2 ** level
+        go(rcopy(sms.at[level], smr.at[level], sm_s.at[level], sm_r.at[level], peer)).wait_recv()
+        if level + 1 < dp.bit_length() - 1:
+            sms[level + 1] = sms[level] + smr[level]
+        else:
+            small_out[...] = sms[level] + smr[level]
+    for off in far:
+        src = (g + off) % dp
+        rcopy(gall.at[src], gall.at[src], gg_s.at[src], gg_r.at[src], src).wait_recv()
+    summed = gall[0]
+    for d in range(1, dp):
+        summed = summed + gall[d]
+    gsum[pl.ds(t, 1)] = summed[None]
+    go(rcopy(gsum.at[t], gsum.at[t], y_s.at[5], y_r.at[5], g, o))
+
+    def give(i, value, stage, dst):
+        n = R // sz.cap
+        stage[:n] = value.astype(BF).reshape(n, sz.cap, H)
+        copies = [pltpu.make_async_copy(stage.at[k], dst.at[pl.ds(k * sz.cap, sz.cap)], o_s.at[i, k]) for k in range(n)]
+        for copy in copies:
+            copy.start()
+        return copies
+
+    for i in range(4, 7):
+        z_add(i, 0)
+        z_send(i, 1)
+
+    for off in far:
+        arrived(2, gn_o, (g + off) % dp)
+    stores = give(0, dot_tn(p_bk[...], gn_o[...].reshape(sz.slots, H)), ry_in, out_rows)
+    for i in range(7):
+        z_add(i, 1)
+    for off in far:
+        arrived(3, gn_g, (g + off) % dp)
+    stores += give(1, dot_tn(p_in[...], gn_g[...].reshape(sz.slots, H)), ry_ct, out_grads)
+    rcopy(gsum.at[o], gsum.at[o], y_s.at[5], y_r.at[5], g, o).wait_recv()
+    gain_out[...] = gsum[...]
+    for copy in sent:
+        copy.wait_send()
+    for store in stores:
+        store.wait()
+
+
+def fused(sz, block_in, cotangent, lengths, dest_slot, return_slot, norm_gain, inner_weight, state_weight,
+          step_weight, conv_inner, conv_inner_bias, conv_state, conv_state_bias, step_bias, log_rate,
+          skip_gain, gate_gain, out_weight):
+    dp, R, H, C, S = sz.dp, sz.rows, sz.half, sz.inner, sz.state
+    W = sz.width
+
+    def line(v):
+        return jnp.pad(v.reshape(1, -1), ((0, 0), (0, C - v.size)))
+    params = jnp.concatenate([
+        conv_inner, line(conv_inner_bias), line(gate_gain), line(norm_gain),
+        line(jnp.repeat(skip_gain, C // sz.heads)),
+        line(jnp.concatenate([conv_state.reshape(-1), conv_state_bias])),
+        line(step_bias), line(log_rate), jnp.zeros((5, C), F32)], axis=0)
+    win = inner_weight.reshape(W, 2 * C)
+    wstep = jnp.pad(step_weight, ((0, 0), (0, 128 - sz.heads)))
+    vm = pl.BlockSpec(memory_space=pltpu.VMEM)
+    hb = pl.BlockSpec(memory_space=pl.ANY)
+    sm = pl.BlockSpec(memory_space=pltpu.SMEM)
+    V = pltpu.VMEM
+    packed = V((dp, sz.cap, H), BF)
+    D = pltpu.SemaphoreType.DMA
+    nch = len(sz.chunks)
+    scratch = [
+        V((W, 2 * C), BF), V((C, W), BF), V((W, 2 * S), BF), V((W, 128), BF),
+        *[packed] * 8,
+        V((sz.slots, R), BF), V((sz.slots, R), BF), V((R, sz.slots), BF), V((R, sz.slots), BF),
+        V((2, R, H), BF), V((2, R, H), BF), V((R, W), BF), V((R, W), BF),
+        V((4, R, sz.quarter), BF), V((4, R, sz.quarter), BF), V((4, R, sz.quarter), BF),
+        V((sz.quarter, 4 * R), BF), V((sz.quarter, 4 * R), BF),
+        V((R, C), F32), V((R, C), F32), V((R, C), F32), V((R, C), BF), V((R, C), F32), V((R, C), F32),
+        V((4, R, sz.cols), BF), V((sz.nz, sz.share, sz.cols), BF), V((2, sz.share, sz.cols), BF), V((1, sz.share, sz.cols), BF),
+        V((R, R), F32), V((R, R), F32), V((R, R), F32), V((2, R, R), BF),
+        V((R, 2 * S), F32), V((R, 2 * S), F32), V((R, 2 * S), BF), V((R, 128), F32), V((R, 128), F32), V((128, R), F32),
+        V((R, 128), F32), V((R, 128), F32), V((R, 128), F32), V((R, 128), F32), V((R, 128), F32), V((R, 128), F32),
+        V((2, 8, R), F32), V((2, 8, R), F32), V((2, R, H), BF), V((2, R, H), BF),
+        V((R, 2 * S), BF), V((R, 2 * S), BF),
+        V((4, 8, C), F32), V((4, 8, C), F32), V((dp, 8, 128), F32), V((2, 8, 128), F32),
+        D((4, dp)), D((4, dp)), D((2, dp)), D((2, dp)), D((nch, 3)), D((nch, 3)), D((2, 3)), D((2, 3)),
+        D((nch, sz.nz - 1)), D((nch, sz.nz - 1)), D((6,)), D((6,)), D((dp,)), D((dp,)), D((4,)), D((4,)), D((6,)), D((2, dp)),
+    ]
+    out = jax.ShapeDtypeStruct
+    rows_out, grads_out, inner_g, proj_g, extra_g, small, gain = pl.pallas_call(
+        functools.partial(block_kernel, sz),
+        out_shape=(out((R, H), BF), out((R, H), BF), out((sz.share, 2 * C), F32), out((sz.share, C), F32),
+                   out((sz.share, sz.extra), F32), out((8, C), F32), out((2, 8, 128), F32)),
+        in_specs=[vm, vm, sm, hb, hb, hb, hb, hb, hb, vm],
+        out_specs=(hb, hb) + (vm,) * 5,
+        scratch_shapes=scratch,
+        compiler_params=pltpu.CompilerParams(collective_id=0, has_side_effects=True, vmem_limit_bytes=66000000),
+        name="block",
+    )(dest_slot.reshape(dp, R), return_slot.reshape(dp, R), lengths, block_in, cotangent, win, out_weight,
+      state_weight, wstep, params)
+    own = lax.axis_index("dp")
+    gain_sum = gain[:, :H // 128].reshape(W)
+    heads = sz.heads
+    return (
+        rows_out, grads_out,
+        lax.dynamic_slice_in_dim(gain_sum, own * sz.share, sz.share),
+        inner_g.reshape(sz.share, 2, C),
+        extra_g[:, :2 * S], extra_g[:, 2 * S:2 * S + heads],
+        small[:4], small[4], small[7, :8 * S].reshape(4, 2 * S), small[7, 8 * S:10 * S],
+        small[7, 10 * S:10 * S + heads], small[7, 10 * S + 128:10 * S + 128 + heads],
+        jnp.sum(small[6].reshape(heads, -1), axis=1), small[5], proj_g.T,
+    )
+
+
+def with_collectives(
     block_in,
     cotangent,
     lengths,
@@ -423,6 +1179,20 @@
     )
 
 
+def on_device(*args):
+    groups = lax.axis_size("dp")
+    rows, half = args[0].shape
+    inner, heads, state = args[6].shape[2], args[8].shape[1], args[7].shape[1] // 2
+    capacity = 2 * rows // groups
+    fits = (
+        groups % 4 == 0 and 16 <= 4 * groups <= 64 and capacity % 16 == 0 and (2 * half // groups) % 16 == 0
+        and rows == STRETCH and args[2].shape[1] == 1 and inner == 64 * heads and inner == 2 * half
+    )
+    if fits:
+        return fused(Sizes(groups, rows, half, inner, heads, state, capacity), *args)
+    return with_collectives(*args)
+
+
 def solution(mesh):
     placed = (
         P("dp", "tensor"),

time: 698 us -> 254 us (0.36); the launches traced: 688 us -> 254 us
  waiting for transfers between devices: 280 us -> 0 us
  Pallas kernels: 0 us -> 219 us
  local copies, waits for them, and re-layouts: 126 us -> 32.4 us
  blocking collectives: 93.5 us -> 0 us
  matrix products: 86.2 us -> 0 us
  other arithmetic: 59.9 us -> 0.64 us
  starting transfers between devices: 25.3 us -> 0 us
  between operations: 16.9 us -> 1.56 us
    pallas_call x0 -> x1, Pallas kernels: none -> 219 us  [fused(): pl.pallas_call(functools.partial(block_kernel, sz), out_shape=(out((R, H)...]
    reduce_scatter x4 -> x0, waiting for transfers between devices: 203 us -> none  [the longest x1 113 us: on_device(): lax.psum_scatter(inner_weight_grad.astype(jnp.bfloat16), 'dp', scatter_di...]
    dot_general x21 -> x0, matrix products: 84.8 us -> none  [the longest x1 11.8 us: state_backward(): jnp.einsum('cihp,cjhp->chij', mixed_grad, driven, precision=PRECISE)]
    unnamed x1 -> x0, blocking collectives: 59.3 us -> none
    unnamed x8 -> x0, waiting for transfers between devices: 48.5 us -> none
    scatter x6 -> x0, local copies, waits for them, and re-layouts: 43.7 us -> none  [the longest x2 31 us: arrivals(): filler.at[position.reshape(-1)]]
    psum x2 -> x0, waiting for transfers between devices: 28.5 us -> none  [the longest x1 28.5 us: on_device(): normed_grad = lax.psum(normed_grad, 'tensor')]
    reduce_sum x15 -> x1, other arithmetic: 26.3 us -> 0.63 us  [fused(): jnp.sum(small[6].reshape(heads, -1), axis=1)]
  transfers between devices with their start and end apart: 11 -> 0, of which waited for: 6 -> 0; matrix products, arithmetic and copies ran while one was open for 26% -> 0% of each run, Pallas kernels for 0% -> 0%
where the time goes in v2:
time: 254 us
  Pallas kernels  219 us (86%)
  local copies, waits for them, and re-layouts  32.4 us (13%)
    pallas_call x1, Pallas kernels, fused(): pl.pallas_call(functools.partial(block_kernel, sz), out_shape=(out((R, H)...  219 us
    unnamed x33, local copies, waits for them, and re-layouts  15.2 us

profile of v2, /device:TPU:0, one launch (start us, length us, event | category | flops | bytes accessed | tf_op | source)
XLA Modules:
  0.0 253.7 jit_solution(17757308739157716616)
XLA Ops:
  0.8 9.9 %copy.37 = bf16[192,8,2,1536]{3,1,2,0:T(8,128)(2,1)} copy(bf16[192,8,2,1536]{3,2,1,0:T(2,128)(2,1)} %bitcast.14) | data formatting | bytes 18874368
  10.7 0.2 copy.35
  10.9 0.8 pad.15.refs_8_
  11.8 0.1 reshape_reshape.3
  12.1 1.3 concatenate.7.refs_9_
  13.4 0.6 reshape.66.refs_0_
  14.0 0.6 reshape.67.refs_1_
  15.3 219.1 %block.1 = (bf16[256,768]{1,0:T(8,128)(2,1)}, bf16[256,768]{1,0:T(8,128)(2,1)}, f32[96,3072]{1,0:T(8,128)}, f32[96,1536]{1,0:T(8,128)}, f32[96,384]{1,0:T(8,128)...) custom-call(s32[16,256]{1,0:T(8,128)} %reshape.66.refs_0_, s32[16,256]{1,0:T(8,128)} %reshape.67.refs_1_, ...), custom_call_target="tpu_custom_call" | custom-call | tf_op jit(solution)/shard_map/block/pallas_call | solution.py:931
  234.4 1.6 slice_reduce_fusion
  236.1 0.6 reduce_sum.9
  236.7 0.7 reshape.76
  237.4 0.6 dynamic_slice.3
  238.0 1.2 slice_bitcast_fusion
  239.2 1.4 slice.36
  240.6 0.8 slice_reduce_fusion.3
  241.3 0.6 reshape_squeeze.6
  241.9 1.3 slice.39
  243.2 1.5 slice.34
  244.7 0.8 slice.35
  245.5 0.7 copy.36
  246.2 3.2 %reshape.77 = f32[96,2,1536]{2,1,0:T(2,128)} reshape(f32[96,3072]{1,0:T(8,128)} %get-tuple-element.25) | data formatting | bytes 2359296 | tf_op jit(solution)/shard_map/reshape | solution.py:948
  249.4 1.8 copy.43
  251.2 1.8 copy.44
  252.9 0.8 copy.45
  (38 shorter events, 0.3 us)
Async XLA Ops:
  0.7 10.0 %copy-start.1 = (bf16[1536,24]{0,1:T(8,128)(2,1)S(1)}, bf16[1536,24]{0,1:T(8,128)(2,1)}, u32[]{:S(2)}) copy-start(bf16[1536,24]{0,1:T(8,128)(2,1)} %param.26) | copy-start | bytes 221188
  0.7 11.1 %copy-start.8 = (f32[4,256]{1,0:T(4,128)S(1)}, f32[4,256]{1,0:T(4,128)}, u32[]{:S(2)}) copy-start(f32[4,256]{1,0:T(4,128)} %param.29) | copy-start | bytes 12292
  0.7 11.0 %copy-start.9 = (f32[256]{0:T(256)S(1)}, f32[256]{0:T(256)}, u32[]{:S(2)}) copy-start(f32[256]{0:T(256)} %param.30) | copy-start | bytes 3076
  0.7 11.1 %copy-start.12 = (f32[24]{0:T(128)S(1)}, f32[24]{0:T(128)}, u32[]{:S(2)}) copy-start(f32[24]{0:T(128)} %param.33) | copy-start | bytes 292
  0.7 11.2 %copy-start.10 = (f32[24]{0:T(128)S(1)}, f32[24]{0:T(128)}, u32[]{:S(2)}) copy-start(f32[24]{0:T(128)} %param.31) | copy-start | bytes 292
  0.7 11.2 %copy-start.11 = (f32[24]{0:T(128)S(1)}, f32[24]{0:T(128)}, u32[]{:S(2)}) copy-start(f32[24]{0:T(128)} %param.32) | copy-start | bytes 292
  0.7 11.3 %copy-start.5 = (f32[1536]{0:T(1024)S(1)}, f32[1536]{0:T(1024)}, u32[]{:S(2)}) copy-start(f32[1536]{0:T(1024)} %param.28) | copy-start | bytes 18436
  0.7 11.3 %copy-start.6 = (f32[1536]{0:T(1024)S(1)}, f32[1536]{0:T(1024)}, u32[]{:S(2)}) copy-start(f32[1536]{0:T(1024)} %param.34) | copy-start | bytes 18436
  0.7 11.3 %copy-start.7 = (f32[1536]{0:T(1024)S(1)}, f32[1536]{0:T(1024)}, u32[]{:S(2)}) copy-start(f32[1536]{0:T(1024)} %param.23) | copy-start | bytes 18436
  0.7 11.3 %copy-start.2 = (f32[4,1536]{1,0:T(4,128)S(1)}, f32[4,1536]{1,0:T(4,128)}, u32[]{:S(2)}) copy-start(f32[4,1536]{1,0:T(4,128)} %param.27) | copy-start | bytes 73732
  0.8 12.6 %copy-start.3 = (s32[4096]{0:T(1024)S(1)}, s32[4096]{0:T(1024)}, u32[]{:S(2)}) copy-start(s32[4096]{0:T(1024)} %param.21) | copy-start | bytes 49156
  0.8 13.2 %copy-start.4 = (s32[4096]{0:T(1024)S(1)}, s32[4096]{0:T(1024)}, u32[]{:S(2)}) copy-start(s32[4096]{0:T(1024)} %param.22) | copy-start | bytes 49156
  234.4 18.5 %copy-start = (f32[96,1536]{1,0:T(8,128)S(1)}, f32[96,1536]{1,0:T(8,128)}, u32[]{:S(2)}) copy-start(f32[96,1536]{1,0:T(8,128)} %get-tuple-element.28) | copy-start | bytes 1769476

commit v3 on v1

--- a/solution.py
+++ b/solution.py
@@ -1,6 +1,10 @@
+import functools
+
 import jax
 import jax.numpy as jnp
 from jax import lax
+from jax.experimental import pallas as pl
+from jax.experimental.pallas import tpu as pltpu
 from jax.sharding import PartitionSpec as P
 
 STRETCH = 256
@@ -197,7 +201,839 @@
     return (x_state_grad, written_grad, readout_grad, step_grad, rate_total)
 
 
-def on_device(
+MESH = pl.DeviceIdType.MESH
+BF = jnp.bfloat16
+F32 = jnp.float32
+NEG = -1e30
+
+
+def dot_nn(a, b):
+    return lax.dot_general(a, b, (((1,), (0,)), ((), ())), preferred_element_type=F32)
+
+
+def dot_nt(a, b):
+    return lax.dot_general(a, b, (((1,), (1,)), ((), ())), preferred_element_type=F32)
+
+
+def dot_tn(a, b):
+    return lax.dot_general(a, b, (((0,), (0,)), ((), ())), preferred_element_type=F32)
+
+
+def iota(shape, axis):
+    return lax.broadcasted_iota(jnp.int32, shape, axis)
+
+
+def one_hot(cond):
+    return jnp.where(cond, 1.0, 0.0).astype(BF)
+
+
+def split3(v):
+    high = v.astype(BF)
+    rest = v - high.astype(F32)
+    mid = rest.astype(BF)
+    return high, mid, (rest - mid.astype(F32)).astype(BF)
+
+
+def sigmoid(v):
+    return 1.0 / (1.0 + jnp.exp(-v))
+
+
+def rows_down(v, k):
+    return jnp.where(iota(v.shape, 0) >= k, pltpu.roll(v, k, 0), 0.0)
+
+
+def rows_up(v, k):
+    n = v.shape[0]
+    return jnp.where(iota(v.shape, 0) < n - k, pltpu.roll(v, n - k, 0), 0.0)
+
+
+def pick(v, lane, index):
+    return jnp.sum(jnp.where(lane == index, v, 0.0), axis=1, keepdims=True)
+
+
+class Sizes:
+    def __init__(self, dp, rows, half, inner, heads, state, capacity):
+        self.dp, self.rows, self.half, self.inner = dp, rows, half, inner
+        self.heads, self.state, self.cap = heads, state, capacity
+        self.width = 2 * half
+        self.nz = dp // 4
+        self.share = self.width // dp
+        self.quarter = self.nz * self.share
+        self.slots = dp * capacity
+        self.tiles = inner // 128
+        self.extra = 2 * state + 128
+        self.cols = 3 * inner + self.extra
+        n = inner // 2
+        self.chunks = [(i * n, n) for i in range(6)] + [(6 * n, self.extra)]
+        self.levels = self.nz.bit_length() - 1
+
+
+def targets_of(lines, sz):
+    n = sz.rows // 128
+    return jnp.concatenate([lines[pl.ds(k, sz.dp, stride=n), :] for k in range(n)], axis=1)
+
+
+def send_table(targets, g, sz):
+    strict = one_hot(iota((sz.rows, sz.rows), 0) < iota((sz.rows, sz.rows), 1))
+    every = targets_of(targets, sz)
+    own = jnp.sum(jnp.where(iota(every.shape, 0) == g, every, 0), axis=0, keepdims=True)
+    group = lax.shift_right_logical(own, 8)
+    hot = jnp.where(iota((sz.dp, sz.rows), 0) == group, 1.0, 0.0)
+    before = dot_nn(hot.astype(BF), strict)
+    rank = jnp.sum(hot * before, axis=0, keepdims=True)
+    spot = group.astype(F32) * sz.cap + rank
+    return one_hot(iota((sz.slots, sz.rows), 0).astype(F32) == spot)
+
+
+def owner_table(targets, g, sz):
+    strict = one_hot(iota((sz.rows, sz.rows), 0) < iota((sz.rows, sz.rows), 1))
+    every = targets_of(targets, sz)
+    mine = jnp.where(lax.shift_right_logical(every, 8) == g, 1.0, 0.0)
+    rank = dot_nn(mine.astype(BF), strict)
+    slot = mine * ((every & 255) + 1).astype(F32)
+    lane = iota((sz.dp, 128), 1)
+    found = jnp.zeros((sz.dp, 128), F32)
+    for a in range(sz.cap):
+        one = jnp.sum(jnp.where(rank == float(a), slot, 0.0), axis=1, keepdims=True)
+        found = jnp.where(lane == a, one, found)
+    place = iota((128, sz.slots), 1)
+    spread = one_hot((place % sz.cap) == iota((128, sz.slots), 0))
+    wide = dot_nn(found.astype(BF), spread)
+    keep = (iota((sz.dp, sz.slots), 1) // sz.cap) == iota((sz.dp, sz.slots), 0)
+    row = jnp.sum(jnp.where(keep, wide, 0.0), axis=0, keepdims=True) - 1.0
+    return one_hot(iota((sz.rows, sz.slots), 0).astype(F32) == row)
+
+
+def block_kernel(sz, *refs):
+    (dest, back, length, rows_hbm, ct_hbm, win_hbm, wout_hbm, wst_hbm, wstep_in,
+     tap_x, bias_x, gain_g, gain_n, skip_in, tap_s, bias_s, bias_step, log_rate,
+     out_rows, out_grads, inner_out, proj_out, extra_out, small_out, gain_out,
+     win, wout, wst, wstep, lines,
+     pk_in, pk_ct, rc_in, rc_ct, ry_in, ry_ct, gn_o, gn_g,
+     p_in, p_bk, q_in, q_bk,
+     hid, cts, normed, lowct, perm, xA, xE, tA, tE,
+     yb, pb, r0, rl,
+     inter, interT, igrad, ptile,
+     sraw, sslope, wr, dtv, lac, lar, sgr, rgr, stepsig, acc1, acc2, scale,
+     stat_s, stat_r, half_s, half_r, st_s, st_r,
+     sms, smr, gall, gsum,
+     a2a_s, a2a_r, fw_s, fw_r, quad_s, quad_r, xq_s, xq_r, z_s, z_r, y_s, y_r, gg_s, gg_r, sm_s, sm_r, w_s, o_s) = refs
+    dp, R, H, C = sz.dp, sz.rows, sz.half, sz.inner
+    W, NT_ = sz.width, sz.tiles
+    g = lax.axis_index("dp")
+    t = lax.axis_index("tensor")
+    o = 1 - t
+    c, x, z = g % 2, (g // 2) % 2, g // 4
+    q = g % 4
+    sib, xp = g + 1 - 2 * c, g + 2 - 4 * x
+    diag = sib + 2 - 4 * x
+
+    def rcopy(src, dst, ss, rs, peer, side=None):
+        return pltpu.make_async_remote_copy(
+            src_ref=src, dst_ref=dst, send_sem=ss, recv_sem=rs,
+            device_id=(peer, t if side is None else side), device_id_type=MESH)
+
+    sent = []
+
+    def go(copy):
+        copy.start()
+        sent.append(copy)
+        return copy
+
+    loads = [pltpu.make_async_copy(a, b, w_s.at[i]) for i, (a, b) in enumerate(
+        [(rows_hbm, cts.at[0]), (ct_hbm, cts.at[1]), (wst_hbm, wst), (wout_hbm, wout)])]
+    for load in loads[:2]:
+        load.start()
+
+    barrier = pltpu.get_barrier_semaphore()
+    for off in range(1, dp):
+        pl.semaphore_signal(barrier, inc=1, device_id=((g + off) % dp, t), device_id_type=MESH)
+    pl.semaphore_signal(barrier, inc=1, device_id=(g, o), device_id_type=MESH)
+
+    far = [(g + k) % dp for k in sorted(range(1, dp), key=lambda k: (abs(k - dp // 2), k))]
+
+    def exchange(i, source, target):
+        copies = []
+        for peer in far:
+            copies.append(rcopy(source.at[peer], target.at[g], a2a_s.at[i, peer], a2a_r.at[i, g], peer))
+            copies[-1].start()
+        target[pl.ds(g, 1)] = source[pl.ds(g, 1)]
+        return copies
+
+    def settle(copies):
+        for copy in copies:
+            copy.wait_send()
+
+    def arrived(i, target, src):
+        rcopy(target.at[src], target.at[src], a2a_s.at[i, src], a2a_r.at[i, src], src).wait_recv()
+
+    def pack(table, source, target):
+        for k in range(2):
+            n = sz.slots // 2
+            part = dot_nn(table[k * n:(k + 1) * n, :], source[...]).astype(BF)
+            target[k * (dp // 2):(k + 1) * (dp // 2)] = part.reshape(dp // 2, sz.cap, H)
+
+    p_in[...] = send_table(dest, g, sz)
+    loads[0].wait()
+    pack(p_in, cts.at[0], pk_in)
+    pl.semaphore_wait(barrier, dp)
+    rows_away = exchange(0, pk_in, rc_in)
+    for load in loads[2:]:
+        load.start()
+    p_bk[...] = send_table(back, g, sz)
+    loads[1].wait()
+    pack(p_bk, cts.at[1], pk_ct)
+    grads_away = exchange(1, pk_ct, rc_ct)
+    q_in[...] = owner_table(dest, g, sz)
+    q_bk[...] = owner_table(back, g, sz)
+
+    def forward(i, arr, dst, src):
+        arrived(i, arr, src)
+        return rcopy(arr.at[src], dst.at[src], fw_s.at[i, src], fw_r.at[i, src], g, o)
+
+    def own_forward(i, arr, dst):
+        go(rcopy(arr.at[g], dst.at[g], fw_s.at[i, g], fw_r.at[i, g], g, o))
+
+    own_forward(0, rc_in, ry_in)
+    row_forwards = [rcopy(rc_in.at[src], ry_in.at[src], fw_s.at[0, src], fw_r.at[0, src], g, o) for src in far]
+    sent.extend(row_forwards)
+
+    def forward_rows(k):
+        arrived(0, rc_in, far[k])
+        row_forwards[k].start()
+
+    def take_apart(stage, sems):
+        n = W // 128
+        fetch = [pltpu.make_async_copy(win_hbm.at[pl.ds(k * 128, 128)], stage.at[k % 4], sems.at[k % 4]) for k in range(n)]
+        for copy in fetch[:4]:
+            copy.start()
+        place = iota((256, 256), 0)
+        order = one_hot(iota((256, 256), 1) == jnp.where(place < 128, 2 * place, 2 * place - 255))
+        for k in range(n):
+            fetch[k].wait()
+            for m in range(0, C, 256):
+                pair = jnp.concatenate(
+                    [stage[k % 4, :, :, m + e:m + e + 128].reshape(256, 128) for e in (0, 128)], axis=1)
+                both = dot_nn(order, pair).astype(BF)
+                win[k * 128:(k + 1) * 128, m:m + 256] = both[:128]
+                win[k * 128:(k + 1) * 128, C + m:C + m + 256] = both[128:]
+            if k + 4 < n:
+                fetch[k + 4].start()
+            if k < dp - 1:
+                forward_rows(k)
+
+    pl.run_scoped(take_apart, pltpu.VMEM((4, 128, 2, C), BF), pltpu.SemaphoreType.DMA((4,)))
+    for k in range(W // 128, dp - 1):
+        forward_rows(k)
+    own_forward(1, rc_ct, ry_ct)
+    hid[pl.ds(t, 1)] = dot_nn(q_in[...], rc_in[...].reshape(sz.slots, H)).astype(BF)[None]
+    for d in range(dp):
+        rcopy(ry_in.at[d], ry_in.at[d], fw_s.at[0, d], fw_r.at[0, d], g, o).wait_recv()
+    hid[pl.ds(o, 1)] = dot_nn(q_in[...], ry_in[...].reshape(sz.slots, H)).astype(BF)[None]
+
+    total = jnp.zeros((R, 128), F32)
+    for k in range(W // 128):
+        v = hid[k // (H // 128), :, (k % (H // 128)) * 128:(k % (H // 128)) * 128 + 128].astype(F32)
+        total = total + v * v
+    norm_scale = lax.rsqrt(jnp.sum(total, axis=1, keepdims=True) / W + EPSILON)
+    scale[...] = jnp.broadcast_to(norm_scale, (R, 128))
+    for k in range(W // 128):
+        v = hid[k // (H // 128), :, (k % (H // 128)) * 128:(k % (H // 128)) * 128 + 128].astype(F32)
+        normed[:, k * 128:(k + 1) * 128] = (v * scale[...] * gain_n[:, k * 128:(k + 1) * 128]).astype(BF)
+
+    def quarters(source):
+        for qq in range(4):
+            perm[qq] = jnp.concatenate(
+                [source[:, sz.share * (4 * zz + qq):sz.share * (4 * zz + qq + 1)] for zz in range(sz.nz)], axis=1)
+
+    def send_quarter(i, dst):
+        copies = [
+            rcopy(perm.at[peer % 4], dst.at[rel], xq_s.at[i, rel - 1], xq_r.at[i, rel - 1], peer)
+            for rel, peer in ((2, xp), (3, diag), (1, sib))]
+        for copy in copies:
+            copy.start()
+        dst[0:1] = perm[pl.ds(q, 1)]
+        return copies
+
+    def turn_quarter(i, dst, turned):
+        for rel, peer in ((1, sib), (2, xp), (3, diag)):
+            rcopy(dst.at[rel], dst.at[rel], xq_s.at[i, rel - 1], xq_r.at[i, rel - 1], peer).wait_recv()
+        for rel in range(4):
+            turned[:, rel * R:(rel + 1) * R] = jnp.transpose(dst[rel].astype(F32)).astype(BF)
+
+    quarters(normed)
+    quarter_away = send_quarter(0, xA)
+
+    loads[2].wait()
+    wstep[...] = jnp.zeros_like(wstep)
+    wstep[:sz.heads] = wstep_in[...]
+    lines[...] = jnp.zeros_like(lines)
+    lines[0:1, :sz.heads] = bias_step[...]
+    lines[1:2, :sz.heads] = log_rate[...]
+    row = iota((R, 128), 0)
+    lane = iota((R, 128), 1)
+    live = jnp.where(row < length[0, 0], 1.0, 0.0)
+    sraw[...] = dot_nn(normed[...], wst[...])
+    step_in = dot_nt(normed[...], wstep[...]) + lines[0:1, :]
+    S = sz.state
+    for k in range(2):
+        cut = slice(k * S, (k + 1) * S)
+        raw = sraw[:, cut]
+        conv = bias_s[:, cut] + tap_s[0:1, cut] * raw
+        for tap in range(1, 4):
+            conv = conv + tap_s[tap:tap + 1, cut] * rows_down(raw, tap)
+        sg = sigmoid(conv)
+        sslope[:, cut] = sg * (1.0 + conv * (1.0 - sg))
+        wr[:, cut] = (conv * sg).astype(BF)
+    written, readout = wr[:, :S], wr[:, S:]
+    inter[...] = dot_nt(readout, written)
+    interT[...] = dot_nt(written, readout)
+    stepsig[...] = sigmoid(step_in) * live
+    heads_live = jnp.where(lane < sz.heads, live, 0.0)
+    step = (jnp.maximum(step_in, 0.0) + jnp.log1p(jnp.exp(-jnp.abs(step_in)))) * heads_live
+    rate = -jnp.exp(lines[1:2, :])
+    dtv[...] = step
+    lower = one_hot(iota((R, R), 0) >= iota((R, R), 1))
+    log_decay = sum(dot_nn(lower, part) for part in split3(step * rate))
+    lac[...] = log_decay
+    lar[...] = jnp.transpose(log_decay)
+
+    def cols_of(i):
+        return pl.ds(sz.chunks[i][0], sz.chunks[i][1])
+
+    def quad_send(i):
+        at = cols_of(i)
+        go(rcopy(yb.at[0, :, at], yb.at[2, :, at], quad_s.at[i, 1], quad_r.at[i, 1], xp))
+        go(rcopy(yb.at[0, :, at], yb.at[1, :, at], quad_s.at[i, 0], quad_r.at[i, 0], sib))
+
+    def quad_pass(i):
+        at = cols_of(i)
+        rcopy(yb.at[2, :, at], yb.at[2, :, at], quad_s.at[i, 1], quad_r.at[i, 1], xp).wait_recv()
+        go(rcopy(yb.at[2, :, at], yb.at[3, :, at], quad_s.at[i, 2], quad_r.at[i, 2], sib))
+
+    def z_peer(level):
+        bit = (z // 2 ** level) % 2
+        return bit, g + (1 - 2 * bit) * 4 * 2 ** level
+
+    bases = []
+    at0 = 0
+    for level in range(sz.levels):
+        bases.append(at0)
+        at0 += sz.nz // 2 ** (level + 1)
+    landing = [r0, rl]
+
+    def z_send(i, level):
+        bit, peer = z_peer(level)
+        at = cols_of(i)
+        for k in range(sz.nz // 2 ** (level + 1)):
+            low = z % 2 ** level
+            block = (2 * k + 1 - bit) * 2 ** level + low
+            go(rcopy(pb.at[block, :, at], landing[level].at[k, :, at], z_s.at[i, bases[level] + k],
+                     z_r.at[i, bases[level] + k], peer))
+
+    def z_add(i, level):
+        bit, peer = z_peer(level)
+        at = cols_of(i)
+        start, size = sz.chunks[i]
+        for k in range(sz.nz // 2 ** (level + 1)):
+            low = z % 2 ** level
+            block = (2 * k + bit) * 2 ** level + low
+            sem = bases[level] + k
+            rcopy(landing[level].at[k, :, at], landing[level].at[k, :, at], z_s.at[i, sem], z_r.at[i, sem], peer).wait_recv()
+            for n in range(0, size, 128):
+                cut = slice(start + n, start + n + 128)
+                value = pb[pl.ds(block, 1), :, cut].astype(F32)[0] + landing[level][k, :, cut].astype(F32)
+                if level + 1 < sz.levels:
+                    pb[pl.ds(block, 1), :, cut] = value.astype(BF)[None]
+                elif start + n < C:
+                    proj_out[:, cut] = value
+                elif start + n < 3 * C:
+                    inner_out[:, start + n - C:start + n - C + 128] = value
+                else:
+                    extra_out[:, start + n - 3 * C:start + n - 3 * C + 128] = value
+
+    def partial_sum(i, turned):
+        at = cols_of(i)
+        start, size = sz.chunks[i]
+        rcopy(yb.at[1, :, at], yb.at[1, :, at], quad_s.at[i, 0], quad_r.at[i, 0], sib).wait_recv()
+        rcopy(yb.at[3, :, at], yb.at[3, :, at], quad_s.at[i, 2], quad_r.at[i, 2], sib).wait_recv()
+        n = 384 if size % 256 else 256
+
+        def body(k, carry):
+            at = pl.ds(pl.multiple_of(start + k * n, 128), n)
+            part = dot_nn(turned[...], yb[:, :, at].reshape(4 * R, n))
+            pb[:, :, at] = part.astype(BF).reshape(sz.nz, sz.share, n)
+            return carry
+        lax.fori_loop(0, size // n, body, 0)
+        z_send(i, 0)
+
+    def remainder(gr, xr, xa, xs, mx, ng):
+        def project(dst, base):
+            def body(n, carry):
+                at = pl.multiple_of(n * 256, 256)
+                dst[:, pl.ds(at, 256)] = dot_nn(normed[...], win[:, pl.ds(pl.multiple_of(base + n * 256, 256), 256)])
+                return carry
+            lax.fori_loop(0, C // 256, body, 0)
+
+        project(xr, C)
+        project(gr, 0)
+
+        def send_ct(first, last):
+            for src in far[first:last]:
+                go(forward(1, rc_ct, ry_ct, src))
+
+        send_ct(0, 7)
+
+        def lanes(p):
+            return pl.ds(pl.multiple_of(p * 128, 128), 128)
+
+        B = 64
+
+        def head_line(v, p):
+            first = iota((1, 128), 1) < 64
+            spot = iota(v.shape, 1)
+            return jnp.where(first, pick(v, spot, 2 * p), pick(v, spot, 2 * p + 1))
+
+        def step_columns(p, lane):
+            first = lane < 64
+            return jnp.where(first, pick(dtv[...], lane, 2 * p), pick(dtv[...], lane, 2 * p + 1))
+
+        acc1[...] = jnp.zeros_like(acc1)
+        acc2[...] = jnp.zeros_like(acc2)
+
+        def scan(p, carry):
+            at = lanes(p)
+            lane = iota((R, 128), 1)
+            raw = xr[:, at]
+            conv = bias_x[:, at] + tap_x[0:1, at] * raw
+            for tap in range(1, 4):
+                conv = conv + tap_x[tap:tap + 1, at] * rows_down(raw, tap)
+            sg = sigmoid(conv)
+            act = conv * sg
+            xa[:, at] = act
+            xs[:, at] = (sg * (1.0 + conv * (1.0 - sg))).astype(BF)
+            driven = act * step_columns(p, lane)
+            parts = [jnp.where(lane < 64, driven, 0.0).astype(BF), jnp.where(lane >= 64, driven, 0.0).astype(BF)]
+            cols = [pick(lac[...], lane, 2 * p + k) for k in range(2)]
+            skip = head_line(skip_in[...], p)
+            for b in range(R // B):
+                reach = 128 * ((b * B) // 128 + 1)
+                cut = slice(b * B, (b + 1) * B)
+                causal = iota((B, reach), 0) + b * B >= iota((B, reach), 1)
+                mixed = skip * act[cut]
+                for k in range(2):
+                    spread = cols[k][cut] - lar[pl.ds(2 * p + k, 1), :][:, :reach]
+                    fading = jnp.exp(jnp.where(causal, spread, NEG))
+                    mixing = (inter[cut, :reach] * fading).astype(BF)
+                    mixed = mixed + dot_nn(mixing, parts[k][:reach])
+                mx[cut, at] = mixed
+                gate = gr[cut, at]
+                gated = mixed * gate * sigmoid(gate)
+                acc1[cut] += gated * gated
+            return carry
+
+        step4 = NT_ // 4
+        for k in range(4):
+            lax.fori_loop(k * step4, (k + 1) * step4, scan, 0)
+            send_ct(7 + k, 8 + k)
+
+        whole = float(2 * C)
+
+        def total_over_sides(i, value):
+            stat_s[i] = jnp.transpose(jnp.where(lane == 0, jnp.sum(value, axis=1, keepdims=True), 0.0))[:8]
+            return go(rcopy(stat_s.at[i], stat_r.at[i], y_s.at[i], y_r.at[i], g, o))
+
+        def total_here(i):
+            both = jnp.concatenate([stat_s[i] + stat_r[i], jnp.zeros((120, R), F32)], axis=0)
+            return pick(jnp.transpose(both), lane, 0)
+
+        total_over_sides(0, acc1[...]).wait_recv()
+        gate_scale = lax.rsqrt(total_here(0) / whole + EPSILON)
+        acc1[...] = jnp.broadcast_to(gate_scale, (R, 128))
+
+        def gate_forward(p, carry):
+            at = lanes(p)
+            gate = gr[:, at]
+            yb[0, :, at] = (mx[:, at] * (gate * sigmoid(gate)) * acc1[...] * gain_g[:, at]).astype(BF)
+            return carry
+        lax.fori_loop(0, NT_, gate_forward, 0)
+        turn_quarter(0, xA, tA)
+        quad_send(0)
+        quad_send(1)
+
+        send_ct(11, dp - 1)
+        loads[3].wait()
+
+        def out_half(side, dst, cast):
+            def body(n, carry):
+                at = pl.ds(pl.multiple_of(side * H + n * 256, 256), 256)
+                dst[:, pl.ds(pl.multiple_of(n * 256, 256), 256)] = dot_nn(yb[0, :, :C], wout[:, at]).astype(cast)
+                return carry
+            lax.fori_loop(0, H // 256, body, 0)
+        out_half(o, half_s.at[0], BF)
+        cts[pl.ds(t, 1)] = dot_nn(q_bk[...], rc_ct[...].reshape(sz.slots, H)).astype(BF)[None]
+        for d in range(dp):
+            rcopy(ry_ct.at[d], ry_ct.at[d], fw_s.at[1, d], fw_r.at[1, d], g, o).wait_recv()
+        cts[pl.ds(o, 1)] = dot_nn(q_bk[...], ry_ct[...].reshape(sz.slots, H)).astype(BF)[None]
+        for k in range(W // 128):
+            v = cts[k // (H // 128), :, (k % (H // 128)) * 128:(k % (H // 128)) * 128 + 128].astype(F32)
+            lowct[:, k * 128:(k + 1) * 128] = (v * live).astype(BF)
+
+        def back_project(n, carry):
+            at = pl.ds(pl.multiple_of(n * 256, 256), 256)
+            ng[:, at] = dot_nt(lowct[...], wout[at, :])
+            for k in range(2):
+                here = pl.ds(pl.multiple_of(n * 256 + k * 128, 128), 128)
+                gate = gr[:, here]
+                acc2[...] += mx[:, here] * (gate * sigmoid(gate)) * (gain_g[:, here] * ng[:, here])
+            return carry
+        lax.fori_loop(0, C // 256, back_project, 0)
+        crossed = total_over_sides(1, acc2[...])
+        settle(quarter_away)
+        quarters(lowct)
+        sent.extend(send_quarter(1, xE))
+        crossed.wait_recv()
+        go(rcopy(half_s.at[0], half_r.at[0], y_s.at[2], y_r.at[2], g, o))
+        acc2[...] = acc1[...] * acc1[...] * acc1[...] * (total_here(1) / whole)
+
+        def gate_back(p, carry):
+            at = lanes(p)
+            gate, mixed, grad = gr[:, at], mx[:, at], ng[:, at]
+            sg = sigmoid(gate)
+            act = gate * sg
+            gated = mixed * act
+            gated_grad = acc1[...] * (gain_g[:, at] * grad) - gated * acc2[...]
+            sms[0, 5:6, at] = jnp.sum(grad * gated * acc1[...], axis=0, keepdims=True)
+            mixed_grad = gated_grad * act
+            ng[:, at] = mixed_grad
+            sms[0, 6:7, at] = jnp.sum(mixed_grad * xa[:, at], axis=0, keepdims=True)
+            yb[0, :, pl.ds(pl.multiple_of(C + p * 128, 128), 128)] = (
+                gated_grad * mixed * (sg * (1.0 + gate * (1.0 - sg)))).astype(BF)
+            return carry
+        lax.fori_loop(0, NT_, gate_back, 0)
+        quad_send(2)
+        quad_send(3)
+        out_half(t, gr, F32)
+
+        igrad[...] = jnp.zeros_like(igrad)
+        sgr[...] = jnp.zeros_like(sgr)
+        rgr[...] = jnp.zeros_like(rgr)
+        ptile[...] = jnp.zeros_like(ptile)
+
+        def scan_back(p, carry):
+            at = lanes(p)
+            lane = iota((R, 128), 1)
+            grad = ng[:, at]
+            act = xa[:, at]
+            stepw = step_columns(p, lane)
+            driven = (act * stepw).astype(BF)
+            parts = [jnp.where(lane < 64, grad, 0.0).astype(BF), jnp.where(lane >= 64, grad, 0.0).astype(BF)]
+            cols = [pick(lac[...], lane, 2 * p + k) for k in range(2)]
+            pieces = []
+            for b in range(R // B):
+                skip = 128 * ((b * B) // 128)
+                cut = slice(b * B, (b + 1) * B)
+                causal = iota((B, R - skip), 1) + skip >= iota((B, R - skip), 0) + b * B
+                turned = interT[cut, skip:]
+                piece = jnp.zeros((B, 128), F32)
+                total = igrad[cut, skip:]
+                for k in range(2):
+                    spread = lar[pl.ds(2 * p + k, 1), :][:, skip:] - cols[k][cut]
+                    fading = jnp.exp(jnp.where(causal, spread, NEG))
+                    faded = dot_nt(driven[cut], parts[k][skip:]) * fading
+                    total = total + faded
+                    piece = piece + dot_nn((turned * fading).astype(BF), parts[k][skip:])
+                    ptile[k, cut, skip:] = (faded * turned).astype(BF)
+                igrad[cut, skip:] = total
+                pieces.append(piece)
+            strict = one_hot(iota((R, R), 0) > iota((R, R), 1))
+            for k in range(2):
+                found = []
+                for b in range(R // B):
+                    skip = 128 * ((b * B) // 128)
+                    cut = slice(b * B, (b + 1) * B)
+                    causal = iota((B, R - skip), 1) + skip >= iota((B, R - skip), 0) + b * B
+                    sums = dot_nn(strict[cut], ptile[k, :, skip:])
+                    found.append(jnp.sum(jnp.where(causal, sums, 0.0), axis=1, keepdims=True))
+                rgr[...] = jnp.where(lane == 2 * p + k, jnp.concatenate(found, axis=0), rgr[...])
+            driven_grad = jnp.concatenate(pieces, axis=0)
+            pulled = driven_grad * act
+            low = jnp.sum(jnp.where(lane < 64, pulled, 0.0), axis=1, keepdims=True)
+            high = jnp.sum(jnp.where(lane >= 64, pulled, 0.0), axis=1, keepdims=True)
+            sgr[...] = jnp.where(lane == 2 * p, low, jnp.where(lane == 2 * p + 1, high, sgr[...]))
+            conv_grad = (head_line(skip_in[...], p) * grad + stepw * driven_grad) * xs[:, at].astype(F32)
+            raw = xr[:, at]
+            raw_grad = tap_x[0:1, at] * conv_grad
+            sms[0, 0:1, at] = jnp.sum(conv_grad * raw, axis=0, keepdims=True)
+            sms[0, 4:5, at] = jnp.sum(conv_grad, axis=0, keepdims=True)
+            for tap in range(1, 4):
+                up = rows_up(conv_grad, tap)
+                raw_grad = raw_grad + tap_x[tap:tap + 1, at] * up
+                sms[0, tap:tap + 1, at] = jnp.sum(up * raw, axis=0, keepdims=True)
+            yb[0, :, pl.ds(pl.multiple_of(2 * C + p * 128, 128), 128)] = raw_grad.astype(BF)
+            return carry
+
+        lax.fori_loop(0, NT_ // 2, scan_back, 0)
+        quad_send(4)
+        turn_quarter(1, xE, tE)
+        quad_pass(0)
+        quad_pass(1)
+        partial_sum(0, tE)
+
+        rcopy(half_r.at[0], half_r.at[0], y_s.at[2], y_r.at[2], g, o).wait_recv()
+
+        def answer(table, value, dst):
+            for k in range(2):
+                n = sz.slots // 2
+                part = dot_tn(table[:, k * n:(k + 1) * n], value).astype(BF)
+                dst[k * (dp // 2):(k + 1) * (dp // 2)] = part.reshape(dp // 2, sz.cap, H)
+
+        pieces = []
+        mine = hid[pl.ds(t, 1)][0]
+        for k in range(H // 128):
+            cut = slice(k * 128, (k + 1) * 128)
+            branch = gr[:, cut] + half_r[0, :, cut].astype(F32)
+            pieces.append((mine[:, cut].astype(F32) + live * branch).astype(BF))
+        settle(rows_away)
+        answer(q_bk, jnp.concatenate(pieces, axis=1), pk_in)
+        sent.extend(exchange(2, pk_in, gn_o))
+
+        lax.fori_loop(NT_ // 2, NT_, scan_back, 0)
+        quad_send(5)
+
+        ig = igrad[...].astype(BF)
+        st_s[:, :S] = dot_nn(ig, wr[:, S:]).astype(BF)
+        st_s[:, S:] = dot_tn(ig, wr[:, :S]).astype(BF)
+        go(rcopy(st_s, st_r, y_s.at[3], y_r.at[3], g, o))
+        step_grad = (sgr[...] + rgr[...] * rate) * stepsig[...]
+        yb[0, :, 3 * C + 2 * S:] = step_grad.astype(BF)
+        sms[0, 7:8, 10 * S:10 * S + 128] = jnp.sum(step_grad, axis=0, keepdims=True)
+        sms[0, 7:8, 10 * S + 128:10 * S + 256] = jnp.sum(rgr[...] * dtv[...], axis=0, keepdims=True) * rate
+        partial_sum(1, tE)
+        rcopy(st_r, st_r, y_s.at[3], y_r.at[3], g, o).wait_recv()
+        for k in range(2):
+            cut = slice(k * S, (k + 1) * S)
+            conv_grad = (st_s[:, cut].astype(F32) + st_r[:, cut].astype(F32)) * sslope[:, cut]
+            raw = sraw[:, cut]
+            raw_grad = tap_s[0:1, cut] * conv_grad
+            sms[0, 7:8, cut] = jnp.sum(conv_grad * raw, axis=0, keepdims=True)
+            sms[0, 7:8, 8 * S + k * S:8 * S + (k + 1) * S] = jnp.sum(conv_grad, axis=0, keepdims=True)
+            for tap in range(1, 4):
+                up = rows_up(conv_grad, tap)
+                raw_grad = raw_grad + tap_s[tap:tap + 1, cut] * up
+                sms[0, 7:8, tap * 2 * S + k * S:tap * 2 * S + (k + 1) * S] = jnp.sum(up * raw, axis=0, keepdims=True)
+            yb[0, :, 3 * C + k * S:3 * C + (k + 1) * S] = raw_grad.astype(BF)
+        quad_send(6)
+
+        hops = [2 ** k for k in range(2, dp.bit_length() - 1)] + [1, 2]
+
+        def small_start(i):
+            bit = (g // hops[i]) % 2
+            go(rcopy(sms.at[i], smr.at[i], sm_s.at[i], sm_r.at[i], g + (1 - 2 * bit) * hops[i]))
+
+        def small_end(i):
+            bit = (g // hops[i]) % 2
+            rcopy(sms.at[i], smr.at[i], sm_s.at[i], sm_r.at[i], g + (1 - 2 * bit) * hops[i]).wait_recv()
+            if i + 1 < len(hops):
+                sms[i + 1] = sms[i] + smr[i]
+                small_start(i + 1)
+            else:
+                small_out[...] = sms[i] + smr[i]
+        small_start(0)
+
+        acc1[...] = jnp.zeros_like(acc1)
+
+        def normed_grad(side, dst, cast):
+            def body(n, carry):
+                at = pl.ds(pl.multiple_of(side * H + n * 256, 256), 256)
+                value = dot_nt(yb[0, :, C:3 * C], win[at, :])
+                mine_state = pl.ds(pl.multiple_of(t * S, 128), S)
+                value = value + dot_nt(yb[0, :, pl.ds(pl.multiple_of(3 * C + t * S, 128), S)], wst[at, mine_state])
+                value = value + dot_nn(yb[0, :, 3 * C + 2 * S:], wstep[:, at])
+                for k in range(2):
+                    cut = slice(k * 128, (k + 1) * 128)
+                    here = pl.ds(pl.multiple_of(n * 256 + k * 128, 128), 128)
+                    there = pl.ds(pl.multiple_of(side * H + n * 256 + k * 128, 128), 128)
+                    acc1[...] += hid[pl.ds(side, 1), :, here][0].astype(F32) * (gain_n[:, there] * value[:, cut])
+                dst[:, pl.ds(pl.multiple_of(n * 256, 256), 256)] = value.astype(cast)
+                return carry
+            lax.fori_loop(0, H // 256, body, 0)
+        normed_grad(o, half_s.at[1], BF)
+        go(rcopy(half_s.at[1], half_r.at[1], y_s.at[4], y_r.at[4], g, o))
+        normed_grad(t, gr, F32)
+        summed_rows = total_over_sides(2, acc1[...])
+        z_add(0, 0)
+        z_send(0, 1)
+        quad_pass(2)
+        partial_sum(2, tA)
+        small_end(0)
+
+        rcopy(half_r.at[1], half_r.at[1], y_s.at[4], y_r.at[4], g, o).wait_recv()
+        summed_rows.wait_recv()
+        pull = total_here(2) / W * (scale[...] * scale[...] * scale[...])
+        pieces = []
+        mine = hid[pl.ds(t, 1)][0]
+        mine_ct = cts[pl.ds(t, 1)][0]
+        gall[pl.ds(g, 1)] = jnp.zeros((1, 8, 128), F32)
+        for k in range(H // 128):
+            cut = slice(k * 128, (k + 1) * 128)
+            there = pl.ds(pl.multiple_of(t * H + k * 128, 128), 128)
+            value = gr[:, cut] + half_r[1, :, cut].astype(F32)
+            rows_here = mine[:, cut].astype(F32)
+            gall[pl.ds(g, 1), k:k + 1, :] = jnp.sum(value * rows_here * scale[...], axis=0, keepdims=True)[None]
+            pieces.append((scale[...] * (gain_n[:, there] * value) - rows_here * pull
+                           + mine_ct[:, cut].astype(F32)).astype(BF))
+        settle(grads_away)
+        answer(q_in, jnp.concatenate(pieces, axis=1), pk_ct)
+        for peer in far:
+            go(rcopy(gall.at[g], gall.at[g], gg_s.at[peer], gg_r.at[g], peer))
+        sent.extend(exchange(3, pk_ct, gn_g))
+
+        def reduce_further(i):
+            z_add(i, 0)
+            z_send(i, 1)
+
+        reduce_further(1)
+        quad_pass(3)
+        partial_sum(3, tA)
+        reduce_further(2)
+        small_end(1)
+        quad_pass(4)
+        partial_sum(4, tA)
+        reduce_further(3)
+        small_end(2)
+        z_add(0, 1)
+        z_add(1, 1)
+        quad_pass(5)
+        partial_sum(5, tA)
+        reduce_further(4)
+        quad_pass(6)
+        partial_sum(6, tA)
+        z_add(2, 1)
+        z_add(3, 1)
+
+        def give(i, value, stage, dst):
+            n = R // sz.cap
+            stage[:n] = value.astype(BF).reshape(n, sz.cap, H)
+            copies = [pltpu.make_async_copy(stage.at[k], dst.at[pl.ds(k * sz.cap, sz.cap)], o_s.at[i, k]) for k in range(n)]
+            for copy in copies:
+                copy.start()
+            return copies
+
+        for src in far:
+            arrived(2, gn_o, src)
+        stores = give(0, dot_tn(p_bk[...], gn_o[...].reshape(sz.slots, H)), ry_in, out_rows)
+        reduce_further(5)
+        reduce_further(6)
+        small_end(3)
+        for src in far:
+            rcopy(gall.at[src], gall.at[src], gg_s.at[src], gg_r.at[src], src).wait_recv()
+        summed = gall[0]
+        for d in range(1, dp):
+            summed = summed + gall[d]
+        gsum[pl.ds(t, 1)] = summed[None]
+        go(rcopy(gsum.at[t], gsum.at[t], y_s.at[5], y_r.at[5], g, o))
+        for src in far:
+            arrived(3, gn_g, src)
+        stores += give(1, dot_tn(p_in[...], gn_g[...].reshape(sz.slots, H)), ry_ct, out_grads)
+        z_add(4, 1)
+        z_add(5, 1)
+        z_add(6, 1)
+        rcopy(gsum.at[o], gsum.at[o], y_s.at[5], y_r.at[5], g, o).wait_recv()
+        gain_out[...] = gsum[...]
+        for copy in sent:
+            copy.wait_send()
+        for store in stores:
+            store.wait()
+
+    big = pltpu.VMEM((R, C), F32)
+    pl.run_scoped(remainder, big, big, big, pltpu.VMEM((R, C), BF), big, big)
+
+
+def finish_kernel(sz, rows, grads, inner, proj, extra, small, gain, o_rows, o_grads, o_gain, o_inner, o_state, o_step,
+                  o_tap_x, o_bias_x, o_tap_s, o_bias_s, o_bias_step, o_rate, o_skip, o_gate, o_proj):
+    C, S = sz.inner, sz.state
+    o_rows[...] = rows[...]
+    o_grads[...] = grads[...]
+    o_inner[:, 0, :] = inner[:, :C]
+    o_inner[:, 1, :] = inner[:, C:]
+    o_proj[...] = jnp.transpose(proj[...])
+    o_state[...] = extra[:, :2 * S]
+    o_step[...] = extra[:, 2 * S:2 * S + sz.heads]
+    o_tap_x[...] = small[0:4, :]
+    o_bias_x[...] = small[4, :]
+    o_gate[...] = small[5, :]
+    for k in range(4):
+        o_tap_s[k:k + 1, :] = small[7:8, k * 2 * S:(k + 1) * 2 * S]
+    o_bias_s[...] = small[7, 8 * S:10 * S]
+    o_bias_step[...] = small[7, 10 * S:10 * S + sz.heads]
+    o_rate[...] = small[7, 10 * S + 128:10 * S + 128 + sz.heads]
+    shape = (C, sz.heads)
+    member = one_hot(iota(shape, 0) // (C // sz.heads) == iota(shape, 1))
+    skip = jnp.broadcast_to(small[6:7, :], (8, C))
+    o_skip[...] = sum(dot_nn(part, member) for part in split3(skip))[0]
+    flat = jnp.concatenate([gain[h, k:k + 1, :] for h in range(2) for k in range(sz.half // 128)], axis=1)
+    start = lax.axis_index("dp") * sz.share
+    moved = pltpu.roll(jnp.broadcast_to(flat, (8, sz.width)), lax.rem(sz.width - start, sz.width), 1)
+    o_gain[...] = moved[0, :sz.share]
+
+
+def fused(sz, block_in, cotangent, lengths, dest_slot, return_slot, norm_gain, inner_weight, state_weight,
+          step_weight, conv_inner, conv_inner_bias, conv_state, conv_state_bias, step_bias, log_rate,
+          skip_gain, gate_gain, out_weight):
+    dp, R, H, C, S = sz.dp, sz.rows, sz.half, sz.inner, sz.state
+    W = sz.width
+
+    vm = pl.BlockSpec(memory_space=pltpu.VMEM)
+    hb = pl.BlockSpec(memory_space=pl.ANY)
+    sm = pl.BlockSpec(memory_space=pltpu.SMEM)
+    V = pltpu.VMEM
+    packed = V((dp, sz.cap, H), BF)
+    D = pltpu.SemaphoreType.DMA
+    nch = len(sz.chunks)
+    scratch = [
+        V((W, 2 * C), BF), V((C, W), BF), V((W, 2 * S), BF), V((128, W), BF), V((8, 128), F32),
+        *[packed] * 8,
+        V((sz.slots, R), BF), V((sz.slots, R), BF), V((R, sz.slots), BF), V((R, sz.slots), BF),
+        V((2, R, H), BF), V((2, R, H), BF), V((R, W), BF), V((R, W), BF),
+        V((4, R, sz.quarter), BF), V((4, R, sz.quarter), BF), V((4, R, sz.quarter), BF),
+        V((sz.quarter, 4 * R), BF), V((sz.quarter, 4 * R), BF),
+        V((4, R, sz.cols), BF), V((sz.nz, sz.share, sz.cols), BF), V((2, sz.share, sz.cols), BF), V((1, sz.share, sz.cols), BF),
+        V((R, R), F32), V((R, R), F32), V((R, R), F32), V((2, R, R), BF),
+        V((R, 2 * S), F32), V((R, 2 * S), F32), V((R, 2 * S), BF), V((R, 128), F32), V((R, 128), F32), V((128, R), F32),
+        V((R, 128), F32), V((R, 128), F32), V((R, 128), F32), V((R, 128), F32), V((R, 128), F32), V((R, 128), F32),
+        V((3, 8, R), F32), V((3, 8, R), F32), V((2, R, H), BF), V((2, R, H), BF),
+        V((R, 2 * S), BF), V((R, 2 * S), BF),
+        V((4, 8, C), F32), V((4, 8, C), F32), V((dp, 8, 128), F32), V((2, 8, 128), F32),
+        D((4, dp)), D((4, dp)), D((2, dp)), D((2, dp)), D((nch, 3)), D((nch, 3)), D((2, 3)), D((2, 3)),
+        D((nch, sz.nz - 1)), D((nch, sz.nz - 1)), D((6,)), D((6,)), D((dp,)), D((dp,)), D((4,)), D((4,)), D((4,)), D((2, dp)),
+    ]
+    out = jax.ShapeDtypeStruct
+    rows_out, grads_out, inner_g, proj_g, extra_g, small, gain = pl.pallas_call(
+        functools.partial(block_kernel, sz),
+        out_shape=(out((R, H), BF), out((R, H), BF), out((sz.share, 2 * C), F32), out((sz.share, C), F32),
+                   out((sz.share, sz.extra), F32), out((8, C), F32), out((2, 8, 128), F32)),
+        in_specs=[vm, vm, sm, hb, hb, hb, hb, hb] + [vm] * 10,
+        out_specs=(hb, hb) + (vm,) * 5,
+        scratch_shapes=scratch,
+        compiler_params=pltpu.CompilerParams(collective_id=0, has_side_effects=True, vmem_limit_bytes=66000000),
+        name="block",
+    )(dest_slot.reshape(-1, 128), return_slot.reshape(-1, 128), lengths, block_in, cotangent, inner_weight, out_weight,
+      state_weight, step_weight.T, conv_inner, conv_inner_bias[None], gate_gain[None], norm_gain[None], skip_gain[None],
+      conv_state, conv_state_bias[None], step_bias[None], log_rate[None])
+    return pl.pallas_call(
+        functools.partial(finish_kernel, sz),
+        out_shape=(out((R, H), BF), out((R, H), BF), out((sz.share,), F32), out((sz.share, 2, C), F32),
+                   out((sz.share, 2 * S), F32), out((sz.share, sz.heads), F32), out((4, C), F32), out((C,), F32),
+                   out((4, 2 * S), F32), out((2 * S,), F32), out((sz.heads,), F32), out((sz.heads,), F32),
+                   out((sz.heads,), F32), out((C,), F32), out((C, sz.share), F32)),
+        in_specs=[vm] * 7,
+        out_specs=(vm,) * 15,
+        name="finish",
+    )(rows_out, grads_out, inner_g, proj_g, extra_g, small, gain)
+
+
+def with_collectives(
     block_in,
     cotangent,
     lengths,
@@ -423,6 +1259,20 @@
     )
 
 
+def on_device(*args):
+    groups = lax.axis_size("dp")
+    rows, half = args[0].shape
+    inner, heads, state = args[6].shape[2], args[8].shape[1], args[7].shape[1] // 2
+    capacity = 2 * rows // groups
+    fits = (
+        groups % 4 == 0 and 16 <= 4 * groups <= 64 and capacity % 16 == 0 and (2 * half // groups) % 16 == 0
+        and rows == STRETCH and args[2].shape[1] == 1 and inner == 64 * heads and inner == 2 * half
+    )
+    if fits:
+        return fused(Sizes(groups, rows, half, inner, heads, state, capacity), *args)
+    return with_collectives(*args)
+
+
 def solution(mesh):
     placed = (
         P("dp", "tensor"),

time: 698 us -> 208 us (0.30)
  the two profiles are of different devices: /device:TPU:0 before, /device:TPU:26 now
where the time goes in v3:
time: 208 us
  Pallas kernels  199 us (96%)
  local copies, waits for them, and re-layouts  7.56 us (4%)
    pallas_call x1, Pallas kernels, fused(): pl.pallas_call(functools.partial(block_kernel, sz), out_shape=(out((R, H)...  195 us

profile of v3, /device:TPU:26, one launch (start us, length us, event | category | flops | bytes accessed | tf_op | source)
XLA Modules:
  0.0 208.0 jit_solution(2640211553040344095)
XLA Ops:
  1.3 1.3 broadcast_in_dim.23.refs_12_
  2.6 1.3 broadcast_in_dim.21.refs_10_
  3.9 1.3 broadcast_in_dim.22.refs_11_
  5.2 195.4 %block.1 = (bf16[256,768]{1,0:T(8,128)(2,1)}, bf16[256,768]{1,0:T(8,128)(2,1)}, f32[96,3072]{1,0:T(8,128)}, f32[96,1536]{1,0:T(8,128)}, f32[96,384]{1,0:T(8,128)...) custom-call(s32[32,128]{1,0:T(8,128)} %bitcast.8, s32[32,128]{1,0:T(8,128)} %bitcast.9, s32[1,1]{1,0:T(1,128)S(6)} %copy.35.refs_2_, ...), custom_call_target="tpu_custom_call" | custom-call | tf_op jit(solution)/shard_map/block/pallas_call | solution.py:1012
  200.6 3.7 %finish.1 = (bf16[256,768]{1,0:T(8,128)(2,1)}, bf16[256,768]{1,0:T(8,128)(2,1)}, f32[96]{0:T(128)}, f32[96,2,1536]{2,1,0:T(2,128)}, f32[96,256]{1,0:T(8,128)}, /...) custom-call(bf16[256,768]{1,0:T(8,128)(2,1)} %get-tuple-element.22.r, ...), custom_call_target="tpu_custom_call" | custom-call | tf_op jit(solution)/shard_map/finish/pallas_call | solution.py:1024
  204.3 1.5 copy.33
  205.8 2.2 %copy.34 = f32[1536,96]{0,1:T(8,128)} copy(f32[1536,96]{1,0:T(8,128)} %get-tuple-element.43) | data formatting | bytes 1179648 | tf_op jit(solution)/shard_map/finish/pallas_call | solution.py:1024

commit v4 on v3

--- a/solution.py
+++ b/solution.py
@@ -309,15 +309,15 @@
      tap_x, bias_x, gain_g, gain_n, skip_in, tap_s, bias_s, bias_step, log_rate,
      out_rows, out_grads, inner_out, proj_out, extra_out, small_out, gain_out,
      win, wout, wst, wstep, lines,
-     pk_in, pk_ct, rc_in, rc_ct, ry_in, ry_ct, gn_o, gn_g,
-     p_in, p_bk, q_in, q_bk,
+     pk_in, pk_ct, rc_in, rc_ct, gn_o, gn_g,
+     p_own, q_in, q_bk,
      hid, cts, normed, lowct, perm, xA, xE, tA, tE,
-     yb, pb, r0, rl,
-     inter, interT, igrad, ptile,
+     yb, pb, r0, r1,
+     inter, igrad, ptile,
      sraw, sslope, wr, dtv, lac, lar, sgr, rgr, stepsig, acc1, acc2, scale,
-     stat_s, stat_r, half_s, half_r, st_s, st_r,
+     stat_s, stat_r, half_s, half_r, raw_r, st_s, st_r,
      sms, smr, gall, gsum,
-     a2a_s, a2a_r, fw_s, fw_r, quad_s, quad_r, xq_s, xq_r, z_s, z_r, y_s, y_r, gg_s, gg_r, sm_s, sm_r, w_s, o_s) = refs
+     a2a_s, a2a_r, fw_s, fw_r, quad_s, quad_r, xq_s, xq_r, z_s, z_r, y_s, y_r, gg_s, gg_r, sm_s, sm_r, w_s, own_s, relay_s, raw_sem, taken) = refs
     dp, R, H, C = sz.dp, sz.rows, sz.half, sz.inner
     W, NT_ = sz.width, sz.tiles
     g = lax.axis_index("dp")
@@ -341,7 +341,7 @@
         return copy
 
     loads = [pltpu.make_async_copy(a, b, w_s.at[i]) for i, (a, b) in enumerate(
-        [(rows_hbm, cts.at[0]), (ct_hbm, cts.at[1]), (wst_hbm, wst), (wout_hbm, wout)])]
+        [(rows_hbm, lowct.at[:, pl.ds(0, H)]), (ct_hbm, lowct.at[:, pl.ds(H, H)]), (wst_hbm, wst), (wout_hbm, wout)])]
     for load in loads[:2]:
         load.start()
 
@@ -350,22 +350,106 @@
         pl.semaphore_signal(barrier, inc=1, device_id=((g + off) % dp, t), device_id_type=MESH)
     pl.semaphore_signal(barrier, inc=1, device_id=(g, o), device_id_type=MESH)
 
-    far = [(g + k) % dp for k in sorted(range(1, dp), key=lambda k: (abs(k - dp // 2), k))]
-
-    def exchange(i, source, target):
-        copies = []
-        for peer in far:
-            copies.append(rcopy(source.at[peer], target.at[g], a2a_s.at[i, peer], a2a_r.at[i, g], peer))
-            copies[-1].start()
-        target[pl.ds(g, 1)] = source[pl.ds(g, 1)]
+    side = z // 2
+    zo, zi, fi, fo = 3 * side, 1 + side, 2 - side, 3 - 3 * side
+    is_outer = (z + side + 1) % 2
+    is_inner = 1 - is_outer
+    far = [
+        ((z + dz) % sz.nz) * 4 + ((x + dx) % 2) * 2 + (c + dc) % 2
+        for dz in (2, 1, 3, 0) for dx in (1, 0) for dc in (1, 0) if dz + dx + dc]
+    level = [z * 4 + ((x + dx) % 2) * 2 + (c + dc) % 2 for dx, dc in ((1, 1), (1, 0), (0, 1))]
+    across = [zz * 4 + ((x + dx) % 2) * 2 + (c + dc) % 2 for zz in (fo, fi) for dx in (1, 0) for dc in (1, 0)]
+    beside_z = is_outer * zi + (1 - is_outer) * zo
+    beside = [beside_z * 4 + ((x + dx) % 2) * 2 + (c + dc) % 2 for dx, dc in ((1, 1), (1, 0), (0, 1))]
+    partner = beside_z * 4 + q
+    parts = [pl.ds(0, H // 3 * 2), pl.ds(H // 3 * 2, H // 3)]
+
+    def exchange(i, source, target, at=slice(None)):
+        copies = [
+            rcopy(source.at[peer, :, at], target.at[g, :, at], a2a_s.at[i, peer], a2a_r.at[i, g], peer) for peer in far]
+        for copy in copies:
+            copy.start()
         return copies
 
     def settle(copies):
         for copy in copies:
             copy.wait_send()
 
-    def arrived(i, target, src):
-        rcopy(target.at[src], target.at[src], a2a_s.at[i, src], a2a_r.at[i, src], src).wait_recv()
+    def arrived(i, target, at=slice(None)):
+        for src in far:
+            rcopy(target.at[src, :, at], target.at[src, :, at], a2a_s.at[i, src], a2a_r.at[i, src], src).wait_recv()
+
+    def answer(table, value, dst):
+        for k in range(2):
+            n = sz.slots // 2
+            part = dot_tn(table[:, k * n:(k + 1) * n], value).astype(BF)
+            dst[k * (dp // 2):(k + 1) * (dp // 2)] = part.reshape(dp // 2, sz.cap, H)
+
+    def block_to(i, source, target, peer, owner, sems):
+        return rcopy(source.at[peer], target.at[owner], sems.at[i - 4, peer], a2a_r.at[i, owner], peer)
+
+    def raw_copy(i):
+        return rcopy(lowct.at[:, pl.ds((i - 4) * H, H)], raw_r, raw_sem.at[0, i - 4], raw_sem.at[1, i - 4], partner)
+
+    def near_x(peers, same):
+        if len(peers) == 3:
+            return peers[2:] if same else peers[:2]
+        return [peer for k, peer in enumerate(peers) if (k % 4 >= 2) == same]
+
+    def reply_send(i, packed, target, same):
+        @pl.when(is_outer == 0)
+        def _():
+            for peer in near_x(across, same) + near_x(beside, same) + ([partner] if same else []):
+                block_to(i, packed, target, peer, g, own_s).start()
+        for peer in near_x(level, same):
+            block_to(i, packed, target, peer, g, own_s).start()
+
+    def reply(i, table, value, packed, target):
+        answer(table, value, packed)
+        target[pl.ds(g, 1)] = packed[pl.ds(g, 1)]
+
+        @pl.when(is_outer == 1)
+        def _():
+            if i == 5:
+                pl.semaphore_wait(taken, 1)
+            lowct[:, (i - 4) * H:(i - 3) * H] = value
+            raw_copy(i).start()
+
+    def relay_send(i, packed, target, same):
+        @pl.when(is_outer == 0)
+        def _():
+            for peer in near_x(across, same) + near_x(level, same):
+                block_to(i, packed, target, peer, partner, relay_s).start()
+
+    def relay(i, targets, packed, target):
+        @pl.when(is_outer == 0)
+        def _():
+            raw_copy(i).wait_recv()
+            answer(owner_table(targets, partner, sz), raw_r[...], packed)
+            if i == 4:
+                pl.semaphore_signal(taken, inc=1, device_id=(partner, t), device_id_type=MESH)
+            target[pl.ds(partner, 1)] = packed[pl.ds(g, 1)]
+
+    def replied(i, target):
+        def wait(src):
+            rcopy(target.at[src], target.at[src], own_s.at[i - 4, src], a2a_r.at[i, src], src).wait_recv()
+        for src in level + across + beside:
+            wait(src)
+
+        @pl.when(is_outer == 1)
+        def _():
+            wait(partner)
+
+    def reply_settle(i, packed, passed, target):
+        for peer in level:
+            block_to(i, packed, target, peer, g, own_s).wait_send()
+
+        @pl.when(is_outer == 0)
+        def _():
+            for peer in across + beside + [partner]:
+                block_to(i, packed, target, peer, g, own_s).wait_send()
+            for peer in across + level:
+                block_to(i, passed, target, peer, partner, relay_s).wait_send()
 
     def pack(table, source, target):
         for k in range(2):
@@ -373,34 +457,32 @@
             part = dot_nn(table[k * n:(k + 1) * n, :], source[...]).astype(BF)
             target[k * (dp // 2):(k + 1) * (dp // 2)] = part.reshape(dp // 2, sz.cap, H)
 
-    p_in[...] = send_table(dest, g, sz)
+    p_own[...] = send_table(dest, g, sz)
     loads[0].wait()
-    pack(p_in, cts.at[0], pk_in)
+    pack(p_own, lowct.at[:, pl.ds(0, H)], pk_in)
     pl.semaphore_wait(barrier, dp)
-    rows_away = exchange(0, pk_in, rc_in)
+    rows_away = exchange(0, pk_in, rc_in, parts[0]) + exchange(1, pk_in, rc_in, parts[1])
+    rc_in[pl.ds(g, 1)] = pk_in[pl.ds(g, 1)]
     for load in loads[2:]:
         load.start()
-    p_bk[...] = send_table(back, g, sz)
+    p_own[...] = send_table(back, g, sz)
     loads[1].wait()
-    pack(p_bk, cts.at[1], pk_ct)
-    grads_away = exchange(1, pk_ct, rc_ct)
+    pack(p_own, lowct.at[:, pl.ds(H, H)], pk_ct)
+    rc_ct[pl.ds(g, 1)] = pk_ct[pl.ds(g, 1)]
     q_in[...] = owner_table(dest, g, sz)
     q_bk[...] = owner_table(back, g, sz)
 
-    def forward(i, arr, dst, src):
-        arrived(i, arr, src)
-        return rcopy(arr.at[src], dst.at[src], fw_s.at[i, src], fw_r.at[i, src], g, o)
-
-    def own_forward(i, arr, dst):
-        go(rcopy(arr.at[g], dst.at[g], fw_s.at[i, g], fw_r.at[i, g], g, o))
-
-    own_forward(0, rc_in, ry_in)
-    row_forwards = [rcopy(rc_in.at[src], ry_in.at[src], fw_s.at[0, src], fw_r.at[0, src], g, o) for src in far]
-    sent.extend(row_forwards)
-
-    def forward_rows(k):
-        arrived(0, rc_in, far[k])
-        row_forwards[k].start()
+    def unpack(i, table, source, full, part):
+        at = parts[part]
+        arrived(2 * i + part, source, at)
+        n = at.size
+        full[pl.ds(t, 1), :, at] = dot_nn(table[...], source[:, :, at].reshape(sz.slots, n)).astype(BF)[None]
+        go(rcopy(full.at[t, :, at], full.at[t, :, at], fw_s.at[i, part], fw_r.at[i, part], g, o))
+
+    def other_half(i, full):
+        for part in range(2):
+            at = parts[part]
+            rcopy(full.at[o, :, at], full.at[o, :, at], fw_s.at[i, part], fw_r.at[i, part], g, o).wait_recv()
 
     def take_apart(stage, sems):
         n = W // 128
@@ -419,17 +501,13 @@
                 win[k * 128:(k + 1) * 128, C + m:C + m + 256] = both[128:]
             if k + 4 < n:
                 fetch[k + 4].start()
-            if k < dp - 1:
-                forward_rows(k)
 
     pl.run_scoped(take_apart, pltpu.VMEM((4, 128, 2, C), BF), pltpu.SemaphoreType.DMA((4,)))
-    for k in range(W // 128, dp - 1):
-        forward_rows(k)
-    own_forward(1, rc_ct, ry_ct)
-    hid[pl.ds(t, 1)] = dot_nn(q_in[...], rc_in[...].reshape(sz.slots, H)).astype(BF)[None]
-    for d in range(dp):
-        rcopy(ry_in.at[d], ry_in.at[d], fw_s.at[0, d], fw_r.at[0, d], g, o).wait_recv()
-    hid[pl.ds(o, 1)] = dot_nn(q_in[...], ry_in[...].reshape(sz.slots, H)).astype(BF)[None]
+    grads_away = exchange(2, pk_ct, rc_ct, parts[0])
+    unpack(0, q_in, rc_in, hid, 0)
+    grads_away += exchange(3, pk_ct, rc_ct, parts[1])
+    unpack(0, q_in, rc_in, hid, 1)
+    other_half(0, hid)
 
     total = jnp.zeros((R, 128), F32)
     for k in range(W // 128):
@@ -439,7 +517,7 @@
     scale[...] = jnp.broadcast_to(norm_scale, (R, 128))
     for k in range(W // 128):
         v = hid[k // (H // 128), :, (k % (H // 128)) * 128:(k % (H // 128)) * 128 + 128].astype(F32)
-        normed[:, k * 128:(k + 1) * 128] = (v * scale[...] * gain_n[:, k * 128:(k + 1) * 128]).astype(BF)
+        normed[:, k * 128:(k + 1) * 128] = (v * scale[...] * gain_n[k:k + 1, :]).astype(BF)
 
     def quarters(source):
         for qq in range(4):
@@ -455,11 +533,37 @@
         dst[0:1] = perm[pl.ds(q, 1)]
         return copies
 
-    def turn_quarter(i, dst, turned):
+    def turn_quarter(dst, turned):
         for rel, peer in ((1, sib), (2, xp), (3, diag)):
-            rcopy(dst.at[rel], dst.at[rel], xq_s.at[i, rel - 1], xq_r.at[i, rel - 1], peer).wait_recv()
+            rcopy(dst.at[rel], dst.at[rel], xq_s.at[0, rel - 1], xq_r.at[0, rel - 1], peer).wait_recv()
         for rel in range(4):
             turned[:, rel * R:(rel + 1) * R] = jnp.transpose(dst[rel].astype(F32)).astype(BF)
+
+    def fold_half(which, place):
+        value = cts[pl.ds(which, 1)][0]
+        for qq in range(4):
+            cut = jnp.concatenate(
+                [value[:, sz.share * (4 * zz + qq):sz.share * (4 * zz + qq + 1)] for zz in range(sz.nz // 2)], axis=1)
+            cut = jnp.where(iota(cut.shape, 0) < length[0, 0], cut.astype(F32), 0.0).astype(BF)
+            perm[qq, place * (R // 2):(place + 1) * (R // 2)] = jnp.concatenate([cut[:R // 2], cut[R // 2:]], axis=1)
+
+    def fold_copy(sem, quarter, place, half, rel, peer, to):
+        return rcopy(perm.at[quarter, pl.ds(place * (R // 2), R // 2)], xE.at[half, rel], xq_s.at[1, sem], xq_r.at[1, sem], peer, to)
+
+    def fold_pass(rel, half):
+        return rcopy(xE.at[half, rel], xE.at[half, rel], xq_s.at[1, 2 + rel], xq_r.at[1, 2 + rel], g, o)
+
+    def turn_folds():
+        fold_copy(0, 0, 0, t, 1, sib, t).wait_recv()
+        fold_copy(3, 0, 0, o, 1, sib, t).wait_recv()
+        for rel in (2, 3):
+            fold_pass(rel, o).wait_recv()
+        n = sz.quarter // 2
+        for half in range(2):
+            for rel in range(4):
+                flat = jnp.transpose(xE[half, rel].astype(F32)).astype(BF)
+                tE[half * n:(half + 1) * n, rel * R:rel * R + R // 2] = flat[:n]
+                tE[half * n:(half + 1) * n, rel * R + R // 2:(rel + 1) * R] = flat[n:]
 
     quarters(normed)
     quarter_away = send_quarter(0, xA)
@@ -487,7 +591,6 @@
         wr[:, cut] = (conv * sg).astype(BF)
     written, readout = wr[:, :S], wr[:, S:]
     inter[...] = dot_nt(readout, written)
-    interT[...] = dot_nt(written, readout)
     stepsig[...] = sigmoid(step_in) * live
     heads_live = jnp.where(lane < sz.heads, live, 0.0)
     step = (jnp.maximum(step_in, 0.0) + jnp.log1p(jnp.exp(-jnp.abs(step_in)))) * heads_live
@@ -511,46 +614,79 @@
         rcopy(yb.at[2, :, at], yb.at[2, :, at], quad_s.at[i, 1], quad_r.at[i, 1], xp).wait_recv()
         go(rcopy(yb.at[2, :, at], yb.at[3, :, at], quad_s.at[i, 2], quad_r.at[i, 2], sib))
 
-    def z_peer(level):
-        bit = (z // 2 ** level) % 2
-        return bit, g + (1 - 2 * bit) * 4 * 2 ** level
-
-    bases = []
-    at0 = 0
-    for level in range(sz.levels):
-        bases.append(at0)
-        at0 += sz.nz // 2 ** (level + 1)
-    landing = [r0, rl]
-
-    def z_send(i, level):
-        bit, peer = z_peer(level)
+    def z_copy(i, k):
         at = cols_of(i)
-        for k in range(sz.nz // 2 ** (level + 1)):
-            low = z % 2 ** level
-            block = (2 * k + 1 - bit) * 2 ** level + low
-            go(rcopy(pb.at[block, :, at], landing[level].at[k, :, at], z_s.at[i, bases[level] + k],
-                     z_r.at[i, bases[level] + k], peer))
-
-    def z_add(i, level):
-        bit, peer = z_peer(level)
+        column = g % 4
+        if k < 3:
+            block, slot, peer = (zi, fi, fo)[k], r0.at[k], zi
+        elif k < 5:
+            block, slot, peer = (fi, fo)[k - 3], r1.at[k - 3], fi
+        else:
+            block, slot, peer = zo, r0.at[0], zo
+        return rcopy(pb.at[block, :, at], slot.at[:, at], z_s.at[i, k], z_r.at[i, k], peer * 4 + column)
+
+    def z_wait(i, k):
         at = cols_of(i)
+        slot = r0.at[k] if k < 3 else r1.at[k - 3] if k < 5 else r0.at[0]
+        rcopy(slot.at[:, at], slot.at[:, at], z_s.at[i, k], z_r.at[i, k], g + 4 - 8 * (z // 3)).wait_recv()
+
+    def each_tile(i, block, landed, keep):
         start, size = sz.chunks[i]
-        for k in range(sz.nz // 2 ** (level + 1)):
-            low = z % 2 ** level
-            block = (2 * k + bit) * 2 ** level + low
-            sem = bases[level] + k
-            rcopy(landing[level].at[k, :, at], landing[level].at[k, :, at], z_s.at[i, sem], z_r.at[i, sem], peer).wait_recv()
-            for n in range(0, size, 128):
-                cut = slice(start + n, start + n + 128)
-                value = pb[pl.ds(block, 1), :, cut].astype(F32)[0] + landing[level][k, :, cut].astype(F32)
-                if level + 1 < sz.levels:
-                    pb[pl.ds(block, 1), :, cut] = value.astype(BF)[None]
-                elif start + n < C:
-                    proj_out[:, cut] = value
-                elif start + n < 3 * C:
-                    inner_out[:, start + n - C:start + n - C + 128] = value
-                else:
-                    extra_out[:, start + n - 3 * C:start + n - 3 * C + 128] = value
+        for n in range(0, size, 128):
+            cut = slice(start + n, start + n + 128)
+            value = pb[pl.ds(block, 1), :, cut].astype(F32)[0] + landed[:, cut].astype(F32)
+            if keep:
+                pb[pl.ds(block, 1), :, cut] = value.astype(BF)[None]
+            elif start + n < C:
+                proj_out[:, cut] = value
+            elif start + n < 3 * C:
+                inner_out[:, start + n - C:start + n - C + 128] = value
+            else:
+                extra_out[:, start + n - 3 * C:start + n - 3 * C + 128] = value
+
+    def z_first(i):
+        @pl.when(is_outer == 1)
+        def _():
+            for k in range(3):
+                z_copy(i, 2 - k).start()
+
+    def z_second(i):
+        @pl.when(is_outer == 0)
+        def _():
+            for k in (2, 1):
+                z_wait(i, k)
+                each_tile(i, (zi, fi, fo)[k], r0.at[k], True)
+                z_copy(i, 2 + k).start()
+            z_wait(i, 0)
+            each_tile(i, zi, r0.at[0], True)
+
+    def z_third(i):
+        @pl.when(is_outer == 0)
+        def _():
+            z_wait(i, 4)
+            each_tile(i, zo, r1.at[1], True)
+            z_copy(i, 5).start()
+            z_wait(i, 3)
+            each_tile(i, zi, r1.at[0], False)
+
+    def z_fourth(i):
+        @pl.when(is_outer == 1)
+        def _():
+            z_wait(i, 5)
+            each_tile(i, zo, r0.at[0], False)
+
+    def z_settle():
+        @pl.when(is_outer == 1)
+        def _():
+            for i in range(len(sz.chunks)):
+                for k in range(3):
+                    z_copy(i, k).wait_send()
+
+        @pl.when(is_outer == 0)
+        def _():
+            for i in range(len(sz.chunks)):
+                for k in range(3, 6):
+                    z_copy(i, k).wait_send()
 
     def partial_sum(i, turned):
         at = cols_of(i)
@@ -565,7 +701,7 @@
             pb[:, :, at] = part.astype(BF).reshape(sz.nz, sz.share, n)
             return carry
         lax.fori_loop(0, size // n, body, 0)
-        z_send(i, 0)
+        z_first(i)
 
     def remainder(gr, xr, xa, xs, mx, ng):
         def project(dst, base):
@@ -578,11 +714,7 @@
         project(xr, C)
         project(gr, 0)
 
-        def send_ct(first, last):
-            for src in far[first:last]:
-                go(forward(1, rc_ct, ry_ct, src))
-
-        send_ct(0, 7)
+        unpack(1, q_bk, rc_ct, cts, 0)
 
         def lanes(p):
             return pl.ds(pl.multiple_of(p * 128, 128), 128)
@@ -605,7 +737,7 @@
             at = lanes(p)
             lane = iota((R, 128), 1)
             raw = xr[:, at]
-            conv = bias_x[:, at] + tap_x[0:1, at] * raw
+            conv = bias_x[pl.ds(p, 1), :] + tap_x[0:1, at] * raw
             for tap in range(1, 4):
                 conv = conv + tap_x[tap:tap + 1, at] * rows_down(raw, tap)
             sg = sigmoid(conv)
@@ -632,10 +764,7 @@
                 acc1[cut] += gated * gated
             return carry
 
-        step4 = NT_ // 4
-        for k in range(4):
-            lax.fori_loop(k * step4, (k + 1) * step4, scan, 0)
-            send_ct(7 + k, 8 + k)
+        lax.fori_loop(0, NT_, scan, 0)
 
         whole = float(2 * C)
 
@@ -647,21 +776,35 @@
             both = jnp.concatenate([stat_s[i] + stat_r[i], jnp.zeros((120, R), F32)], axis=0)
             return pick(jnp.transpose(both), lane, 0)
 
-        total_over_sides(0, acc1[...]).wait_recv()
+        squares = total_over_sides(0, acc1[...])
+        unpack(1, q_bk, rc_ct, cts, 1)
+        turn_quarter(xA, tA)
+        settle(quarter_away)
+        fold_half(t, 0)
+        for rel, peer in ((2, xp), (3, diag)):
+            go(fold_copy(rel - 1, peer % 4, 0, t, rel, peer, t))
+        squares.wait_recv()
         gate_scale = lax.rsqrt(total_here(0) / whole + EPSILON)
         acc1[...] = jnp.broadcast_to(gate_scale, (R, 128))
 
         def gate_forward(p, carry):
             at = lanes(p)
             gate = gr[:, at]
-            yb[0, :, at] = (mx[:, at] * (gate * sigmoid(gate)) * acc1[...] * gain_g[:, at]).astype(BF)
+            yb[0, :, at] = (mx[:, at] * (gate * sigmoid(gate)) * acc1[...] * gain_g[pl.ds(p, 1), :]).astype(BF)
             return carry
         lax.fori_loop(0, NT_, gate_forward, 0)
-        turn_quarter(0, xA, tA)
         quad_send(0)
+
+        other_half(1, cts)
+        for k in range(W // 128):
+            v = cts[k // (H // 128), :, (k % (H // 128)) * 128:(k % (H // 128)) * 128 + 128].astype(F32)
+            lowct[:, k * 128:(k + 1) * 128] = (v * live).astype(BF)
+        fold_half(o, 1)
+        xE[t, 0] = perm[q, :R // 2]
+        xE[o, 0] = perm[q, R // 2:]
+        go(fold_copy(0, sib % 4, 0, t, 1, sib, t))
+        go(fold_copy(3, sib % 4, 1, o, 1, sib, t))
         quad_send(1)
-
-        send_ct(11, dp - 1)
         loads[3].wait()
 
         def out_half(side, dst, cast):
@@ -670,14 +813,6 @@
                 dst[:, pl.ds(pl.multiple_of(n * 256, 256), 256)] = dot_nn(yb[0, :, :C], wout[:, at]).astype(cast)
                 return carry
             lax.fori_loop(0, H // 256, body, 0)
-        out_half(o, half_s.at[0], BF)
-        cts[pl.ds(t, 1)] = dot_nn(q_bk[...], rc_ct[...].reshape(sz.slots, H)).astype(BF)[None]
-        for d in range(dp):
-            rcopy(ry_ct.at[d], ry_ct.at[d], fw_s.at[1, d], fw_r.at[1, d], g, o).wait_recv()
-        cts[pl.ds(o, 1)] = dot_nn(q_bk[...], ry_ct[...].reshape(sz.slots, H)).astype(BF)[None]
-        for k in range(W // 128):
-            v = cts[k // (H // 128), :, (k % (H // 128)) * 128:(k % (H // 128)) * 128 + 128].astype(F32)
-            lowct[:, k * 128:(k + 1) * 128] = (v * live).astype(BF)
 
         def back_project(n, carry):
             at = pl.ds(pl.multiple_of(n * 256, 256), 256)
@@ -685,15 +820,17 @@
             for k in range(2):
                 here = pl.ds(pl.multiple_of(n * 256 + k * 128, 128), 128)
                 gate = gr[:, here]
-                acc2[...] += mx[:, here] * (gate * sigmoid(gate)) * (gain_g[:, here] * ng[:, here])
+                acc2[...] += mx[:, here] * (gate * sigmoid(gate)) * (gain_g[pl.ds(2 * n + k, 1), :] * ng[:, here])
             return carry
         lax.fori_loop(0, C // 256, back_project, 0)
         crossed = total_over_sides(1, acc2[...])
-        settle(quarter_away)
-        quarters(lowct)
-        sent.extend(send_quarter(1, xE))
+        for rel in (2, 3):
+            fold_copy(rel - 1, 0, 0, t, rel, xp, t).wait_recv()
+            go(fold_pass(rel, t))
+        out_half(o, half_s, BF)
+        branch_away = rcopy(half_s, half_r, y_s.at[2], y_r.at[2], g, o)
+        branch_away.start()
         crossed.wait_recv()
-        go(rcopy(half_s.at[0], half_r.at[0], y_s.at[2], y_r.at[2], g, o))
         acc2[...] = acc1[...] * acc1[...] * acc1[...] * (total_here(1) / whole)
 
         def gate_back(p, carry):
@@ -702,7 +839,7 @@
             sg = sigmoid(gate)
             act = gate * sg
             gated = mixed * act
-            gated_grad = acc1[...] * (gain_g[:, at] * grad) - gated * acc2[...]
+            gated_grad = acc1[...] * (gain_g[pl.ds(p, 1), :] * grad) - gated * acc2[...]
             sms[0, 5:6, at] = jnp.sum(grad * gated * acc1[...], axis=0, keepdims=True)
             mixed_grad = gated_grad * act
             ng[:, at] = mixed_grad
@@ -715,6 +852,7 @@
         quad_send(3)
         out_half(t, gr, F32)
 
+        inter[...] = dot_nt(written, readout)
         igrad[...] = jnp.zeros_like(igrad)
         sgr[...] = jnp.zeros_like(sgr)
         rgr[...] = jnp.zeros_like(rgr)
@@ -734,7 +872,7 @@
                 skip = 128 * ((b * B) // 128)
                 cut = slice(b * B, (b + 1) * B)
                 causal = iota((B, R - skip), 1) + skip >= iota((B, R - skip), 0) + b * B
-                turned = interT[cut, skip:]
+                turned = inter[cut, skip:]
                 piece = jnp.zeros((B, 128), F32)
                 total = igrad[cut, skip:]
                 for k in range(2):
@@ -773,30 +911,24 @@
             yb[0, :, pl.ds(pl.multiple_of(2 * C + p * 128, 128), 128)] = raw_grad.astype(BF)
             return carry
 
-        lax.fori_loop(0, NT_ // 2, scan_back, 0)
+        quad_pass(0)
+        lax.fori_loop(0, NT_ // 4, scan_back, 0)
+        turn_folds()
+        partial_sum(0, tE)
+        lax.fori_loop(NT_ // 4, NT_ // 2, scan_back, 0)
         quad_send(4)
-        turn_quarter(1, xE, tE)
-        quad_pass(0)
-        quad_pass(1)
-        partial_sum(0, tE)
-
-        rcopy(half_r.at[0], half_r.at[0], y_s.at[2], y_r.at[2], g, o).wait_recv()
-
-        def answer(table, value, dst):
-            for k in range(2):
-                n = sz.slots // 2
-                part = dot_tn(table[:, k * n:(k + 1) * n], value).astype(BF)
-                dst[k * (dp // 2):(k + 1) * (dp // 2)] = part.reshape(dp // 2, sz.cap, H)
+
+        rcopy(half_r, half_r, y_s.at[2], y_r.at[2], g, o).wait_recv()
 
         pieces = []
         mine = hid[pl.ds(t, 1)][0]
         for k in range(H // 128):
             cut = slice(k * 128, (k + 1) * 128)
-            branch = gr[:, cut] + half_r[0, :, cut].astype(F32)
+            branch = gr[:, cut] + half_r[:, cut].astype(F32)
             pieces.append((mine[:, cut].astype(F32) + live * branch).astype(BF))
         settle(rows_away)
-        answer(q_bk, jnp.concatenate(pieces, axis=1), pk_in)
-        sent.extend(exchange(2, pk_in, gn_o))
+        reply(4, q_bk, jnp.concatenate(pieces, axis=1), pk_in, gn_o)
+        reply_send(4, pk_in, gn_o, True)
 
         lax.fori_loop(NT_ // 2, NT_, scan_back, 0)
         quad_send(5)
@@ -809,7 +941,8 @@
         yb[0, :, 3 * C + 2 * S:] = step_grad.astype(BF)
         sms[0, 7:8, 10 * S:10 * S + 128] = jnp.sum(step_grad, axis=0, keepdims=True)
         sms[0, 7:8, 10 * S + 128:10 * S + 256] = jnp.sum(rgr[...] * dtv[...], axis=0, keepdims=True) * rate
-        partial_sum(1, tE)
+        quad_pass(1)
+        z_second(0)
         rcopy(st_r, st_r, y_s.at[3], y_r.at[3], g, o).wait_recv()
         for k in range(2):
             cut = slice(k * S, (k + 1) * S)
@@ -824,6 +957,7 @@
                 sms[0, 7:8, tap * 2 * S + k * S:tap * 2 * S + (k + 1) * S] = jnp.sum(up * raw, axis=0, keepdims=True)
             yb[0, :, 3 * C + k * S:3 * C + (k + 1) * S] = raw_grad.astype(BF)
         quad_send(6)
+        reply_send(4, pk_in, gn_o, False)
 
         hops = [2 ** k for k in range(2, dp.bit_length() - 1)] + [1, 2]
 
@@ -854,21 +988,23 @@
                     cut = slice(k * 128, (k + 1) * 128)
                     here = pl.ds(pl.multiple_of(n * 256 + k * 128, 128), 128)
                     there = pl.ds(pl.multiple_of(side * H + n * 256 + k * 128, 128), 128)
-                    acc1[...] += hid[pl.ds(side, 1), :, here][0].astype(F32) * (gain_n[:, there] * value[:, cut])
+                    acc1[...] += hid[pl.ds(side, 1), :, here][0].astype(F32) * (gain_n[pl.ds(side * (H // 128) + 2 * n + k, 1), :] * value[:, cut])
                 dst[:, pl.ds(pl.multiple_of(n * 256, 256), 256)] = value.astype(cast)
                 return carry
             lax.fori_loop(0, H // 256, body, 0)
-        normed_grad(o, half_s.at[1], BF)
-        go(rcopy(half_s.at[1], half_r.at[1], y_s.at[4], y_r.at[4], g, o))
+        branch_away.wait_send()
+        normed_grad(o, half_s, BF)
+        go(rcopy(half_s, half_r, y_s.at[4], y_r.at[4], g, o))
         normed_grad(t, gr, F32)
         summed_rows = total_over_sides(2, acc1[...])
-        z_add(0, 0)
-        z_send(0, 1)
+        partial_sum(1, tE)
+        relay(4, back, rc_ct, gn_o)
+        relay_send(4, rc_ct, gn_o, True)
+        relay_send(4, rc_ct, gn_o, False)
         quad_pass(2)
         partial_sum(2, tA)
-        small_end(0)
-
-        rcopy(half_r.at[1], half_r.at[1], y_s.at[4], y_r.at[4], g, o).wait_recv()
+
+        rcopy(half_r, half_r, y_s.at[4], y_r.at[4], g, o).wait_recv()
         summed_rows.wait_recv()
         pull = total_here(2) / W * (scale[...] * scale[...] * scale[...])
         pieces = []
@@ -878,53 +1014,60 @@
         for k in range(H // 128):
             cut = slice(k * 128, (k + 1) * 128)
             there = pl.ds(pl.multiple_of(t * H + k * 128, 128), 128)
-            value = gr[:, cut] + half_r[1, :, cut].astype(F32)
+            value = gr[:, cut] + half_r[:, cut].astype(F32)
             rows_here = mine[:, cut].astype(F32)
             gall[pl.ds(g, 1), k:k + 1, :] = jnp.sum(value * rows_here * scale[...], axis=0, keepdims=True)[None]
-            pieces.append((scale[...] * (gain_n[:, there] * value) - rows_here * pull
+            pieces.append((scale[...] * (gain_n[pl.ds(t * (H // 128) + k, 1), :] * value) - rows_here * pull
                            + mine_ct[:, cut].astype(F32)).astype(BF))
         settle(grads_away)
-        answer(q_in, jnp.concatenate(pieces, axis=1), pk_ct)
+        reply(5, q_in, jnp.concatenate(pieces, axis=1), pk_ct, gn_g)
+        reply_send(5, pk_ct, gn_g, True)
+        reply_send(5, pk_ct, gn_g, False)
         for peer in far:
             go(rcopy(gall.at[g], gall.at[g], gg_s.at[peer], gg_r.at[g], peer))
-        sent.extend(exchange(3, pk_ct, gn_g))
-
-        def reduce_further(i):
-            z_add(i, 0)
-            z_send(i, 1)
-
-        reduce_further(1)
+
+        small_end(0)
+        z_second(1)
         quad_pass(3)
         partial_sum(3, tA)
-        reduce_further(2)
-        small_end(1)
+        z_second(2)
+        z_third(0)
+        relay(5, dest, rc_in, gn_g)
+        relay_send(5, rc_in, gn_g, True)
+        relay_send(5, rc_in, gn_g, False)
+        z_third(1)
         quad_pass(4)
         partial_sum(4, tA)
-        reduce_further(3)
-        small_end(2)
-        z_add(0, 1)
-        z_add(1, 1)
+        small_end(1)
+        z_third(2)
+        z_second(3)
         quad_pass(5)
         partial_sum(5, tA)
-        reduce_further(4)
+        z_second(4)
         quad_pass(6)
+        small_end(2)
+        z_third(3)
         partial_sum(6, tA)
-        z_add(2, 1)
-        z_add(3, 1)
-
-        def give(i, value, stage, dst):
-            n = R // sz.cap
-            stage[:n] = value.astype(BF).reshape(n, sz.cap, H)
-            copies = [pltpu.make_async_copy(stage.at[k], dst.at[pl.ds(k * sz.cap, sz.cap)], o_s.at[i, k]) for k in range(n)]
-            for copy in copies:
-                copy.start()
-            return copies
-
-        for src in far:
-            arrived(2, gn_o, src)
-        stores = give(0, dot_tn(p_bk[...], gn_o[...].reshape(sz.slots, H)), ry_in, out_rows)
-        reduce_further(5)
-        reduce_further(6)
+        z_third(4)
+        z_second(5)
+        z_second(6)
+
+        def give(i, value, dst):
+            lowct[:, i * H:(i + 1) * H] = value.astype(BF)
+            store = pltpu.make_async_copy(lowct.at[:, pl.ds(i * H, H)], dst, w_s.at[i])
+            store.start()
+            return store
+
+        replied(4, gn_o)
+
+        @pl.when(is_outer == 1)
+        def _():
+            raw_copy(4).wait_send()
+            raw_copy(5).wait_send()
+        stores = [give(0, dot_tn(p_own[...], gn_o[...].reshape(sz.slots, H)), out_rows)]
+        p_own[...] = send_table(dest, g, sz)
+        for i in range(4):
+            z_fourth(i)
         small_end(3)
         for src in far:
             rcopy(gall.at[src], gall.at[src], gg_s.at[src], gg_r.at[src], src).wait_recv()
@@ -933,16 +1076,19 @@
             summed = summed + gall[d]
         gsum[pl.ds(t, 1)] = summed[None]
         go(rcopy(gsum.at[t], gsum.at[t], y_s.at[5], y_r.at[5], g, o))
-        for src in far:
-            arrived(3, gn_g, src)
-        stores += give(1, dot_tn(p_in[...], gn_g[...].reshape(sz.slots, H)), ry_ct, out_grads)
-        z_add(4, 1)
-        z_add(5, 1)
-        z_add(6, 1)
+        replied(5, gn_g)
+        stores.append(give(1, dot_tn(p_own[...], gn_g[...].reshape(sz.slots, H)), out_grads))
+        z_third(5)
+        z_third(6)
+        for i in range(4, 7):
+            z_fourth(i)
         rcopy(gsum.at[o], gsum.at[o], y_s.at[5], y_r.at[5], g, o).wait_recv()
         gain_out[...] = gsum[...]
         for copy in sent:
             copy.wait_send()
+        z_settle()
+        reply_settle(4, pk_in, rc_ct, gn_o)
+        reply_settle(5, pk_ct, rc_in, gn_g)
         for store in stores:
             store.wait()
 
@@ -957,9 +1103,9 @@
     o_grads[...] = grads[...]
     o_inner[:, 0, :] = inner[:, :C]
     o_inner[:, 1, :] = inner[:, C:]
-    o_proj[...] = jnp.transpose(proj[...])
+    o_proj[...] = proj[...]
     o_state[...] = extra[:, :2 * S]
-    o_step[...] = extra[:, 2 * S:2 * S + sz.heads]
+    o_step[...] = jnp.transpose(extra[:, 2 * S:])[:sz.heads]
     o_tap_x[...] = small[0:4, :]
     o_bias_x[...] = small[4, :]
     o_gate[...] = small[5, :]
@@ -993,20 +1139,21 @@
     nch = len(sz.chunks)
     scratch = [
         V((W, 2 * C), BF), V((C, W), BF), V((W, 2 * S), BF), V((128, W), BF), V((8, 128), F32),
-        *[packed] * 8,
-        V((sz.slots, R), BF), V((sz.slots, R), BF), V((R, sz.slots), BF), V((R, sz.slots), BF),
+        *[packed] * 6,
+        V((sz.slots, R), BF), V((R, sz.slots), BF), V((R, sz.slots), BF),
         V((2, R, H), BF), V((2, R, H), BF), V((R, W), BF), V((R, W), BF),
-        V((4, R, sz.quarter), BF), V((4, R, sz.quarter), BF), V((4, R, sz.quarter), BF),
+        V((4, R, sz.quarter), BF), V((4, R, sz.quarter), BF), V((2, 4, R // 2, sz.quarter), BF),
         V((sz.quarter, 4 * R), BF), V((sz.quarter, 4 * R), BF),
-        V((4, R, sz.cols), BF), V((sz.nz, sz.share, sz.cols), BF), V((2, sz.share, sz.cols), BF), V((1, sz.share, sz.cols), BF),
-        V((R, R), F32), V((R, R), F32), V((R, R), F32), V((2, R, R), BF),
+        V((4, R, sz.cols), BF), V((sz.nz, sz.share, sz.cols), BF), V((3, sz.share, sz.cols), BF), V((2, sz.share, sz.cols), BF),
+        V((R, R), F32), V((R, R), F32), V((2, R, R), BF),
         V((R, 2 * S), F32), V((R, 2 * S), F32), V((R, 2 * S), BF), V((R, 128), F32), V((R, 128), F32), V((128, R), F32),
         V((R, 128), F32), V((R, 128), F32), V((R, 128), F32), V((R, 128), F32), V((R, 128), F32), V((R, 128), F32),
-        V((3, 8, R), F32), V((3, 8, R), F32), V((2, R, H), BF), V((2, R, H), BF),
+        V((3, 8, R), F32), V((3, 8, R), F32), V((R, H), BF), V((R, H), BF), V((R, H), BF),
         V((R, 2 * S), BF), V((R, 2 * S), BF),
         V((4, 8, C), F32), V((4, 8, C), F32), V((dp, 8, 128), F32), V((2, 8, 128), F32),
-        D((4, dp)), D((4, dp)), D((2, dp)), D((2, dp)), D((nch, 3)), D((nch, 3)), D((2, 3)), D((2, 3)),
-        D((nch, sz.nz - 1)), D((nch, sz.nz - 1)), D((6,)), D((6,)), D((dp,)), D((dp,)), D((4,)), D((4,)), D((4,)), D((2, dp)),
+        D((6, dp)), D((6, dp)), D((2, 2)), D((2, 2)), D((nch, 3)), D((nch, 3)), D((2, 6)), D((2, 6)),
+        D((nch, 6)), D((nch, 6)), D((6,)), D((6,)), D((dp,)), D((dp,)), D((4,)), D((4,)), D((4,)), D((2, dp)), D((2, dp)), D((2, 2)),
+        pltpu.SemaphoreType.REGULAR,
     ]
     out = jax.ShapeDtypeStruct
     rows_out, grads_out, inner_g, proj_g, extra_g, small, gain = pl.pallas_call(
@@ -1019,18 +1166,19 @@
         compiler_params=pltpu.CompilerParams(collective_id=0, has_side_effects=True, vmem_limit_bytes=66000000),
         name="block",
     )(dest_slot.reshape(-1, 128), return_slot.reshape(-1, 128), lengths, block_in, cotangent, inner_weight, out_weight,
-      state_weight, step_weight.T, conv_inner, conv_inner_bias[None], gate_gain[None], norm_gain[None], skip_gain[None],
+      state_weight, step_weight.T, conv_inner, conv_inner_bias.reshape(-1, 128), gate_gain.reshape(-1, 128), norm_gain.reshape(-1, 128), skip_gain[None],
       conv_state, conv_state_bias[None], step_bias[None], log_rate[None])
-    return pl.pallas_call(
+    results = pl.pallas_call(
         functools.partial(finish_kernel, sz),
         out_shape=(out((R, H), BF), out((R, H), BF), out((sz.share,), F32), out((sz.share, 2, C), F32),
-                   out((sz.share, 2 * S), F32), out((sz.share, sz.heads), F32), out((4, C), F32), out((C,), F32),
+                   out((sz.share, 2 * S), F32), out((sz.heads, sz.share), F32), out((4, C), F32), out((C,), F32),
                    out((4, 2 * S), F32), out((2 * S,), F32), out((sz.heads,), F32), out((sz.heads,), F32),
-                   out((sz.heads,), F32), out((C,), F32), out((C, sz.share), F32)),
+                   out((sz.heads,), F32), out((C,), F32), out((sz.share, C), F32)),
         in_specs=[vm] * 7,
         out_specs=(vm,) * 15,
         name="finish",
     )(rows_out, grads_out, inner_g, proj_g, extra_g, small, gain)
+    return results[:5] + (results[5].T,) + results[6:14] + (results[14].T,)
 
 
 def with_collectives(
@@ -1265,7 +1413,7 @@
     inner, heads, state = args[6].shape[2], args[8].shape[1], args[7].shape[1] // 2
     capacity = 2 * rows // groups
     fits = (
-        groups % 4 == 0 and 16 <= 4 * groups <= 64 and capacity % 16 == 0 and (2 * half // groups) % 16 == 0
+        groups == 16 and capacity % 16 == 0 and (2 * half // groups) % 16 == 0
         and rows == STRETCH and args[2].shape[1] == 1 and inner == 64 * heads and inner == 2 * half
     )
     if fits:

time: 208 us -> 169 us (0.81)
  the two profiles are of different devices: /device:TPU:26 before, /device:TPU:0 now
where the time goes in v4:
time: 169 us
  Pallas kernels  167 us (99%)
    pallas_call x1, Pallas kernels, fused(): pl.pallas_call(functools.partial(block_kernel, sz), out_shape=(out((R, H)...  164 us
    pallas_call x1, Pallas kernels, fused(): pl.pallas_call(functools.partial(finish_kernel, sz), out_shape=(out((R, H...  3.54 us

profile of v4, /device:TPU:0, one launch (start us, length us, event | category | flops | bytes accessed | tf_op | source)
XLA Modules:
  0.0 168.9 jit_solution(15374504074883772099)
XLA Ops:
  1.3 163.9 %block.1 = (bf16[256,768]{1,0:T(8,128)(2,1)}, bf16[256,768]{1,0:T(8,128)(2,1)}, f32[96,3072]{1,0:T(8,128)}, f32[96,1536]{1,0:T(8,128)}, f32[96,384]{1,0:T(8,128)...) custom-call(s32[32,128]{1,0:T(8,128)} %bitcast.13, s32[32,128]{1,0:T(8,128)} %bitcast.14, s32[1,1]{1,0:T(1,128)S(6)} %copy.33.refs_2_, ...), custom_call_target="tpu_custom_call" | custom-call | tf_op jit(solution)/shard_map/block/pallas_call | solution.py:1159
  165.2 3.5 %finish.1 = (bf16[256,768]{1,0:T(8,128)(2,1)}, bf16[256,768]{1,0:T(8,128)(2,1)}, f32[96]{0:T(128)}, f32[96,2,1536]{2,1,0:T(2,128)}, f32[96,256]{1,0:T(8,128)}, /...) custom-call(bf16[256,768]{1,0:T(8,128)(2,1)} %get-tuple-element.37.r, ...), custom_call_target="tpu_custom_call" | custom-call | tf_op jit(solution)/shard_map/finish/pallas_call | solution.py:1171

commit v5 on v4

--- a/solution.py
+++ b/solution.py
@@ -264,7 +264,8 @@
         self.extra = 2 * state + 128
         self.cols = 3 * inner + self.extra
         n = inner // 2
-        self.chunks = [(i * n, n) for i in range(6)] + [(6 * n, self.extra)]
+        sizes = [n // 3 * 2, n // 3 * 4, n, n, n, n, self.extra]
+        self.chunks = [(sum(sizes[:k]), size) for k, size in enumerate(sizes)]
         self.levels = self.nz.bit_length() - 1
 
 
@@ -312,12 +313,12 @@
      pk_in, pk_ct, rc_in, rc_ct, gn_o, gn_g,
      p_own, q_in, q_bk,
      hid, cts, normed, lowct, perm, xA, xE, tA, tE,
-     yb, pb, r0, r1,
+     yb, pb, r0, r1, f_inner, f_proj, f_extra,
      inter, igrad, ptile,
      sraw, sslope, wr, dtv, lac, lar, sgr, rgr, stepsig, acc1, acc2, scale,
      stat_s, stat_r, half_s, half_r, raw_r, st_s, st_r,
      sms, smr, gall, gsum,
-     a2a_s, a2a_r, fw_s, fw_r, quad_s, quad_r, xq_s, xq_r, z_s, z_r, y_s, y_r, gg_s, gg_r, sm_s, sm_r, w_s, own_s, relay_s, raw_sem, taken) = refs
+     a2a_s, a2a_r, fw_s, fw_r, quad_s, quad_r, xq_s, xq_r, z_s, z_r, y_s, y_r, gg_s, gg_r, sm_s, sm_r, w_s, own_s, relay_s, raw_sem, o_s, taken) = refs
     dp, R, H, C = sz.dp, sz.rows, sz.half, sz.inner
     W, NT_ = sz.width, sz.tiles
     g = lax.axis_index("dp")
@@ -364,20 +365,20 @@
     partner = beside_z * 4 + q
     parts = [pl.ds(0, H // 3 * 2), pl.ds(H // 3 * 2, H // 3)]
 
+    def span(ref, n, ss, rs, at=slice(None)):
+        return rcopy(ref.at[pl.ds(0, n), :, at], ref.at[pl.ds(0, n), :, at], ss, rs, partner)
+
     def exchange(i, source, target, at=slice(None)):
-        copies = [
-            rcopy(source.at[peer, :, at], target.at[g, :, at], a2a_s.at[i, peer], a2a_r.at[i, g], peer) for peer in far]
-        for copy in copies:
-            copy.start()
-        return copies
+        for peer in far:
+            rcopy(source.at[peer, :, at], target.at[g, :, at], a2a_s.at[i], a2a_r.at[i], peer).start()
+        return [span(source, dp - 1, a2a_s.at[i], a2a_r.at[i], at)]
 
     def settle(copies):
         for copy in copies:
             copy.wait_send()
 
     def arrived(i, target, at=slice(None)):
-        for src in far:
-            rcopy(target.at[src, :, at], target.at[src, :, at], a2a_s.at[i, src], a2a_r.at[i, src], src).wait_recv()
+        span(target, dp - 1, a2a_s.at[i], a2a_r.at[i], at).wait_recv()
 
     def answer(table, value, dst):
         for k in range(2):
@@ -386,7 +387,7 @@
             dst[k * (dp // 2):(k + 1) * (dp // 2)] = part.reshape(dp // 2, sz.cap, H)
 
     def block_to(i, source, target, peer, owner, sems):
-        return rcopy(source.at[peer], target.at[owner], sems.at[i - 4, peer], a2a_r.at[i, owner], peer)
+        return rcopy(source.at[peer], target.at[owner], sems.at[i - 4], a2a_r.at[i], peer)
 
     def raw_copy(i):
         return rcopy(lowct.at[:, pl.ds((i - 4) * H, H)], raw_r, raw_sem.at[0, i - 4], raw_sem.at[1, i - 4], partner)
@@ -431,25 +432,23 @@
             target[pl.ds(partner, 1)] = packed[pl.ds(g, 1)]
 
     def replied(i, target):
-        def wait(src):
-            rcopy(target.at[src], target.at[src], own_s.at[i - 4, src], a2a_r.at[i, src], src).wait_recv()
-        for src in level + across + beside:
-            wait(src)
-
         @pl.when(is_outer == 1)
         def _():
-            wait(partner)
-
-    def reply_settle(i, packed, passed, target):
-        for peer in level:
-            block_to(i, packed, target, peer, g, own_s).wait_send()
+            span(target, dp - 1, own_s.at[i - 4], a2a_r.at[i]).wait_recv()
 
         @pl.when(is_outer == 0)
         def _():
-            for peer in across + beside + [partner]:
-                block_to(i, packed, target, peer, g, own_s).wait_send()
-            for peer in across + level:
-                block_to(i, passed, target, peer, partner, relay_s).wait_send()
+            span(target, dp - 2, own_s.at[i - 4], a2a_r.at[i]).wait_recv()
+
+    def reply_settle(i, packed):
+        @pl.when(is_outer == 1)
+        def _():
+            span(packed, len(level), own_s.at[i - 4], a2a_r.at[i]).wait_send()
+
+        @pl.when(is_outer == 0)
+        def _():
+            span(packed, dp - 1, own_s.at[i - 4], a2a_r.at[i]).wait_send()
+            span(packed, len(across + level), relay_s.at[i - 4], a2a_r.at[i]).wait_send()
 
     def pack(table, source, target):
         for k in range(2):
@@ -606,13 +605,13 @@
 
     def quad_send(i):
         at = cols_of(i)
-        go(rcopy(yb.at[0, :, at], yb.at[2, :, at], quad_s.at[i, 1], quad_r.at[i, 1], xp))
-        go(rcopy(yb.at[0, :, at], yb.at[1, :, at], quad_s.at[i, 0], quad_r.at[i, 0], sib))
+        rcopy(yb.at[0, :, at], yb.at[2, :, at], quad_s.at[1], quad_r.at[i, 1], xp).start()
+        rcopy(yb.at[0, :, at], yb.at[1, :, at], quad_s.at[0], quad_r.at[i, 0], sib).start()
 
     def quad_pass(i):
         at = cols_of(i)
-        rcopy(yb.at[2, :, at], yb.at[2, :, at], quad_s.at[i, 1], quad_r.at[i, 1], xp).wait_recv()
-        go(rcopy(yb.at[2, :, at], yb.at[3, :, at], quad_s.at[i, 2], quad_r.at[i, 2], sib))
+        rcopy(yb.at[2, :, at], yb.at[2, :, at], quad_s.at[1], quad_r.at[i, 1], xp).wait_recv()
+        rcopy(yb.at[2, :, at], yb.at[3, :, at], quad_s.at[2], quad_r.at[i, 2], sib).start()
 
     def z_copy(i, k):
         at = cols_of(i)
@@ -623,12 +622,12 @@
             block, slot, peer = (fi, fo)[k - 3], r1.at[k - 3], fi
         else:
             block, slot, peer = zo, r0.at[0], zo
-        return rcopy(pb.at[block, :, at], slot.at[:, at], z_s.at[i, k], z_r.at[i, k], peer * 4 + column)
+        return rcopy(pb.at[block, :, at], slot.at[:, at], z_s, z_r.at[i, k], peer * 4 + column)
 
     def z_wait(i, k):
         at = cols_of(i)
         slot = r0.at[k] if k < 3 else r1.at[k - 3] if k < 5 else r0.at[0]
-        rcopy(slot.at[:, at], slot.at[:, at], z_s.at[i, k], z_r.at[i, k], g + 4 - 8 * (z // 3)).wait_recv()
+        rcopy(slot.at[:, at], slot.at[:, at], z_s, z_r.at[i, k], g + 4 - 8 * (z // 3)).wait_recv()
 
     def each_tile(i, block, landed, keep):
         start, size = sz.chunks[i]
@@ -638,11 +637,11 @@
             if keep:
                 pb[pl.ds(block, 1), :, cut] = value.astype(BF)[None]
             elif start + n < C:
-                proj_out[:, cut] = value
+                f_proj[:, cut] = value
             elif start + n < 3 * C:
-                inner_out[:, start + n - C:start + n - C + 128] = value
+                f_inner[:, start + n - C:start + n - C + 128] = value
             else:
-                extra_out[:, start + n - 3 * C:start + n - 3 * C + 128] = value
+                f_extra[:, start + n - 3 * C:start + n - 3 * C + 128] = value
 
     def z_first(i):
         @pl.when(is_outer == 1)
@@ -675,24 +674,30 @@
             z_wait(i, 5)
             each_tile(i, zo, r0.at[0], False)
 
-    def z_settle():
-        @pl.when(is_outer == 1)
-        def _():
-            for i in range(len(sz.chunks)):
-                for k in range(3):
-                    z_copy(i, k).wait_send()
-
-        @pl.when(is_outer == 0)
-        def _():
-            for i in range(len(sz.chunks)):
-                for k in range(3, 6):
-                    z_copy(i, k).wait_send()
+    def write_out(i):
+        start, size = sz.chunks[i]
+        if i < 2:
+            pairs = [(f_proj.at[:, pl.ds(start, size)], proj_out.at[:, pl.ds(start, size)])]
+        elif i < 6:
+            cut = pl.ds(start - C, size)
+            pairs = [(f_inner.at[:, cut], inner_out.at[:, cut])]
+        else:
+            pairs = [(f_extra, extra_out)]
+        copies = [pltpu.make_async_copy(a, b, o_s.at[i]) for a, b in pairs]
+        for copy in copies:
+            copy.start()
+        return copies
+
+    def settle_sums():
+        for k in range(3):
+            rcopy(yb.at[0], yb.at[0], quad_s.at[k], quad_r.at[0, k], sib).wait_send()
+        rcopy(r0, r0, z_s, z_r.at[0, 0], partner).wait_send()
 
     def partial_sum(i, turned):
         at = cols_of(i)
         start, size = sz.chunks[i]
-        rcopy(yb.at[1, :, at], yb.at[1, :, at], quad_s.at[i, 0], quad_r.at[i, 0], sib).wait_recv()
-        rcopy(yb.at[3, :, at], yb.at[3, :, at], quad_s.at[i, 2], quad_r.at[i, 2], sib).wait_recv()
+        rcopy(yb.at[1, :, at], yb.at[1, :, at], quad_s.at[0], quad_r.at[i, 0], sib).wait_recv()
+        rcopy(yb.at[3, :, at], yb.at[3, :, at], quad_s.at[2], quad_r.at[i, 2], sib).wait_recv()
         n = 384 if size % 256 else 256
 
         def body(k, carry):
@@ -851,6 +856,9 @@
         quad_send(2)
         quad_send(3)
         out_half(t, gr, F32)
+        quad_pass(0)
+        turn_folds()
+        partial_sum(0, tE)
 
         inter[...] = dot_nt(written, readout)
         igrad[...] = jnp.zeros_like(igrad)
@@ -911,11 +919,7 @@
             yb[0, :, pl.ds(pl.multiple_of(2 * C + p * 128, 128), 128)] = raw_grad.astype(BF)
             return carry
 
-        quad_pass(0)
-        lax.fori_loop(0, NT_ // 4, scan_back, 0)
-        turn_folds()
-        partial_sum(0, tE)
-        lax.fori_loop(NT_ // 4, NT_ // 2, scan_back, 0)
+        lax.fori_loop(0, NT_ // 2, scan_back, 0)
         quad_send(4)
 
         rcopy(half_r, half_r, y_s.at[2], y_r.at[2], g, o).wait_recv()
@@ -930,6 +934,7 @@
         reply(4, q_bk, jnp.concatenate(pieces, axis=1), pk_in, gn_o)
         reply_send(4, pk_in, gn_o, True)
 
+        quad_pass(1)
         lax.fori_loop(NT_ // 2, NT_, scan_back, 0)
         quad_send(5)
 
@@ -941,7 +946,7 @@
         yb[0, :, 3 * C + 2 * S:] = step_grad.astype(BF)
         sms[0, 7:8, 10 * S:10 * S + 128] = jnp.sum(step_grad, axis=0, keepdims=True)
         sms[0, 7:8, 10 * S + 128:10 * S + 256] = jnp.sum(rgr[...] * dtv[...], axis=0, keepdims=True) * rate
-        quad_pass(1)
+        partial_sum(1, tE)
         z_second(0)
         rcopy(st_r, st_r, y_s.at[3], y_r.at[3], g, o).wait_recv()
         for k in range(2):
@@ -972,7 +977,7 @@
                 sms[i + 1] = sms[i] + smr[i]
                 small_start(i + 1)
             else:
-                small_out[...] = sms[i] + smr[i]
+                smr[0] = sms[i] + smr[i]
         small_start(0)
 
         acc1[...] = jnp.zeros_like(acc1)
@@ -997,7 +1002,6 @@
         go(rcopy(half_s, half_r, y_s.at[4], y_r.at[4], g, o))
         normed_grad(t, gr, F32)
         summed_rows = total_over_sides(2, acc1[...])
-        partial_sum(1, tE)
         relay(4, back, rc_ct, gn_o)
         relay_send(4, rc_ct, gn_o, True)
         relay_send(4, rc_ct, gn_o, False)
@@ -1024,7 +1028,7 @@
         reply_send(5, pk_ct, gn_g, True)
         reply_send(5, pk_ct, gn_g, False)
         for peer in far:
-            go(rcopy(gall.at[g], gall.at[g], gg_s.at[peer], gg_r.at[g], peer))
+            rcopy(gall.at[g], gall.at[g], gg_s, gg_r, peer).start()
 
         small_end(0)
         z_second(1)
@@ -1035,22 +1039,20 @@
         relay(5, dest, rc_in, gn_g)
         relay_send(5, rc_in, gn_g, True)
         relay_send(5, rc_in, gn_g, False)
-        z_third(1)
         quad_pass(4)
         partial_sum(4, tA)
-        small_end(1)
+        z_third(1)
+        quad_pass(5)
+        partial_sum(5, tA)
         z_third(2)
         z_second(3)
-        quad_pass(5)
-        partial_sum(5, tA)
+        quad_pass(6)
+        partial_sum(6, tA)
+        small_end(1)
         z_second(4)
-        quad_pass(6)
         small_end(2)
         z_third(3)
-        partial_sum(6, tA)
-        z_third(4)
         z_second(5)
-        z_second(6)
 
         def give(i, value, dst):
             lowct[:, i * H:(i + 1) * H] = value.astype(BF)
@@ -1068,9 +1070,12 @@
         p_own[...] = send_table(dest, g, sz)
         for i in range(4):
             z_fourth(i)
+            stores += write_out(i)
         small_end(3)
-        for src in far:
-            rcopy(gall.at[src], gall.at[src], gg_s.at[src], gg_r.at[src], src).wait_recv()
+        stores.append(pltpu.make_async_copy(smr.at[0], small_out, o_s.at[7]))
+        stores[-1].start()
+        span(gall, dp - 1, gg_s, gg_r).wait_recv()
+        sent.append(span(gall, dp - 1, gg_s, gg_r))
         summed = gall[0]
         for d in range(1, dp):
             summed = summed + gall[d]
@@ -1078,17 +1083,24 @@
         go(rcopy(gsum.at[t], gsum.at[t], y_s.at[5], y_r.at[5], g, o))
         replied(5, gn_g)
         stores.append(give(1, dot_tn(p_own[...], gn_g[...].reshape(sz.slots, H)), out_grads))
+        z_second(6)
+        z_third(4)
+        z_fourth(4)
+        stores += write_out(4)
         z_third(5)
+        z_fourth(5)
+        stores += write_out(5)
         z_third(6)
-        for i in range(4, 7):
-            z_fourth(i)
+        z_fourth(6)
+        stores += write_out(6)
         rcopy(gsum.at[o], gsum.at[o], y_s.at[5], y_r.at[5], g, o).wait_recv()
-        gain_out[...] = gsum[...]
+        stores.append(pltpu.make_async_copy(gsum, gain_out, o_s.at[8]))
+        stores[-1].start()
         for copy in sent:
             copy.wait_send()
-        z_settle()
-        reply_settle(4, pk_in, rc_ct, gn_o)
-        reply_settle(5, pk_ct, rc_in, gn_g)
+        settle_sums()
+        reply_settle(4, pk_in)
+        reply_settle(5, pk_ct)
         for store in stores:
             store.wait()
 
@@ -1145,14 +1157,15 @@
         V((4, R, sz.quarter), BF), V((4, R, sz.quarter), BF), V((2, 4, R // 2, sz.quarter), BF),
         V((sz.quarter, 4 * R), BF), V((sz.quarter, 4 * R), BF),
         V((4, R, sz.cols), BF), V((sz.nz, sz.share, sz.cols), BF), V((3, sz.share, sz.cols), BF), V((2, sz.share, sz.cols), BF),
+        V((sz.share, 2 * C), F32), V((sz.share, C), F32), V((sz.share, sz.extra), F32),
         V((R, R), F32), V((R, R), F32), V((2, R, R), BF),
         V((R, 2 * S), F32), V((R, 2 * S), F32), V((R, 2 * S), BF), V((R, 128), F32), V((R, 128), F32), V((128, R), F32),
         V((R, 128), F32), V((R, 128), F32), V((R, 128), F32), V((R, 128), F32), V((R, 128), F32), V((R, 128), F32),
         V((3, 8, R), F32), V((3, 8, R), F32), V((R, H), BF), V((R, H), BF), V((R, H), BF),
         V((R, 2 * S), BF), V((R, 2 * S), BF),
         V((4, 8, C), F32), V((4, 8, C), F32), V((dp, 8, 128), F32), V((2, 8, 128), F32),
-        D((6, dp)), D((6, dp)), D((2, 2)), D((2, 2)), D((nch, 3)), D((nch, 3)), D((2, 6)), D((2, 6)),
-        D((nch, 6)), D((nch, 6)), D((6,)), D((6,)), D((dp,)), D((dp,)), D((4,)), D((4,)), D((4,)), D((2, dp)), D((2, dp)), D((2, 2)),
+        D((6,)), D((6,)), D((2, 2)), D((2, 2)), D((3,)), D((nch, 3)), D((2, 6)), D((2, 6)),
+        D, D((nch, 6)), D((6,)), D((6,)), D, D, D((4,)), D((4,)), D((4,)), D((2,)), D((2,)), D((2, 2)), D((9,)),
         pltpu.SemaphoreType.REGULAR,
     ]
     out = jax.ShapeDtypeStruct
@@ -1161,7 +1174,7 @@
         out_shape=(out((R, H), BF), out((R, H), BF), out((sz.share, 2 * C), F32), out((sz.share, C), F32),
                    out((sz.share, sz.extra), F32), out((8, C), F32), out((2, 8, 128), F32)),
         in_specs=[vm, vm, sm, hb, hb, hb, hb, hb] + [vm] * 10,
-        out_specs=(hb, hb) + (vm,) * 5,
+        out_specs=(hb,) * 7,
         scratch_shapes=scratch,
         compiler_params=pltpu.CompilerParams(collective_id=0, has_side_effects=True, vmem_limit_bytes=66000000),
         name="block",

time: 169 us -> 166 us (0.982)
  Pallas kernels: 167 us -> 165 us
    pallas_call x1, Pallas kernels: 164 us -> 161 us  [fused(): pl.pallas_call(functools.partial(block_kernel, sz), out_shape=(out((R, H)...]
where the time goes in v5:
time: 166 us
  Pallas kernels  165 us (99%)
    pallas_call x1, Pallas kernels, fused(): pl.pallas_call(functools.partial(block_kernel, sz), out_shape=(out((R, H)...  161 us
    pallas_call x1, Pallas kernels, fused(): pl.pallas_call(functools.partial(finish_kernel, sz), out_shape=(out((R, H...  3.54 us

profile of v5, /device:TPU:0, one launch (start us, length us, event | category | flops | bytes accessed | tf_op | source)
XLA Modules:
  0.0 166.1 jit_solution(11993014770875460932)
XLA Ops:
  1.3 161.1 %block.1 = (bf16[256,768]{1,0:T(8,128)(2,1)}, bf16[256,768]{1,0:T(8,128)(2,1)}, f32[96,3072]{1,0:T(8,128)}, f32[96,1536]{1,0:T(8,128)}, f32[96,384]{1,0:T(8,128)...) custom-call(s32[32,128]{1,0:T(8,128)} %bitcast.13, s32[32,128]{1,0:T(8,128)} %bitcast.14, s32[1,1]{1,0:T(1,128)S(6)} %copy.33.refs_2_, ...), custom_call_target="tpu_custom_call" | custom-call | tf_op jit(solution)/shard_map/block/pallas_call | solution.py:1172
  162.4 3.5 %finish.1 = (bf16[256,768]{1,0:T(8,128)(2,1)}, bf16[256,768]{1,0:T(8,128)(2,1)}, f32[96]{0:T(128)}, f32[96,2,1536]{2,1,0:T(2,128)}, f32[96,256]{1,0:T(8,128)}, /...) custom-call(bf16[256,768]{1,0:T(8,128)(2,1)} %get-tuple-element.37.r, ...), custom_call_target="tpu_custom_call" | custom-call | tf_op jit(solution)/shard_map/finish/pallas_call | solution.py:1184

commit v6 on v5

--- a/solution.py
+++ b/solution.py
@@ -363,7 +363,7 @@
     beside_z = is_outer * zi + (1 - is_outer) * zo
     beside = [beside_z * 4 + ((x + dx) % 2) * 2 + (c + dc) % 2 for dx, dc in ((1, 1), (1, 0), (0, 1))]
     partner = beside_z * 4 + q
-    parts = [pl.ds(0, H // 3 * 2), pl.ds(H // 3 * 2, H // 3)]
+    parts = [pl.ds(k * (H // 3), H // 3) for k in range(3)]
 
     def span(ref, n, ss, rs, at=slice(None)):
         return rcopy(ref.at[pl.ds(0, n), :, at], ref.at[pl.ds(0, n), :, at], ss, rs, partner)
@@ -371,7 +371,6 @@
     def exchange(i, source, target, at=slice(None)):
         for peer in far:
             rcopy(source.at[peer, :, at], target.at[g, :, at], a2a_s.at[i], a2a_r.at[i], peer).start()
-        return [span(source, dp - 1, a2a_s.at[i], a2a_r.at[i], at)]
 
     def settle(copies):
         for copy in copies:
@@ -387,7 +386,7 @@
             dst[k * (dp // 2):(k + 1) * (dp // 2)] = part.reshape(dp // 2, sz.cap, H)
 
     def block_to(i, source, target, peer, owner, sems):
-        return rcopy(source.at[peer], target.at[owner], sems.at[i - 4], a2a_r.at[i], peer)
+        return rcopy(source.at[peer], target.at[owner], sems.at[i - 4], a2a_r.at[i + 2], peer)
 
     def raw_copy(i):
         return rcopy(lowct.at[:, pl.ds((i - 4) * H, H)], raw_r, raw_sem.at[0, i - 4], raw_sem.at[1, i - 4], partner)
@@ -434,21 +433,21 @@
     def replied(i, target):
         @pl.when(is_outer == 1)
         def _():
-            span(target, dp - 1, own_s.at[i - 4], a2a_r.at[i]).wait_recv()
+            span(target, dp - 1, own_s.at[i - 4], a2a_r.at[i + 2]).wait_recv()
 
         @pl.when(is_outer == 0)
         def _():
-            span(target, dp - 2, own_s.at[i - 4], a2a_r.at[i]).wait_recv()
+            span(target, dp - 2, own_s.at[i - 4], a2a_r.at[i + 2]).wait_recv()
 
     def reply_settle(i, packed):
         @pl.when(is_outer == 1)
         def _():
-            span(packed, len(level), own_s.at[i - 4], a2a_r.at[i]).wait_send()
+            span(packed, len(level), own_s.at[i - 4], a2a_r.at[i + 2]).wait_send()
 
         @pl.when(is_outer == 0)
         def _():
-            span(packed, dp - 1, own_s.at[i - 4], a2a_r.at[i]).wait_send()
-            span(packed, len(across + level), relay_s.at[i - 4], a2a_r.at[i]).wait_send()
+            span(packed, dp - 1, own_s.at[i - 4], a2a_r.at[i + 2]).wait_send()
+            span(packed, len(across + level), relay_s.at[i - 4], a2a_r.at[i + 2]).wait_send()
 
     def pack(table, source, target):
         for k in range(2):
@@ -456,56 +455,55 @@
             part = dot_nn(table[k * n:(k + 1) * n, :], source[...]).astype(BF)
             target[k * (dp // 2):(k + 1) * (dp // 2)] = part.reshape(dp // 2, sz.cap, H)
 
-    p_own[...] = send_table(dest, g, sz)
-    loads[0].wait()
-    pack(p_own, lowct.at[:, pl.ds(0, H)], pk_in)
-    pl.semaphore_wait(barrier, dp)
-    rows_away = exchange(0, pk_in, rc_in, parts[0]) + exchange(1, pk_in, rc_in, parts[1])
-    rc_in[pl.ds(g, 1)] = pk_in[pl.ds(g, 1)]
-    for load in loads[2:]:
-        load.start()
-    p_own[...] = send_table(back, g, sz)
-    loads[1].wait()
-    pack(p_own, lowct.at[:, pl.ds(H, H)], pk_ct)
-    rc_ct[pl.ds(g, 1)] = pk_ct[pl.ds(g, 1)]
-    q_in[...] = owner_table(dest, g, sz)
-    q_bk[...] = owner_table(back, g, sz)
-
     def unpack(i, table, source, full, part):
         at = parts[part]
-        arrived(2 * i + part, source, at)
+        arrived(3 * i + part, source, at)
         n = at.size
         full[pl.ds(t, 1), :, at] = dot_nn(table[...], source[:, :, at].reshape(sz.slots, n)).astype(BF)[None]
         go(rcopy(full.at[t, :, at], full.at[t, :, at], fw_s.at[i, part], fw_r.at[i, part], g, o))
 
     def other_half(i, full):
-        for part in range(2):
+        for part in range(3):
             at = parts[part]
             rcopy(full.at[o, :, at], full.at[o, :, at], fw_s.at[i, part], fw_r.at[i, part], g, o).wait_recv()
 
     def take_apart(stage, sems):
-        n = W // 128
-        fetch = [pltpu.make_async_copy(win_hbm.at[pl.ds(k * 128, 128)], stage.at[k % 4], sems.at[k % 4]) for k in range(n)]
-        for copy in fetch[:4]:
+        n, held = W // 128, stage.shape[0]
+        fetch = [
+            pltpu.make_async_copy(win_hbm.at[pl.ds(k * 128, 128)], stage.at[k % held], sems.at[k % held]) for k in range(n)]
+        for copy in fetch[:held] + loads[2:]:
             copy.start()
+        p_own[...] = send_table(dest, g, sz)
+        loads[0].wait()
+        pack(p_own, lowct.at[:, pl.ds(0, H)], pk_in)
+        pl.semaphore_wait(barrier, dp)
+        for k in range(3):
+            exchange(k, pk_in, rc_in, parts[k])
+        rc_in[pl.ds(g, 1)] = pk_in[pl.ds(g, 1)]
+        p_own[...] = send_table(back, g, sz)
+        loads[1].wait()
+        pack(p_own, lowct.at[:, pl.ds(H, H)], pk_ct)
+        rc_ct[pl.ds(g, 1)] = pk_ct[pl.ds(g, 1)]
+        q_in[...] = owner_table(dest, g, sz)
+        q_bk[...] = owner_table(back, g, sz)
         place = iota((256, 256), 0)
         order = one_hot(iota((256, 256), 1) == jnp.where(place < 128, 2 * place, 2 * place - 255))
         for k in range(n):
             fetch[k].wait()
             for m in range(0, C, 256):
                 pair = jnp.concatenate(
-                    [stage[k % 4, :, :, m + e:m + e + 128].reshape(256, 128) for e in (0, 128)], axis=1)
+                    [stage[k % held, :, :, m + e:m + e + 128].reshape(256, 128) for e in (0, 128)], axis=1)
                 both = dot_nn(order, pair).astype(BF)
                 win[k * 128:(k + 1) * 128, m:m + 256] = both[:128]
                 win[k * 128:(k + 1) * 128, C + m:C + m + 256] = both[128:]
-            if k + 4 < n:
-                fetch[k + 4].start()
-
-    pl.run_scoped(take_apart, pltpu.VMEM((4, 128, 2, C), BF), pltpu.SemaphoreType.DMA((4,)))
-    grads_away = exchange(2, pk_ct, rc_ct, parts[0])
-    unpack(0, q_in, rc_in, hid, 0)
-    grads_away += exchange(3, pk_ct, rc_ct, parts[1])
-    unpack(0, q_in, rc_in, hid, 1)
+            if k + held < n:
+                fetch[k + held].start()
+
+    pl.run_scoped(take_apart, pltpu.VMEM((10, 128, 2, C), BF), pltpu.SemaphoreType.DMA((10,)))
+    for k in range(3):
+        unpack(0, q_in, rc_in, hid, k)
+    for k in range(3):
+        exchange(3 + k, pk_ct, rc_ct, parts[k])
     other_half(0, hid)
 
     total = jnp.zeros((R, 128), F32)
@@ -783,6 +781,7 @@
 
         squares = total_over_sides(0, acc1[...])
         unpack(1, q_bk, rc_ct, cts, 1)
+        unpack(1, q_bk, rc_ct, cts, 2)
         turn_quarter(xA, tA)
         settle(quarter_away)
         fold_half(t, 0)
@@ -930,7 +929,8 @@
             cut = slice(k * 128, (k + 1) * 128)
             branch = gr[:, cut] + half_r[:, cut].astype(F32)
             pieces.append((mine[:, cut].astype(F32) + live * branch).astype(BF))
-        settle(rows_away)
+        for k in range(3):
+            span(pk_in, dp - 1, a2a_s.at[k], a2a_r.at[k], parts[k]).wait_send()
         reply(4, q_bk, jnp.concatenate(pieces, axis=1), pk_in, gn_o)
         reply_send(4, pk_in, gn_o, True)
 
@@ -1023,7 +1023,8 @@
             gall[pl.ds(g, 1), k:k + 1, :] = jnp.sum(value * rows_here * scale[...], axis=0, keepdims=True)[None]
             pieces.append((scale[...] * (gain_n[pl.ds(t * (H // 128) + k, 1), :] * value) - rows_here * pull
                            + mine_ct[:, cut].astype(F32)).astype(BF))
-        settle(grads_away)
+        for k in range(3):
+            span(pk_ct, dp - 1, a2a_s.at[3 + k], a2a_r.at[3 + k], parts[k]).wait_send()
         reply(5, q_in, jnp.concatenate(pieces, axis=1), pk_ct, gn_g)
         reply_send(5, pk_ct, gn_g, True)
         reply_send(5, pk_ct, gn_g, False)
@@ -1164,7 +1165,7 @@
         V((3, 8, R), F32), V((3, 8, R), F32), V((R, H), BF), V((R, H), BF), V((R, H), BF),
         V((R, 2 * S), BF), V((R, 2 * S), BF),
         V((4, 8, C), F32), V((4, 8, C), F32), V((dp, 8, 128), F32), V((2, 8, 128), F32),
-        D((6,)), D((6,)), D((2, 2)), D((2, 2)), D((3,)), D((nch, 3)), D((2, 6)), D((2, 6)),
+        D((6,)), D((8,)), D((2, 3)), D((2, 3)), D((3,)), D((nch, 3)), D((2, 6)), D((2, 6)),
         D, D((nch, 6)), D((6,)), D((6,)), D, D, D((4,)), D((4,)), D((4,)), D((2,)), D((2,)), D((2, 2)), D((9,)),
         pltpu.SemaphoreType.REGULAR,
     ]

time: 166 us -> 162 us (0.976)
  Pallas kernels: 165 us -> 161 us
    pallas_call x1, Pallas kernels: 161 us -> 157 us  [fused(): pl.pallas_call(functools.partial(block_kernel, sz), out_shape=(out((R, H)...]
where the time goes in v6:
time: 162 us
  Pallas kernels  161 us (99%)
    pallas_call x1, Pallas kernels, fused(): pl.pallas_call(functools.partial(block_kernel, sz), out_shape=(out((R, H)...  157 us
    pallas_call x1, Pallas kernels, fused(): pl.pallas_call(functools.partial(finish_kernel, sz), out_shape=(out((R, H...  3.54 us

profile of v6, /device:TPU:0, one launch (start us, length us, event | category | flops | bytes accessed | tf_op | source)
XLA Modules:
  0.0 162.0 jit_solution(6238173924629096621)
XLA Ops:
  1.3 157.0 %block.1 = (bf16[256,768]{1,0:T(8,128)(2,1)}, bf16[256,768]{1,0:T(8,128)(2,1)}, f32[96,3072]{1,0:T(8,128)}, f32[96,1536]{1,0:T(8,128)}, f32[96,384]{1,0:T(8,128)...) custom-call(s32[32,128]{1,0:T(8,128)} %bitcast.13, s32[32,128]{1,0:T(8,128)} %bitcast.14, s32[1,1]{1,0:T(1,128)S(6)} %copy.33.refs_2_, ...), custom_call_target="tpu_custom_call" | custom-call | tf_op jit(solution)/shard_map/block/pallas_call | solution.py:1173
  158.3 3.5 %finish.1 = (bf16[256,768]{1,0:T(8,128)(2,1)}, bf16[256,768]{1,0:T(8,128)(2,1)}, f32[96]{0:T(128)}, f32[96,2,1536]{2,1,0:T(2,128)}, f32[96,256]{1,0:T(8,128)}, /...) custom-call(bf16[256,768]{1,0:T(8,128)(2,1)} %get-tuple-element.37.r, ...), custom_call_target="tpu_custom_call" | custom-call | tf_op jit(solution)/shard_map/finish/pallas_call | solution.py:1185

commit v7 on v6

--- a/solution.py
+++ b/solution.py
@@ -264,7 +264,7 @@
         self.extra = 2 * state + 128
         self.cols = 3 * inner + self.extra
         n = inner // 2
-        sizes = [n // 3 * 2, n // 3 * 4, n, n, n, n, self.extra]
+        sizes = [n // 3 * 2, n // 3 * 4, n, n, n, n // 2, n // 2, self.extra]
         self.chunks = [(sum(sizes[:k]), size) for k, size in enumerate(sizes)]
         self.levels = self.nz.bit_length() - 1
 
@@ -676,7 +676,7 @@
         start, size = sz.chunks[i]
         if i < 2:
             pairs = [(f_proj.at[:, pl.ds(start, size)], proj_out.at[:, pl.ds(start, size)])]
-        elif i < 6:
+        elif i < 7:
             cut = pl.ds(start - C, size)
             pairs = [(f_inner.at[:, cut], inner_out.at[:, cut])]
         else:
@@ -935,8 +935,10 @@
         reply_send(4, pk_in, gn_o, True)
 
         quad_pass(1)
-        lax.fori_loop(NT_ // 2, NT_, scan_back, 0)
+        lax.fori_loop(NT_ // 2, NT_ // 4 * 3, scan_back, 0)
         quad_send(5)
+        lax.fori_loop(NT_ // 4 * 3, NT_, scan_back, 0)
+        quad_send(6)
 
         ig = igrad[...].astype(BF)
         st_s[:, :S] = dot_nn(ig, wr[:, S:]).astype(BF)
@@ -961,7 +963,7 @@
                 raw_grad = raw_grad + tap_s[tap:tap + 1, cut] * up
                 sms[0, 7:8, tap * 2 * S + k * S:tap * 2 * S + (k + 1) * S] = jnp.sum(up * raw, axis=0, keepdims=True)
             yb[0, :, 3 * C + k * S:3 * C + (k + 1) * S] = raw_grad.astype(BF)
-        quad_send(6)
+        quad_send(7)
         reply_send(4, pk_in, gn_o, False)
 
         hops = [2 ** k for k in range(2, dp.bit_length() - 1)] + [1, 2]
@@ -1046,14 +1048,17 @@
         quad_pass(5)
         partial_sum(5, tA)
         z_third(2)
-        z_second(3)
         quad_pass(6)
         partial_sum(6, tA)
+        z_second(3)
+        quad_pass(7)
+        partial_sum(7, tA)
         small_end(1)
         z_second(4)
         small_end(2)
+        z_second(5)
         z_third(3)
-        z_second(5)
+        z_second(6)
 
         def give(i, value, dst):
             lowct[:, i * H:(i + 1) * H] = value.astype(BF)
@@ -1073,7 +1078,7 @@
             z_fourth(i)
             stores += write_out(i)
         small_end(3)
-        stores.append(pltpu.make_async_copy(smr.at[0], small_out, o_s.at[7]))
+        stores.append(pltpu.make_async_copy(smr.at[0], small_out, o_s.at[8]))
         stores[-1].start()
         span(gall, dp - 1, gg_s, gg_r).wait_recv()
         sent.append(span(gall, dp - 1, gg_s, gg_r))
@@ -1084,18 +1089,16 @@
         go(rcopy(gsum.at[t], gsum.at[t], y_s.at[5], y_r.at[5], g, o))
         replied(5, gn_g)
         stores.append(give(1, dot_tn(p_own[...], gn_g[...].reshape(sz.slots, H)), out_grads))
-        z_second(6)
+        z_second(7)
         z_third(4)
         z_fourth(4)
         stores += write_out(4)
-        z_third(5)
-        z_fourth(5)
-        stores += write_out(5)
-        z_third(6)
-        z_fourth(6)
-        stores += write_out(6)
+        for i in range(5, 8):
+            z_third(i)
+            z_fourth(i)
+            stores += write_out(i)
         rcopy(gsum.at[o], gsum.at[o], y_s.at[5], y_r.at[5], g, o).wait_recv()
-        stores.append(pltpu.make_async_copy(gsum, gain_out, o_s.at[8]))
+        stores.append(pltpu.make_async_copy(gsum, gain_out, o_s.at[9]))
         stores[-1].start()
         for copy in sent:
             copy.wait_send()
@@ -1166,7 +1169,7 @@
         V((R, 2 * S), BF), V((R, 2 * S), BF),
         V((4, 8, C), F32), V((4, 8, C), F32), V((dp, 8, 128), F32), V((2, 8, 128), F32),
         D((6,)), D((8,)), D((2, 3)), D((2, 3)), D((3,)), D((nch, 3)), D((2, 6)), D((2, 6)),
-        D, D((nch, 6)), D((6,)), D((6,)), D, D, D((4,)), D((4,)), D((4,)), D((2,)), D((2,)), D((2, 2)), D((9,)),
+        D, D((nch, 6)), D((6,)), D((6,)), D, D, D((4,)), D((4,)), D((4,)), D((2,)), D((2,)), D((2, 2)), D((10,)),
         pltpu.SemaphoreType.REGULAR,
     ]
     out = jax.ShapeDtypeStruct

time: 162 us -> 162 us (level)
  no operation moved by 1% of the time
where the time goes in v7:
time: 162 us
  Pallas kernels  161 us (99%)
    pallas_call x1, Pallas kernels, fused(): pl.pallas_call(functools.partial(block_kernel, sz), out_shape=(out((R, H)...  157 us
    pallas_call x1, Pallas kernels, fused(): pl.pallas_call(functools.partial(finish_kernel, sz), out_shape=(out((R, H...  3.54 us

profile of v7, /device:TPU:0, one launch (start us, length us, event | category | flops | bytes accessed | tf_op | source)
XLA Modules:
  0.0 162.1 jit_solution(17212421002063056453)
XLA Ops:
  1.3 157.0 %block.1 = (bf16[256,768]{1,0:T(8,128)(2,1)}, bf16[256,768]{1,0:T(8,128)(2,1)}, f32[96,3072]{1,0:T(8,128)}, f32[96,1536]{1,0:T(8,128)}, f32[96,384]{1,0:T(8,128)...) custom-call(s32[32,128]{1,0:T(8,128)} %bitcast.13, s32[32,128]{1,0:T(8,128)} %bitcast.14, s32[1,1]{1,0:T(1,128)S(6)} %copy.33.refs_2_, ...), custom_call_target="tpu_custom_call" | custom-call | tf_op jit(solution)/shard_map/block/pallas_call | solution.py:1176
  158.3 3.5 %finish.1 = (bf16[256,768]{1,0:T(8,128)(2,1)}, bf16[256,768]{1,0:T(8,128)(2,1)}, f32[96]{0:T(128)}, f32[96,2,1536]{2,1,0:T(2,128)}, f32[96,256]{1,0:T(8,128)}, /...) custom-call(bf16[256,768]{1,0:T(8,128)(2,1)} %get-tuple-element.37.r, ...), custom_call_target="tpu_custom_call" | custom-call | tf_op jit(solution)/shard_map/finish/pallas_call | solution.py:1188
